TPU v7x, 32 devices: a whole 2x2x4 slice. The times are simulated.
32 devices in a mesh: dp: 8 (over z, x), row: 2 (over y), col: 2 (over core).
Axes of the slice: x: 2, y: 2, z: 4, core: 2. Of those that a mesh axis runs over, the one named last changes fastest.
Arguments:
- tokens: bfloat16 [32768, 768], P(('dp', 'col'), 'row'), may hold values from -6 to 6
- condition: bfloat16 [128, 768], P('dp', 'col'), may hold values from -6 to 6
- adaptive: bfloat16 [6, 768, 768], P(None, 'col', 'row'), may hold values from -0.21875 to 0.21875
- adabias: bfloat16 [6, 768], P(None, 'row'), may hold values from -3 to 3
- attend: bfloat16 [3, 768, 768], P(None, 'row', 'col'), may hold values from -0.21875 to 0.21875
- attbias: bfloat16 [2, 768], P(None, 'col'), may hold values from -3 to 3
- outproj: bfloat16 [768, 768], P('col', 'row'), may hold values from -1.25 to 1.25
- outbias: bfloat16 [768], P('row'), may hold values from -3 to 3
- expand: bfloat16 [768, 3072], P('row', 'col'), may hold values from -0.21875 to 0.21875
- expbias: bfloat16 [3072], P('col'), may hold values from -3 to 3
- shrink: bfloat16 [3072, 768], P('col', 'row'), may hold values from -0.109375 to 0.109375
- shrbias: bfloat16 [768], P('row'), may hold values from -3 to 3
- cotangent: bfloat16 [32768, 768], P(('dp', 'col'), 'row'), may hold values from -6 to 6
Outputs:
- result: bfloat16 [32768, 768], P(('dp', 'col'), 'row')
- input_gradient: bfloat16 [32768, 768], P(('dp', 'col'), 'row')
- condition_gradient: bfloat16 [128, 768], P('dp', 'col')
- adaptive_gradient: float32 [6, 768, 768], P(None, 'col', 'row')
- adabias_gradient: float32 [6, 768], P(None, 'row')
- attend_gradient: float32 [3, 768, 768], P(None, 'row', 'col')
- attbias_gradient: float32 [2, 768], P(None, 'col')
- outproj_gradient: float32 [768, 768], P('col', 'row')
- outbias_gradient: float32 [768], P('row')
- expand_gradient: float32 [768, 3072], P('row', 'col')
- expbias_gradient: float32 [3072], P('col')
- shrink_gradient: float32 [3072, 768], P('col', 'row')
- shrbias_gradient: float32 [768], P('row')
All inputs are finite; a program needn't handle non-finite values.
Results may differ from a plain program's by a relative error of at most 0.01575.
The roundings to bfloat16 on the way count: a program that leaves them out, or rounds other values in their place, can miss the bound.
Values may be sent and summed in bfloat16 or wider, within the bound.
No kernel may reach another device: no remote copies, remote signals or barrier semaphores. Data moves between devices by JAX's collectives and lax.ppermute only.
A program may use at most 256 MiB of HBM per device.

v0:
```python
import jax
import jax.numpy as jnp
from jax import lax
from jax.sharding import PartitionSpec as P

D = 768
SEQ = 256
HEAD_DIM = 64


EPS = 1e-06
F32 = jnp.float32
B16 = jnp.bfloat16
CONTRACT_LAST = (((1,), (1,)), ((), ()))
CONTRACT_FIRST = (((0,), (0,)), ((), ()))


def gather_cols(values):
    return lax.all_gather(values, "col", axis=0, tiled=True)


def gather_rows(values):
    return lax.all_gather(values, "row", axis=0, tiled=True)


def contract_rows(left, weight, product):
    return lax.psum_scatter(product(left, weight), "row", scatter_dimension=0, tiled=True)


def reduce_cols(left, product):
    return lax.psum_scatter(
        product(left).astype(jnp.bfloat16), "col", scatter_dimension=0, tiled=True
    ).astype(jnp.float32)


def cross(left, right):
    return lax.dot_general(left, right, CONTRACT_FIRST, preferred_element_type=F32)


def normalize(values):
    totals, squares = lax.psum((jnp.sum(values, axis=1), jnp.sum(values * values, axis=1)), "row")
    center = totals / D
    inverse = lax.rsqrt(squares / D - center * center + EPS)
    return ((values - center[:, None]) * inverse[:, None], inverse)


def norm_grad(upstream, normal, inverse):
    first_sum, second_sum = lax.psum(
        (jnp.sum(upstream, axis=1), jnp.sum(upstream * normal, axis=1)), "row"
    )
    return inverse[:, None] * (upstream - first_sum[:, None] / D - normal * second_sum[:, None] / D)


def latent_sum(values):
    return jnp.sum(values.reshape(-1, SEQ, values.shape[1]), axis=1)


def block_size(rows):
    latents = rows // SEQ
    return min(latents, max(1, 512 // SEQ))


def split_heads(values, per_block):
    latents = values.shape[0] // SEQ
    return values.reshape(
        latents // per_block, per_block, SEQ, values.shape[1] // HEAD_DIM, HEAD_DIM
    )


def attention_forward(queries, key_rows, value_rows):
    per_block = block_size(queries.shape[0])
    factor = HEAD_DIM ** (-0.5)

    def one_block(group):
        q_part, k_part, v_part = group
        scores = jnp.einsum("lqhe,lkhe->lhqk", q_part, k_part, preferred_element_type=F32) * factor
        summit = jnp.max(scores, axis=-1, keepdims=True)
        exponent = jnp.exp(scores - summit)
        totals = jnp.sum(exponent, axis=-1, keepdims=True)
        probs = (exponent / totals).astype(B16)
        output = jnp.einsum("lhqk,lkhe->lqhe", probs, v_part, preferred_element_type=F32)
        return (output.astype(B16), (summit + jnp.log(totals))[..., 0])

    outputs, logsum = lax.map(
        one_block,
        (
            split_heads(queries, per_block),
            split_heads(key_rows, per_block),
            split_heads(value_rows, per_block),
        ),
    )
    return (outputs.reshape(queries.shape), logsum)


def attention_backward(queries, key_rows, value_rows, upstream, logsum):
    per_block = block_size(queries.shape[0])
    factor = HEAD_DIM ** (-0.5)

    def one_block(group):
        q_part, k_part, v_part, d_part, l_part = group
        scores = jnp.einsum("lqhe,lkhe->lhqk", q_part, k_part, preferred_element_type=F32) * factor
        probs = jnp.exp(scores - l_part[..., None])
        d_probs = jnp.einsum("lqhe,lkhe->lhqk", d_part, v_part, preferred_element_type=F32)
        d_scores = (probs * (d_probs - jnp.sum(probs * d_probs, axis=-1, keepdims=True))).astype(
            B16
        )
        d_query = (
            jnp.einsum("lhqk,lkhe->lqhe", d_scores, k_part, preferred_element_type=F32) * factor
        )
        d_keys = (
            jnp.einsum("lhqk,lqhe->lkhe", d_scores, q_part, preferred_element_type=F32) * factor
        )
        d_values = jnp.einsum(
            "lhqk,lqhe->lkhe", probs.astype(B16), d_part, preferred_element_type=F32
        )
        return (d_query.astype(B16), d_keys.astype(B16), d_values.astype(B16))

    pieces = lax.map(
        one_block,
        (
            split_heads(queries, per_block),
            split_heads(key_rows, per_block),
            split_heads(value_rows, per_block),
            split_heads(upstream, per_block),
            logsum,
        ),
    )
    return jnp.concatenate([piece.reshape(queries.shape) for piece in pieces], axis=1)


def project_three(piece, weight):
    return jnp.einsum("td,kde->tke", piece, weight, preferred_element_type=F32).reshape(
        piece.shape[0], 3 * weight.shape[2]
    )


def plain_dot(piece, weight):
    return jnp.dot(piece, weight, preferred_element_type=F32)


def dot_transposed(piece, weight):
    return lax.dot_general(piece, weight, CONTRACT_LAST, preferred_element_type=F32)


def shards(
    tokens,
    condition,
    adaptive,
    adabias,
    attend,
    attbias,
    outproj,
    outbias,
    expand,
    expbias,
    shrink,
    shrbias,
    cotangent,
):
    raw_condition = condition.astype(F32)
    act_cond = jax.nn.silu(raw_condition).astype(B16)
    mod_terms = jnp.einsum("ld,kde->lke", act_cond, adaptive, preferred_element_type=F32)
    modulation = lax.psum_scatter(
        mod_terms, "col", scatter_dimension=0, tiled=True
    ) + adabias.astype(F32)
    expanded = jnp.repeat(modulation, SEQ, axis=0)
    shift_one, scale_one, gate_one, shift_two, scale_two, gate_two = [
        expanded[:, number] for number in range(6)
    ]
    inputs = tokens.astype(F32)
    normal_one, inverse_one = normalize(inputs)
    first_all = gather_cols((normal_one * (1.0 + scale_one) + shift_one).astype(B16))
    width = attend.shape[2]
    triple = contract_rows(first_all, attend, project_three)
    biases = attbias.astype(F32)
    queries = (triple[:, :width] + biases[0]).astype(B16)
    key_rows = triple[:, width : 2 * width].astype(B16)
    value_rows = (triple[:, 2 * width :] + biases[1]).astype(B16)
    attended, logsum = attention_forward(queries, key_rows, value_rows)
    attended_all = gather_rows(attended)
    branch_one = reduce_cols(
        attended_all, lambda piece: jnp.dot(piece, outproj, preferred_element_type=F32)
    ) + outbias.astype(F32)
    middle = inputs + gate_one * branch_one
    normal_two, inverse_two = normalize(middle)
    second_all = gather_cols((normal_two * (1.0 + scale_two) + shift_two).astype(B16))
    hidden = contract_rows(second_all, expand, plain_dot) + expbias.astype(F32)
    active_all = gather_rows(jax.nn.gelu(hidden, approximate=True).astype(B16))
    branch_two = reduce_cols(
        active_all, lambda piece: jnp.dot(piece, shrink, preferred_element_type=F32)
    ) + shrbias.astype(F32)
    result = (middle + gate_two * branch_two).astype(B16)
    upstream = cotangent.astype(F32)
    gate_two_terms = upstream * branch_two
    d_branch_two = gather_cols((gate_two * upstream).astype(B16))
    shrbias_grad = jnp.sum(d_branch_two, axis=0, dtype=F32)
    shrink_grad = cross(active_all, d_branch_two)
    d_active = contract_rows(d_branch_two, shrink, dot_transposed)
    gelu_pull = jax.vjp(lambda values: jax.nn.gelu(values, approximate=True), hidden)[1]
    d_hidden = gather_rows(gelu_pull(d_active)[0].astype(B16))
    expbias_grad = jnp.sum(d_hidden, axis=0, dtype=F32)
    expand_grad = cross(second_all, d_hidden)
    d_second = reduce_cols(
        d_hidden,
        lambda piece: lax.dot_general(piece, expand, CONTRACT_LAST, preferred_element_type=F32),
    )
    d_middle = upstream + norm_grad(d_second * (1.0 + scale_two), normal_two, inverse_two)
    gate_one_terms = d_middle * branch_one
    d_branch_one = gather_cols((gate_one * d_middle).astype(B16))
    outbias_grad = jnp.sum(d_branch_one, axis=0, dtype=F32)
    outproj_grad = cross(attended_all, d_branch_one)
    d_attended = contract_rows(d_branch_one, outproj, dot_transposed).astype(B16)
    d_triple = gather_rows(attention_backward(queries, key_rows, value_rows, d_attended, logsum))
    attbias_grad = jnp.stack(
        [
            jnp.sum(d_triple[:, :width], axis=0, dtype=F32),
            jnp.sum(d_triple[:, 2 * width :], axis=0, dtype=F32),
        ]
    )
    attend_grad = jnp.einsum(
        "td,tke->kde",
        first_all,
        d_triple.reshape(d_triple.shape[0], 3, width),
        preferred_element_type=F32,
    )
    d_first = reduce_cols(
        d_triple,
        lambda piece: jnp.einsum(
            "tke,kde->td",
            piece.reshape(piece.shape[0], 3, width),
            attend,
            preferred_element_type=F32,
        ),
    )
    input_gradient = (
        d_middle + norm_grad(d_first * (1.0 + scale_one), normal_one, inverse_one)
    ).astype(B16)
    d_modulation = jnp.stack(
        [
            latent_sum(d_first),
            latent_sum(d_first * normal_one),
            latent_sum(gate_one_terms),
            latent_sum(d_second),
            latent_sum(d_second * normal_two),
            latent_sum(gate_two_terms),
        ],
        axis=1,
    ).astype(B16)
    mod_all = lax.all_gather(d_modulation, "col", axis=0, tiled=True)
    adabias_grad = jnp.sum(mod_all, axis=0, dtype=F32)
    adaptive_grad = jnp.einsum("ld,lke->kde", act_cond, mod_all, preferred_element_type=F32)
    d_act = lax.psum(
        jnp.einsum("lke,kde->ld", mod_all, adaptive, preferred_element_type=F32), "row"
    )
    condition_gradient = jax.vjp(jax.nn.silu, raw_condition)[1](d_act)[0].astype(B16)
    (
        adaptive_grad,
        adabias_grad,
        attend_grad,
        attbias_grad,
        outproj_grad,
        outbias_grad,
        expand_grad,
        expbias_grad,
        shrink_grad,
        shrbias_grad,
    ) = lax.psum(
        (
            adaptive_grad,
            adabias_grad,
            attend_grad,
            attbias_grad,
            outproj_grad,
            outbias_grad,
            expand_grad,
            expbias_grad,
            shrink_grad,
            shrbias_grad,
        ),
        "dp",
    )
    return (
        result,
        input_gradient,
        condition_gradient,
        adaptive_grad,
        adabias_grad,
        attend_grad,
        attbias_grad,
        outproj_grad,
        outbias_grad,
        expand_grad,
        expbias_grad,
        shrink_grad,
        shrbias_grad,
    )


def solution(mesh):
    placed = (
        P(("dp", "col"), "row"),
        P("dp", "col"),
        P(None, "col", "row"),
        P(None, "row"),
        P(None, "row", "col"),
        P(None, "col"),
        P("col", "row"),
        P("row"),
        P("row", "col"),
        P("col"),
        P("col", "row"),
        P("row"),
        P(("dp", "col"), "row"),
    )
    return jax.shard_map(
        shards,
        mesh=mesh,
        in_specs=placed,
        out_specs=(
            P(("dp", "col"), "row"),
            P(("dp", "col"), "row"),
            P("dp", "col"),
            P(None, "col", "row"),
            P(None, "row"),
            P(None, "row", "col"),
            P(None, "col"),
            P("col", "row"),
            P("row"),
            P("row", "col"),
            P("col"),
            P("col", "row"),
            P("row"),
        ),
        check_vma=False,
    )
```

profile of v0, /device:TPU:0, one launch (start us, length us, event | category | flops | bytes accessed | tf_op | source)
XLA Modules:
  0.0 2069.1 jit_solution(9537398042940920459)
XLA Ops:
  11.1 9.6 all-reduce.5
  22.0 7.6 broadcast_in_dim.21
  29.6 4.2 fusion.60
  33.8 13.4 all-gather.9.cloned.1.call-done
  47.2 10.6 fusion.76
  58.6 212.3 %reduce-scatter.12.cloned.1.call-done = f32[2048,1152]{0,1:T(8,128)} async-done(((f32[4096,1152]{0,1:T(8,128)}), f32[2048,1152]{0,1:T(8,128)}) %reduce-scatter.12.cloned.1.call-update) | async-done | bytes 9437200 | tf_op jit(solution)/shard_map/reduce_scatter | solution.py:27
  270.9 4.9 fusion.71
  275.8 3.8 reshape.127
  279.7 2.9 copy.40
  282.6 3.8 reshape.128
  286.4 2.9 copy.41
  289.3 3.3 slice.121
  292.6 3.8 reshape.129
  296.4 2.9 copy.42
  301.3 21.0 %while.26 = (s32[]{:T(128)}, bf16[4,2,256,6,64]{2,1,0,4,3:T(2,128)(2,1)}, f32[4,2,6,256]{3,2,1,0:T(8,128)S(1)}, bf16[4,2,256,6,64]{2,4,3,1,0:T(8,128)(2,1)}, bf1...) while((s32[]{:T(128)}, bf16[4,2,256,6,64]{2,1,0,4,3:T(2,128)(2,1)}, ...), condition=%wide.region_9.10_spmd, body=%wide.region_6.9_spmd.sunk | while | flops 208598016 | bytes 11909201 | solution.py:84
  322.3 3.8 reshape.130
  326.2 45.0 %all-gather.11.cloned.1.call-done = bf16[4096,384]{0,1:T(8,128)(2,1)} async-done(((bf16[2048,384]{0,1:T(8,128)(2,1)}), bf16[4096,384]{0,1:T(8,128)(2,1)}) %all-gather.11.cloned.1.call-update) | async-done | bytes 3145744 | tf_op jit(solution)/shard_map/all_gather | solution.py:23
  371.2 5.7 convolution_convert_fusion
  377.6 10.4 reduce-scatter.14.cloned.1.call-done
  388.0 4.6 fusion.100
  392.6 8.3 all-reduce.4
  400.9 7.3 fusion.53
  409.6 11.0 all-gather.13.cloned.1.call-done
  420.6 14.9 fusion.101
  436.7 14.3 fusion.102
  451.7 267.2 %reduce-scatter.16.cloned.1.call-done = f32[2048,1536]{1,0:T(8,128)} async-done(((f32[4096,1536]{1,0:T(8,128)}), f32[2048,1536]{1,0:T(8,128)}) %reduce-scatter.16.cloned.1.call-update) | async-done | bytes 12582928 | tf_op jit(solution)/shard_map/reduce_scatter | solution.py:27
  719.0 281.8 %reduce-scatter.20.cloned.1.call-done = f32[2048,1536]{1,0:T(8,128)} async-done(((f32[4096,1536]{1,0:T(8,128)}), f32[2048,1536]{1,0:T(8,128)}) %reduce-scatter.20.cloned.1.call-update) | async-done | bytes 12582928 | tf_op jit(solution)/shard_map/reduce_scatter | solution.py:27
  1000.7 18.2 fusion.52
  1020.0 151.7 %all-gather.15.cloned.1.call-done = bf16[4096,1536]{1,0:T(8,128)(2,1)} async-done(((bf16[2048,1536]{1,0:T(8,128)(2,1)}), bf16[4096,1536]{1,0:T(8,128)(2,1)}) %all-gather.15.cloned.1.call-update) | async-done | bytes 12582928 | tf_op jit(solution)/shard_map/all_gather | solution.py:23
  1171.7 10.8 convolution_convert_fusion.2
  1182.5 143.3 %all-gather.19.cloned.1.call-done = bf16[4096,1536]{1,0:T(8,128)(2,1)} async-done(((bf16[2048,1536]{1,0:T(8,128)(2,1)}), bf16[4096,1536]{1,0:T(8,128)(2,1)}) %all-gather.19.cloned.1.call-update) | async-done | bytes 12582928 | tf_op jit(solution)/shard_map/all_gather | solution.py:23
  1325.9 10.9 convolution_convert_fusion.1
  1339.0 14.3 reduce-scatter.22.cloned.1.call-done
  1353.3 6.4 fusion.85
  1359.7 8.3 all-reduce.3
  1368.0 5.9 bitcast_reduce_fusion.1
  1375.6 3.4 multiply_convert_fusion.2
  1379.1 12.2 all-gather.21.cloned.1.call-done
  1391.3 6.7 fusion.103
  1398.3 78.1 %reduce-scatter.24.cloned.1.call-done = f32[2048,384]{1,0:T(8,128)} async-done(((f32[4096,384]{1,0:T(8,128)}), f32[2048,384]{1,0:T(8,128)}) %reduce-scatter.24.cloned.1.call-update) | async-done | bytes 3145744 | tf_op jit(solution)/shard_map/reduce_scatter | solution.py:27
  1476.4 3.2 convert_element_type.164
  1481.3 2.4 reshape.131
  1489.6 44.4 %while.27 = (s32[]{:T(128)}, bf16[4,2,256,6,64]{2,1,0,4,3:T(2,128)(2,1)}, bf16[4,2,256,6,64]{2,1,0,4,3:T(2,128)(2,1)}, bf16[4,2,256,6,64]{2,1,0,4,3:T(2,128)(2,1...) while((s32[]{:T(128)}, ...), condition=%wide.region_26.27_spmd, body=%wide.region_24.26_spmd.sunk | while | flops 513733632 | bytes 30760048 | solution.py:118
  1534.0 4.0 reshape.132
  1538.0 2.4 reshape.133
  1540.3 4.0 reshape.134
  1544.3 3.8 pad_maximum_fusion
  1548.6 117.7 %all-gather.23.cloned.1.call-done = bf16[4096,1152]{0,1:T(8,128)(2,1)} async-done(((bf16[2048,1152]{0,1:T(8,128)(2,1)}), bf16[4096,1152]{0,1:T(8,128)(2,1)}) %all-gather.23.cloned.1.call-update) | async-done | bytes 9437200 | tf_op jit(solution)/shard_map/all_gather | solution.py:23
  1666.3 10.9 bitcast_convert_fusion
  1677.3 11.7 fusion.106
  1689.1 9.7 fusion.105
  1698.8 2.6 fusion.104
  1701.4 6.3 fusion.82
  1712.1 2.5 convolution_bitcast_fusion
  1714.6 2.5 convert_reduce_fusion.1
  1717.1 7.7 convert_reduce_fusion
  1725.3 3.7 convert_reduce_fusion.4
  1729.2 39.9 %all-reduce = (f32[6,384]{1,0:T(8,128)}, f32[2,384]{1,0:T(2,128)}, f32[384]{0:T(512)}, f32[1536]{0:T(1024)}, f32[384]{0:T(512)}) all-reduce(f32[6,384]{1,0:T(8,128)S(1)} %convert_reduce_fusion.6, f32[2,384]{1,0:T(2,128)S(1)} %pad_maximum_fusion.1, f32[384]{0:T(512)S(1)} %convert_reduce_fusion.2, ...), channel_id=1, replica_groups=mesh['dp'=8,'row'=2,'col'=2] {'dp'}, use_global_device_ids=true, to_apply=%region_41.42 | all-reduce | flops 5376 | bytes 43008 | tf_op jit(solution)/shard_map/psum | solution.py:267
  1769.6 3.3 fusion.86
  1773.0 7.0 all-reduce.2
  1780.6 5.2 fusion.66
  1785.8 262.5 %all-reduce.8.cloned.1.call-done = (f32[6,384,384]{1,2,0:T(8,128)}, f32[3,384,384]{1,2,0:T(8,128)}, f32[384,384]{1,0:T(8,128)}, f32[384,1536]{1,0:T(8,128)}, f32[1536,384]{1,0:T(8,128)}) async-done(((f32[6,384,384]{1,2,0:T(8,128)}, f32[3,384,384]{1,2,0:T(8,128)}, f32[384,384]{1,0:T(8,128)}, f32[384,1536]{1,0:T(8,128)}, f32[1536,384]{1,0:T(8,128)}), (f32[6,384,384]{1,2,0:T(8,128)}, f32[3,384,384]{1,2,0:T(8,128)}, ...) | async-done | bytes 10616848 | tf_op jit(solution)/shard_map/psum | solution.py:267
  2048.3 5.3 copy.53
  2057.4 3.2 copy.128
  (204 shorter events, 101.8 us)
Async XLA Ops:
  7.2 1.5 copy-start
  7.2 3.3 copy-start.1
  7.2 3.9 copy-start.24
  7.2 13.9 reduce-scatter.10.cloned.1.call-start
  10.4 36.8 %all-gather.9.cloned.1.call-start = ((), (), s32[]{:S(2)}) async-start(), calls=%async_computation.10 | async-start | bytes 4718592 | tf_op jit(solution)/shard_map/all_gather | solution.py:19
  20.7 8.8 copy-start.19
  20.8 8.8 copy-start.21
  33.8 237.1 %reduce-scatter.12.cloned.1.call-start = ((), (), s32[]{:S(2)}) async-start(), calls=%async_computation.11 | async-start | bytes 28311552 | tf_op jit(solution)/shard_map/reduce_scatter | solution.py:27
  57.9 0.7 copy-start.26
  57.9 313.3 %all-gather.11.cloned.1.call-start = ((), (), s32[]{:S(2)}) async-start(), calls=%async_computation.12 | async-start | bytes 4718592 | tf_op jit(solution)/shard_map/all_gather | solution.py:23
  326.1 61.8 %reduce-scatter.14.cloned.1.call-start = ((), (), s32[]{:S(2)}) async-start(), calls=%async_computation.13 | async-start | bytes 4718592 | tf_op jit(solution)/shard_map/reduce_scatter | solution.py:31
  376.9 0.7 copy-start.27
  376.9 43.6 %all-gather.13.cloned.1.call-start = ((), (), s32[]{:S(2)}) async-start(), calls=%async_computation.14 | async-start | bytes 4718592 | tf_op jit(solution)/shard_map/all_gather | solution.py:19
  408.2 12.3 copy-start.15
  408.3 27.8 %all-gather.17.cloned.1.call-start = ((), (), s32[]{:S(2)}) async-start(), calls=%async_computation.18 | async-start | bytes 4718592 | tf_op jit(solution)/shard_map/all_gather | solution.py:19
  409.0 310.0 %reduce-scatter.16.cloned.1.call-start = ((), (), s32[]{:S(2)}) async-start(), calls=%async_computation.15 | async-start | bytes 37748736 | tf_op jit(solution)/shard_map/reduce_scatter | solution.py:27
  435.4 1.3 copy-start.14
  435.4 565.3 %reduce-scatter.20.cloned.1.call-start = ((), (), s32[]{:S(2)}) async-start(), calls=%async_computation.19 | async-start | bytes 37748736 | tf_op jit(solution)/shard_map/reduce_scatter | solution.py:27
  451.0 0.7 copy-start.25
  451.1 720.6 %all-gather.15.cloned.1.call-start = ((), (), s32[]{:S(2)}) async-start(), calls=%async_computation.16 | async-start | bytes 18874368 | tf_op jit(solution)/shard_map/all_gather | solution.py:23
  1019.0 306.9 %all-gather.19.cloned.1.call-start = ((), (), s32[]{:S(2)}) async-start(), calls=%async_computation.20 | async-start | bytes 18874368 | tf_op jit(solution)/shard_map/all_gather | solution.py:23
  1019.7 319.2 %reduce-scatter.18.cloned.1.call-start = ((), (), s32[]{:S(2)}) async-start(), calls=%async_computation.17 | async-start | bytes 4718592 | tf_op jit(solution)/shard_map/reduce_scatter | solution.py:31
  1182.5 143.4 %copy-start.16 = (bf16[384,1536]{1,0:T(8,128)(2,1)S(1)}, bf16[384,1536]{1,0:T(8,128)(2,1)}, u32[]{:S(2)}) copy-start(bf16[384,1536]{1,0:T(8,128)(2,1)} %param.25) | copy-start | bytes 3538948
  1182.5 170.8 %reduce-scatter.22.cloned.1.call-start = ((), (), s32[]{:S(2)}) async-start(), calls=%async_computation.21 | async-start | bytes 4718592 | tf_op jit(solution)/shard_map/reduce_scatter | solution.py:31
  1336.7 0.7 copy-start.28
  1336.8 54.6 %all-gather.21.cloned.1.call-start = ((), (), s32[]{:S(2)}) async-start(), calls=%async_computation.22 | async-start | bytes 4718592 | tf_op jit(solution)/shard_map/all_gather | solution.py:19
  1337.4 30.6 %copy-start.7 = (bf16[2048,384]{1,0:T(8,128)(2,1)S(1)}, bf16[2048,384]{1,0:T(8,128)(2,1)}, u32[]{:S(2)}) copy-start(bf16[2048,384]{1,0:T(8,128)(2,1)} %param.29) | copy-start | bytes 4718596
  1374.0 1.7 copy-start.4
  1375.6 15.7 copy-start.18
  1379.1 97.4 %reduce-scatter.24.cloned.1.call-start = ((), (), s32[]{:S(2)}) async-start(), calls=%async_computation.23 | async-start | bytes 9437184 | tf_op jit(solution)/shard_map/reduce_scatter | solution.py:27
  1398.0 268.3 %all-gather.23.cloned.1.call-start = ((), (), s32[]{:S(2)}) async-start(), calls=%async_computation.24 | async-start | bytes 14155776 | tf_op jit(solution)/shard_map/all_gather | solution.py:23
  1483.7 5.9 copy-start.3
  1534.0 4.0 copy-start.8
  1540.3 4.0 copy-start.9
  1548.1 118.2 %copy-start.17 = (bf16[3,384,384]{2,1,0:T(8,128)(2,1)S(1)}, bf16[3,384,384]{2,1,0:T(8,128)(2,1)}, u32[]{:S(2)}) copy-start(bf16[3,384,384]{2,1,0:T(8,128)(2,1)} %param.21) | copy-start | bytes 2654212
  1548.1 159.6 %reduce-scatter.26.cloned.1.call-start = ((), (), s32[]{:S(2)}) async-start(), calls=%async_computation.25 | async-start | bytes 4718592 | tf_op jit(solution)/shard_map/reduce_scatter | solution.py:31
  1677.2 371.1 %all-reduce.8.cloned.1.call-start = ((), (), s32[]{:S(2)}) async-start(), calls=%async_computation.26 | async-start | bytes 21233664 | tf_op jit(solution)/shard_map/psum | solution.py:267
  1677.3 11.8 copy-start.10
  1677.3 24.1 %slice-start = ((s8[9437184]{0:T(1024)(128)(4,1)}), s8[4194304]{0:T(1024)(128)(4,1)S(1)}, s32[]{:S(2)}) async-start(s8[9437184]{0:T(1024)(128)(4,1)} %bitcast.238), calls=%async_computation.27 | async-start | bytes 8388608
  1677.3 24.1 %slice-start.1 = ((s8[9437184]{0:T(1024)(128)(4,1)}), s8[4194304]{0:T(1024)(128)(4,1)S(1)}, s32[]{:S(2)}) async-start(s8[9437184]{0:T(1024)(128)(4,1)} %bitcast.238), calls=%async_computation.28 | async-start | bytes 8388608
  1689.0 9.7 copy-start.5
  1689.1 9.7 copy-start.29
  1689.1 12.3 slice-start.2
  1698.7 2.6 copy-start.11
  1701.4 6.3 copy-start.2
  1701.4 6.3 copy-start.20
  1701.4 6.3 copy-start.22
  1707.7 4.4 copy-start.23
  1717.1 7.7 copy-start.6
  2048.3 5.3 copy-start.13
  2055.4 5.3 copy-start.12
Sparse Core Ops, SparseCore 0:
  10.8 10.2 reduce-scatter.9
  33.9 13.2 all-gather.8
  58.0 212.8 reduce-scatter.11
  326.3 44.9 all-gather.10
  377.1 10.8 reduce-scatter.13
  408.4 12.1 all-gather.12
  422.7 13.2 all-gather.16
  438.5 280.4 reduce-scatter.15
  721.4 279.3 reduce-scatter.19
  1019.1 152.4 all-gather.14
  1173.3 152.5 all-gather.18
  1328.0 10.8 reduce-scatter.17
  1341.2 12.0 reduce-scatter.21
  1379.2 12.1 all-gather.20
  1398.2 78.2 reduce-scatter.23
  1548.2 118.0 all-gather.22
  1677.3 10.8 reduce-scatter.25
  1714.7 333.5 all-reduce.7
where the time goes:
time: 2080 us; the launch traced here: 2070 us
  waiting for transfers between devices  1630 us (78%)
  matrix products  159 us (8%)
  local copies, waits for them, and re-layouts  98 us (5%)
  other arithmetic  94.7 us (5%)
  blocking collectives  75.2 us (4%)
    reduce_scatter x4, waiting for transfers between devices, contract_rows(): lax.psum_scatter(product(left, weight), 'row', scatter_dimension=0, tiled...  839 us
    all_gather x4, waiting for transfers between devices, gather_rows(): return lax.all_gather(values, 'row', axis=0, tiled=True)  458 us
    psum x1, waiting for transfers between devices, shards(): lax.psum((adaptive_grad, adabias_grad, attend_grad, attbias_grad, outproj...  262 us
  transfers between devices with their start and end apart: 18, of which 17 were waited for; matrix products, arithmetic and copies ran while one was open for 5% of the time, Pallas kernels for 0%

commit v1 on v0

v1 whole, which is shorter than its diff:
```python
import functools

import jax
import jax.numpy as jnp
from jax import lax
from jax.experimental import pallas as pl
from jax.experimental.pallas import tpu as pltpu
from jax.sharding import PartitionSpec as P

D = 768
HALF = D // 2
FF = 3072
SEQ = 256
HEAD_DIM = 64
PAIR = 2 * HEAD_DIM
SIDE = 3 * HALF
EPS = 1e-06
F32 = jnp.float32
B16 = jnp.bfloat16
SWAP = ((0, 1), (1, 0))
SCALE = HEAD_DIM ** (-0.5)
ROOT = (2.0 / 3.141592653589793) ** 0.5
CUBE = 0.044715
PER_TILE = 2
VMEM_BYTES = 60 * 1024 * 1024


def dot(left, right):
    return jnp.dot(left, right, preferred_element_type=F32)


def dot_nt(left, right):
    return lax.dot_general(left, right, (((1,), (1,)), ((), ())), preferred_element_type=F32)


def dot_tn(left, right):
    return lax.dot_general(left, right, (((0,), (0,)), ((), ())), preferred_element_type=F32)


def normalize(values):
    center = jnp.mean(values, axis=1, keepdims=True)
    spread = jnp.mean(values * values, axis=1, keepdims=True) - center * center
    inverse = lax.rsqrt(spread + EPS)
    return (values - center) * inverse, inverse


def norm_grad(upstream, normal, inverse):
    first_mean = jnp.mean(upstream, axis=1, keepdims=True)
    second_mean = jnp.mean(upstream * normal, axis=1, keepdims=True)
    return inverse * (upstream - first_mean - normal * second_mean)


def both(own_ref, oth_ref):
    return jnp.concatenate([own_ref[...], oth_ref[...]], axis=1).astype(F32)


def spread_rows(mod_ref, number):
    rows = [
        jnp.broadcast_to(mod_ref[latent, number : number + 1, :], (SEQ, D))
        for latent in range(mod_ref.shape[0])
    ]
    return rows[0] if len(rows) == 1 else jnp.concatenate(rows, axis=0)


def store_sums(out_ref, number, values):
    for latent in range(out_ref.shape[0]):
        out_ref[latent, number : number + 1, :] = jnp.sum(
            values[latent * SEQ : (latent + 1) * SEQ], axis=0, keepdims=True
        )


def attend_copies(pieces, weight, sem):
    copies = []
    for number, piece in enumerate(pieces):
        row, col = number % 2, number // 2
        for kind in range(3):
            copies.append(
                pltpu.make_async_copy(
                    piece.at[kind],
                    weight.at[pl.ds(row * HALF, HALF), pl.ds(col * SIDE + kind * HALF, HALF)],
                    sem.at[len(copies)],
                )
            )
    return copies


def grid_copies(pieces, weight, sem, first_is_row):
    copies = []
    for number, piece in enumerate(pieces):
        row, col = number % 2, number // 2
        across, down = piece.shape[1], piece.shape[0]
        top, left = (row, col) if first_is_row else (col, row)
        copies.append(
            pltpu.make_async_copy(
                piece,
                weight.at[pl.ds(top * down, down), pl.ds(left * across, across)],
                sem.at[number],
            )
        )
    return copies


def forward_kernel(
    tok_own, tok_oth, mod, bias, w0, w1, w2, w3, first_ref, qkv_ref, att_ref, weight, sem
):
    @pl.when(pl.program_id(0) == 0)
    def _():
        copies = attend_copies((w0, w1, w2, w3), weight, sem)
        for copy in copies:
            copy.start()
        for copy in copies:
            copy.wait()

    normal, _ = normalize(both(tok_own, tok_oth))
    first = (normal * (1.0 + spread_rows(mod, 1)) + spread_rows(mod, 0)).astype(B16)
    first_ref[...] = first
    qkv_ref[...] = (dot(first, weight[...]) + bias[...]).astype(B16)
    low = lax.broadcasted_iota(jnp.int32, (SEQ, PAIR), 1) < HEAD_DIM
    for col in range(2):
        for pair in range(HALF // PAIR):
            base = col * SIDE + pair * PAIR
            q_part = qkv_ref[:, base : base + PAIR] * SCALE
            k_part = qkv_ref[:, base + HALF : base + HALF + PAIR]
            v_part = qkv_ref[:, base + D : base + D + PAIR]
            outs = []
            for keep in (low, jnp.logical_not(low)):
                scores = dot_nt(jnp.where(keep, q_part, 0).astype(B16), k_part)
                exponent = jnp.exp(scores - jnp.max(scores, axis=1, keepdims=True))
                probs = exponent * (1.0 / jnp.sum(exponent, axis=1, keepdims=True))
                outs.append(dot(probs.astype(B16), v_part))
            at = col * HALF + pair * PAIR
            att_ref[:, at : at + PAIR] = jnp.where(low, outs[0], outs[1]).astype(B16)


def middle_kernel(
    tok_own, tok_oth, cot_own, cot_oth, att, mod, outbias, expbias, shrbias,
    o0, o1, o2, o3, x0, x1, x2, x3, s0, s1, s2, s3,
    res_own, res_oth, second_ref, act_own, act_oth, dh_own, dh_oth, e_one_ref, e_two_ref,
    d_mid_ref, d_att_ref, mod_ref, sum_ref,
    w_out, w_exp, w_shr, sem_out, sem_exp, sem_shr,
):
    @pl.when(pl.program_id(0) == 0)
    def _():
        copies = (
            grid_copies((o0, o1, o2, o3), w_out, sem_out, False)
            + grid_copies((x0, x1, x2, x3), w_exp, sem_exp, True)
            + grid_copies((s0, s1, s2, s3), w_shr, sem_shr, False)
        )
        for copy in copies:
            copy.start()
        for copy in copies:
            copy.wait()

    branch_one = dot(att[...], w_out[...]) + outbias[...]
    middle = both(tok_own, tok_oth) + spread_rows(mod, 2) * branch_one
    normal, inverse = normalize(middle)
    second = (normal * (1.0 + spread_rows(mod, 4)) + spread_rows(mod, 3)).astype(B16)
    second_ref[...] = second
    upstream = both(cot_own, cot_oth)
    e_two = (spread_rows(mod, 5) * upstream).astype(B16)
    e_two_ref[...] = e_two
    branch_two = shrbias[...]
    d_second = 0.0
    for part in range(FF // D):
        at = part * D
        hidden = dot(second, w_exp[:, at : at + D]) + expbias[:, at : at + D]
        square = hidden * hidden
        bend = jnp.tanh(hidden * (ROOT + (ROOT * CUBE) * square))
        share = 0.5 + 0.5 * bend
        active = (hidden * share).astype(B16)
        slope = share + (0.5 * hidden) * (1.0 - bend * bend) * (ROOT + (3.0 * ROOT * CUBE) * square)
        branch_two = branch_two + dot(active, w_shr[at : at + D, :])
        d_hidden = (dot_nt(e_two, w_shr[at : at + D, :]) * slope).astype(B16)
        d_second = d_second + dot_nt(d_hidden, w_exp[:, at : at + D])
        act_ref, dh_ref = (act_own, dh_own) if 2 * at < FF else (act_oth, dh_oth)
        into = at % (FF // 2)
        act_ref[:, into : into + D] = active
        dh_ref[:, into : into + D] = d_hidden
        sum_ref[0, :, 2 * D + at : 2 * D + at + D] = jnp.sum(
            d_hidden.astype(F32), axis=0, keepdims=True
        )
    result = (middle + spread_rows(mod, 5) * branch_two).astype(B16)
    res_own[...] = result[:, :HALF]
    res_oth[...] = result[:, HALF:]
    store_sums(mod_ref, 3, upstream * branch_two)
    store_sums(mod_ref, 1, d_second)
    store_sums(mod_ref, 2, d_second * normal)
    d_middle = upstream + norm_grad(d_second * (1.0 + spread_rows(mod, 4)), normal, inverse)
    d_mid_ref[...] = d_middle
    store_sums(mod_ref, 0, d_middle * branch_one)
    e_one = (spread_rows(mod, 2) * d_middle).astype(B16)
    e_one_ref[...] = e_one
    d_att_ref[...] = dot_nt(e_one, w_out[...]).astype(B16)
    sum_ref[0, :, :D] = jnp.sum(e_one.astype(F32), axis=0, keepdims=True)
    sum_ref[0, :, D : 2 * D] = jnp.sum(e_two.astype(F32), axis=0, keepdims=True)


def backward_kernel(
    tok_own, tok_oth, mod, qkv, d_att, d_mid, w0, w1, w2, w3,
    dqkv_own, dqkv_oth, grad_own, grad_oth, mod_ref, sum_ref, weight, sem,
):
    @pl.when(pl.program_id(0) == 0)
    def _():
        copies = attend_copies((w0, w1, w2, w3), weight, sem)
        for copy in copies:
            copy.start()
        for copy in copies:
            copy.wait()

    low = lax.broadcasted_iota(jnp.int32, (SEQ, PAIR), 1) < HEAD_DIM
    for col in range(2):
        out_ref = (dqkv_own, dqkv_oth)[col]
        for pair in range(HALF // PAIR):
            base = col * SIDE + pair * PAIR
            q_part = qkv[:, base : base + PAIR]
            k_part = qkv[:, base + HALF : base + HALF + PAIR]
            v_part = qkv[:, base + D : base + D + PAIR]
            d_part = d_att[:, col * HALF + pair * PAIR : col * HALF + (pair + 1) * PAIR]
            queries, keys, values = [], [], []
            for keep in (low, jnp.logical_not(low)):
                scores = dot_nt(jnp.where(keep, k_part * SCALE, 0).astype(B16), q_part)
                exponent = jnp.exp(scores - jnp.max(scores, axis=0, keepdims=True))
                probs = exponent * (1.0 / jnp.sum(exponent, axis=0, keepdims=True))
                d_probs = dot_nt(jnp.where(keep, v_part, 0).astype(B16), d_part)
                weighted = probs * d_probs
                d_scores = (weighted - probs * jnp.sum(weighted, axis=0, keepdims=True)).astype(B16)
                values.append(dot(probs.astype(B16), d_part))
                keys.append(dot(d_scores, q_part))
                queries.append(dot_tn(d_scores, k_part))
            for kind, (first, then, factor) in enumerate(
                ((*queries, SCALE), (*keys, SCALE), (*values, 1.0))
            ):
                at = kind * HALF + pair * PAIR
                piece = (jnp.where(low, first, then) * factor).astype(B16)
                out_ref[:, at : at + PAIR] = piece
                sum_ref[0, :, col * SIDE + at : col * SIDE + at + PAIR] = jnp.sum(
                    piece.astype(F32), axis=0, keepdims=True
                )
    d_first = dot_nt(dqkv_own[...], weight[:, :SIDE]) + dot_nt(dqkv_oth[...], weight[:, SIDE:])
    normal, inverse = normalize(both(tok_own, tok_oth))
    store_sums(mod_ref, 0, d_first)
    store_sums(mod_ref, 1, d_first * normal)
    grad = (
        d_mid[...] + norm_grad(d_first * (1.0 + spread_rows(mod, 1)), normal, inverse)
    ).astype(B16)
    grad_own[...] = grad[:, :HALF]
    grad_oth[...] = grad[:, HALF:]


def tiles(rows, width):
    return pl.BlockSpec((rows, width), lambda step: (step, 0))


def stacked(count, rows, width):
    return pl.BlockSpec((count, rows, width), lambda step: (step, 0, 0))


def fixed(width):
    return pl.BlockSpec((1, width), lambda step: (0, 0))


def anywhere(count):
    return [pl.BlockSpec(memory_space=pl.ANY)] * count


def params():
    return pltpu.CompilerParams(
        vmem_limit_bytes=VMEM_BYTES, dimension_semantics=("arbitrary",)
    )


def call_forward(tok_own, tok_oth, modulation, bias, pieces):
    count = tok_own.shape[0]
    latents = count // SEQ
    return pl.pallas_call(
        forward_kernel,
        grid=(latents,),
        in_specs=[tiles(SEQ, HALF)] * 2 + [stacked(1, 6, D), fixed(2 * SIDE)] + anywhere(4),
        out_specs=[tiles(SEQ, D), tiles(SEQ, 2 * SIDE), tiles(SEQ, D)],
        out_shape=[
            jax.ShapeDtypeStruct((count, D), B16),
            jax.ShapeDtypeStruct((count, 2 * SIDE), B16),
            jax.ShapeDtypeStruct((count, D), B16),
        ],
        scratch_shapes=[pltpu.VMEM((D, 2 * SIDE), B16), pltpu.SemaphoreType.DMA((12,))],
        compiler_params=params(),
        cost_estimate=pl.CostEstimate(
            flops=14 * 10**9, bytes_accessed=16 * 10**6, transcendentals=count * SEQ * 12
        ),
        name="forward",
    )(tok_own, tok_oth, modulation, bias, *pieces)


def call_middle(tok, cot, att, modulation, biases, out_pieces, exp_pieces, shr_pieces):
    count = att.shape[0]
    latents = count // SEQ
    per_tile = PER_TILE if latents % PER_TILE == 0 else 1
    rows = per_tile * SEQ
    steps = latents // per_tile
    halves = [tiles(rows, HALF)] * 2

    def shape(width, kind=B16):
        return jax.ShapeDtypeStruct((count, width), kind)

    return pl.pallas_call(
        middle_kernel,
        grid=(steps,),
        in_specs=halves
        + halves
        + [tiles(rows, D), stacked(per_tile, 6, D), fixed(D), fixed(FF), fixed(D)]
        + anywhere(12),
        out_specs=halves
        + [tiles(rows, D)]
        + [tiles(rows, FF // 2)] * 4
        + [tiles(rows, D)] * 4
        + [stacked(per_tile, 4, D), stacked(1, 1, 2 * D + FF)],
        out_shape=[shape(HALF), shape(HALF), shape(D)]
        + [shape(FF // 2)] * 4
        + [shape(D), shape(D), shape(D, F32), shape(D)]
        + [
            jax.ShapeDtypeStruct((latents, 4, D), F32),
            jax.ShapeDtypeStruct((steps, 1, 2 * D + FF), F32),
        ],
        scratch_shapes=[
            pltpu.VMEM((D, D), B16),
            pltpu.VMEM((D, FF), B16),
            pltpu.VMEM((FF, D), B16),
            pltpu.SemaphoreType.DMA((4,)),
            pltpu.SemaphoreType.DMA((4,)),
            pltpu.SemaphoreType.DMA((4,)),
        ],
        compiler_params=params(),
        cost_estimate=pl.CostEstimate(
            flops=30 * 10**9, bytes_accessed=50 * 10**6, transcendentals=count * FF
        ),
        name="middle",
    )(*tok, *cot, att, modulation, *biases, *out_pieces, *exp_pieces, *shr_pieces)


def call_backward(tok, modulation, qkv, d_att, d_mid, pieces):
    count = d_att.shape[0]
    latents = count // SEQ
    return pl.pallas_call(
        backward_kernel,
        grid=(latents,),
        in_specs=[tiles(SEQ, HALF)] * 2
        + [stacked(1, 6, D), tiles(SEQ, 2 * SIDE), tiles(SEQ, D), tiles(SEQ, D)]
        + anywhere(4),
        out_specs=[tiles(SEQ, SIDE)] * 2
        + [tiles(SEQ, HALF)] * 2
        + [stacked(1, 2, D), stacked(1, 1, 2 * SIDE)],
        out_shape=[jax.ShapeDtypeStruct((count, SIDE), B16)] * 2
        + [jax.ShapeDtypeStruct((count, HALF), B16)] * 2
        + [
            jax.ShapeDtypeStruct((latents, 2, D), F32),
            jax.ShapeDtypeStruct((latents, 1, 2 * SIDE), F32),
        ],
        scratch_shapes=[pltpu.VMEM((D, 2 * SIDE), B16), pltpu.SemaphoreType.DMA((12,))],
        compiler_params=params(),
        cost_estimate=pl.CostEstimate(
            flops=25 * 10**9, bytes_accessed=20 * 10**6, transcendentals=count * SEQ * 12
        ),
        name="backward",
    )(*tok, modulation, qkv, d_att, d_mid, *pieces)


def swap_row(values):
    return lax.ppermute(values, "row", SWAP)


def swap_col(values):
    return lax.ppermute(values, "col", SWAP)


def swap_dp(values, distance):
    size = lax.axis_size("dp")
    return lax.ppermute(values, "dp", [(place, place ^ distance) for place in range(size)])


def distances():
    size = lax.axis_size("dp")
    return [1 << bit for bit in range(size.bit_length() - 1)]


def after(values, *earlier):
    return lax.optimization_barrier((values,) + earlier)[0]


def halves(values, dim):
    size = values.shape[dim] // 2
    return lax.slice_in_dim(values, 0, size, axis=dim), lax.slice_in_dim(
        values, size, 2 * size, axis=dim
    )


def pick(values, place):
    size = values.shape[0] // 2
    kept = lax.dynamic_slice_in_dim(values, place * size, size, 0)
    sent = lax.dynamic_slice_in_dim(values, (1 - place) * size, size, 0)
    return kept, sent


def in_order(place, mine, theirs):
    return jnp.concatenate(
        [jnp.where(place == 0, mine, theirs), jnp.where(place == 0, theirs, mine)], axis=0
    )


def reduce_grid(own, other, row_dim):
    arrived = swap_col(other().astype(B16))
    total = own() + arrived.astype(F32)
    mine, theirs = halves(total, row_dim)
    return mine + swap_row(theirs.astype(B16)).astype(F32)


def sum_dp(values):
    me = lax.axis_index("dp")
    for distance in distances():
        kept, sent = pick(values, (me // distance) % 2)
        values = kept + swap_dp(sent.astype(B16), distance).astype(F32)
    values = values.astype(B16)
    for distance in reversed(distances()):
        values = in_order((me // distance) % 2, values, swap_dp(values, distance))
    return values.astype(F32)


def gather_dp(values):
    for distance in distances():
        values = jnp.concatenate([values, swap_dp(values, distance)], axis=0)
    return values


def shards(
    tokens, condition, adaptive, adabias, attend, attbias, outproj, outbias,
    expand, expbias, shrink, shrbias, cotangent,
):
    row = lax.axis_index("row")
    col = lax.axis_index("col")

    raw_condition = condition.astype(F32)
    act_cond = jax.nn.silu(raw_condition).astype(B16)
    mod_terms = jnp.einsum("ld,kde->lke", act_cond, adaptive, preferred_element_type=F32)
    kept, sent = pick(mod_terms, col)
    mod_rows = kept + swap_col(sent) + adabias.astype(F32)
    kept, sent = pick(mod_rows, row)
    modulation = jnp.concatenate([kept, swap_row(sent)], axis=2)

    tok_own, sent = pick(tokens, row)
    tok_oth = swap_row(sent)
    tok = (tok_own, tok_oth)

    def pieces(values):
        over = swap_row(values)
        return values, over, swap_col(values), swap_col(over)

    attend_pieces = pieces(after(attend, tok_oth))
    ready = attend_pieces[1]
    out_pieces = pieces(after(outproj, ready))
    exp_pieces = pieces(after(expand, ready))
    shr_pieces = pieces(after(shrink, ready))
    cot_own, sent = pick(cotangent, row)
    cot_oth = swap_row(after(sent, ready))

    by_col = jnp.concatenate([attbias.reshape(-1), expbias]).astype(F32)
    by_row = jnp.concatenate([outbias, shrbias]).astype(F32)
    by_col = (by_col, swap_col(by_col))
    by_row = (by_row, swap_row(by_row))
    blank = jnp.zeros((HALF,), F32)
    bias = jnp.concatenate(
        [piece for part in by_col for piece in (part[:HALF], blank, part[HALF:D])]
    )[None]
    exp_bias = jnp.concatenate([part[D:] for part in by_col])[None]
    out_bias = jnp.concatenate([part[:HALF] for part in by_row])[None]
    shr_bias = jnp.concatenate([part[HALF:] for part in by_row])[None]

    first, qkv, attended = call_forward(tok_own, tok_oth, modulation, bias, attend_pieces)
    (
        res_own, res_oth, second, act_own, act_oth, dh_own, dh_oth, e_one, e_two,
        d_middle, d_attended, mod_late, sums_late,
    ) = call_middle(
        tok, (cot_own, cot_oth), attended, modulation, (out_bias, exp_bias, shr_bias),
        out_pieces, exp_pieces, shr_pieces,
    )
    result = in_order(row, res_own, swap_row(res_oth))
    shrink_part = reduce_grid(lambda: dot_tn(act_own, e_two), lambda: dot_tn(act_oth, e_two), 1)
    expand_part = reduce_grid(lambda: dot_tn(second, dh_own), lambda: dot_tn(second, dh_oth), 0)
    att_own, att_oth = halves(attended, 1)
    outproj_part = reduce_grid(lambda: dot_tn(att_own, e_one), lambda: dot_tn(att_oth, e_one), 1)
    dqkv_own, dqkv_oth, grad_own, grad_oth, mod_early, sums_early = call_backward(
        tok, modulation, qkv, d_attended, d_middle, attend_pieces
    )
    attend_part = reduce_grid(lambda: dot_tn(first, dqkv_own), lambda: dot_tn(first, dqkv_oth), 0)
    input_gradient = in_order(row, grad_own, swap_row(grad_oth))
    shrink_grad = sum_dp(shrink_part)
    expand_grad = sum_dp(expand_part)
    outproj_grad = sum_dp(outproj_part)
    attend_grad = sum_dp(attend_part).reshape(HALF, 3, HALF).transpose(1, 0, 2)

    d_modulation = jnp.concatenate([mod_early, mod_late], axis=1).astype(B16)
    mine, theirs = halves(d_modulation, 2)
    mod_block = in_order(row, mine, swap_row(theirs))
    mod_group = in_order(col, mod_block, swap_col(mod_block))
    mod_all = gather_dp(mod_group)
    cond_all = gather_dp(act_cond)
    adabias_grad = jnp.sum(mod_all, axis=0, dtype=F32)
    adaptive_grad = jnp.einsum("ld,lke->kde", cond_all, mod_all, preferred_element_type=F32)
    d_act = jnp.einsum("lke,kde->ld", mod_group, adaptive, preferred_element_type=F32)
    d_act = d_act + swap_row(d_act)
    condition_gradient = jax.vjp(jax.nn.silu, raw_condition)[1](d_act)[0].astype(B16)

    sums_late = jnp.sum(sums_late, axis=(0, 1))
    sums_early = jnp.sum(sums_early, axis=(0, 1))
    mine, theirs = halves(sums_late[: 2 * D].reshape(2, D), 1)
    row_sums = mine + swap_row(theirs)
    row_sums = row_sums + swap_col(row_sums)
    wide = halves(sums_late[2 * D :], 0)
    narrow = halves(sums_early, 0)
    mine, theirs = [jnp.concatenate([narrow[side], wide[side]]) for side in range(2)]
    col_sums = mine + swap_col(theirs)
    col_sums = col_sums + swap_row(col_sums)
    sums = jnp.concatenate([row_sums.reshape(-1), col_sums])
    for distance in distances():
        sums = sums + swap_dp(sums, distance)
    outbias_grad = sums[:HALF]
    shrbias_grad = sums[HALF:D]
    attbias_grad = jnp.stack([sums[D : D + HALF], sums[2 * D : 2 * D + HALF]])
    expbias_grad = sums[D + SIDE :]
    return (
        result, input_gradient, condition_gradient, adaptive_grad, adabias_grad, attend_grad,
        attbias_grad, outproj_grad, outbias_grad, expand_grad, expbias_grad, shrink_grad,
        shrbias_grad,
    )


def solution(mesh):
    placed = (
        P(("dp", "col"), "row"),
        P("dp", "col"),
        P(None, "col", "row"),
        P(None, "row"),
        P(None, "row", "col"),
        P(None, "col"),
        P("col", "row"),
        P("row"),
        P("row", "col"),
        P("col"),
        P("col", "row"),
        P("row"),
        P(("dp", "col"), "row"),
    )
    return jax.shard_map(
        shards,
        mesh=mesh,
        in_specs=placed,
        out_specs=(
            P(("dp", "col"), "row"),
            P(("dp", "col"), "row"),
            P("dp", "col"),
            P(None, "col", "row"),
            P(None, "row"),
            P(None, "row", "col"),
            P(None, "col"),
            P("col", "row"),
            P("row"),
            P("row", "col"),
            P("col"),
            P("col", "row"),
            P("row"),
        ),
        check_vma=False,
    )
```

time: 2080 us -> 495 us (0.24)
  waiting for transfers between devices: 1630 us -> 242 us
  matrix products: 159 us -> 35.5 us
  Pallas kernels: 0 us -> 97.2 us
  blocking collectives: 75.2 us -> 0 us
  other arithmetic: 94.7 us -> 21.4 us
  local copies, waits for them, and re-layouts: 98 us -> 32.5 us
  starting transfers between devices: 2.35 us -> 58.8 us
    reduce_scatter x9 -> x0, waiting for transfers between devices: 866 us -> none  [the longest x4 839 us: contract_rows(): lax.psum_scatter(product(left, weight), 'row', scatter_dimension=0, tiled...]
    all_gather x8 -> x0, waiting for transfers between devices: 495 us -> none  [the longest x4 458 us: gather_rows(): return lax.all_gather(values, 'row', axis=0, tiled=True)]
    psum x1 -> x0, waiting for transfers between devices: 262 us -> none  [shards(): lax.psum((adaptive_grad, adabias_grad, attend_grad, attbias_grad, outproj...]
    ppermute x0 -> x68, waiting for transfers between devices: none -> 242 us  [the longest x18 153 us: swap_row(): return lax.ppermute(values, 'row', SWAP)]
    dot_general x42 -> x10, matrix products: 157 us -> 35.2 us  [the longest x8 32.1 us: dot_tn(): lax.dot_general(left, right, (((0,), (0,)), ((), ())), preferred_element_...]
    pallas_call x0 -> x3, Pallas kernels: none -> 97.2 us  [the longest x1 49.3 us: call_middle(): pl.pallas_call(middle_kernel, grid=(steps,), in_specs=halves + halves + [...]
    psum x5 -> x0, blocking collectives: 73.1 us -> none  [the longest x1 39.9 us: shards(): lax.psum((adaptive_grad, adabias_grad, attend_grad, attbias_grad, outproj...]
    ppermute x0 -> x68, starting transfers between devices: none -> 58.8 us  [the longest x33 33.1 us: swap_dp(): lax.ppermute(values, 'dp', [(place, place ^ distance) for place in range(...]
  transfers between devices with their start and end apart: 18 -> 68, of which waited for: 17 -> 36; matrix products, arithmetic and copies ran while one was open for 5% -> 16% of each run, Pallas kernels for 0% -> 10%
where the time goes in v1:
time: 495 us; the launch traced here: 490 us
  waiting for transfers between devices  242 us (49%)
  Pallas kernels  97.2 us (20%)
  starting transfers between devices  58.8 us (12%)
  matrix products  35.5 us (7%)
  local copies, waits for them, and re-layouts  32.5 us (7%)
  other arithmetic  21.4 us (4%)
    ppermute x18, waiting for transfers between devices, swap_row(): return lax.ppermute(values, 'row', SWAP)  153 us
    ppermute x33, waiting for transfers between devices, swap_dp(): lax.ppermute(values, 'dp', [(place, place ^ distance) for place in range(...  88.4 us
    pallas_call x1, Pallas kernels, call_middle(): pl.pallas_call(middle_kernel, grid=(steps,), in_specs=halves + halves + [...  49.3 us
    ppermute x33, starting transfers between devices, swap_dp(): lax.ppermute(values, 'dp', [(place, place ^ distance) for place in range(...  33.1 us
    dot_general x8, matrix products, dot_tn(): lax.dot_general(left, right, (((0,), (0,)), ((), ())), preferred_element_...  32.1 us
    pallas_call x1, Pallas kernels, call_backward(): pl.pallas_call(backward_kernel, grid=(latents,), in_specs=[tiles(SEQ, HAL...  31.4 us
    ppermute x18, starting transfers between devices, swap_row(): return lax.ppermute(values, 'row', SWAP)  22.8 us
    pallas_call x1, Pallas kernels, call_forward(): pl.pallas_call(forward_kernel, grid=(latents,), in_specs=[tiles(SEQ, HALF...  16.5 us
  transfers between devices with their start and end apart: 68, of which 36 were waited for; matrix products, arithmetic and copies ran while one was open for 16% of the time, Pallas kernels for 10%

profile of v1, /device:TPU:0, one launch (start us, length us, event | category | flops | bytes accessed | tf_op | source)
XLA Modules:
  0.0 489.7 jit_solution(2644020481441087765)
XLA Ops:
  0.7 2.8 constant_dynamic-slice_fusion.6
  3.5 3.0 collective-permute-start
  10.3 14.2 %collective-permute-done.tok_oth = bf16[1024,384]{1,0:T(8,128)(2,1)} collective-permute-done((bf16[1024,384]{1,0:T(8,128)(2,1)}, bf16[1024,384]{1,0:T(8,128)(2,1)}, u32[]{:S(2)}, u32[]{:S(2)}) %collective-permute-start) | collective-permute-done | bytes 786464 | tf_op jit(solution)/shard_map/ppermute | solution.py:368
  24.4 1.7 collective-permute-start.1
  30.8 14.8 %collective-permute-done.1.w1 = bf16[3,384,384]{2,1,0:T(8,128)(2,1)} collective-permute-done((bf16[3,384,384]{2,1,0:T(8,128)(2,1)}, bf16[3,384,384]{2,1,0:T(8,128)(2,1)}, u32[]{:S(2)}, u32[]{:S(2)}) %collective-permute-start.1) | collective-permute-done | bytes 884768 | tf_op jit(solution)/shard_map/ppermute | solution.py:368
  47.6 1.5 collective-permute-start.4
  50.3 48.0 %collective-permute-done.4 = f32[4,6,384]{2,1,0:T(8,128)S(1)} collective-permute-done((f32[4,6,384]{2,1,0:T(8,128)S(1)}, f32[4,6,384]{2,1,0:T(8,128)S(1)}, u32[]{:S(2)}, u32[]{:S(2)}) %collective-permute-start.4) | collective-permute-done | bytes 36896 | tf_op jit(solution)/shard_map/ppermute | solution.py:368
  102.0 3.2 collective-permute-done.9.o1
  112.1 16.5 %forward.1 = (bf16[1024,768]{1,0:T(8,128)(2,1)}, bf16[1024,2304]{1,0:T(8,128)(2,1)}, bf16[1024,768]{1,0:T(8,128)(2,1)}) custom-call(bf16[1024,384]{1,0:T(8,128)(2,1)} %get-tuple-element.104.tok_own, bf16[1024,384]{1,0:T(8,128)(2,1)} %collective-permute-done.tok_oth, f32[4,6,768]{2,1,0:T(8,128)} %pad_maximum_fusion.11.mod, f32[1,2304]{1,0:T(1,128)} %broadcast_in_dim.17.bias, ...), custom_call_target="tpu_custom_call" | custom-call | flops 14000000000 | bytes 16000000 | tf_op jit(solution)/shard_map/forward/pallas_call | solution.py:275
  128.6 2.0 collective-permute-done.2.cot_oth
  130.6 49.3 %middle.1 = (bf16[1024,384]{1,0:T(8,128)(2,1)}, bf16[1024,384]{1,0:T(8,128)(2,1)}, bf16[1024,768]{1,0:T(8,128)(2,1)}, bf16[1024,1536]{1,0:T(8,128)(2,1)}, bf16[1...) custom-call(bf16[1024,384]{1,0:T(8,128)(2,1)} %get-tuple-element.104, ...), custom_call_target="tpu_custom_call" | custom-call | flops 30000001024 | bytes 50000000 | tf_op jit(solution)/shard_map/middle/pallas_call | solution.py:305
  180.0 6.7 %convolution_convert_fusion = bf16[1536,768]{1,0:T(8,128)(2,1)} fusion(bf16[1024,1536]{1,0:T(8,128)(2,1)} %get-tuple-element.66, bf16[1024,768]{1,0:T(8,128)(2,1)} %get-tuple-element.65), kind=kOutput, calls=%fused_computation.3 | convolution fusion | flops 2417098752 | bytes 7077888 | tf_op jit(solution)/shard_map/dot_general | solution.py:37
  186.6 4.1 convolution_convert_fusion.1
  191.2 1.6 convolution_convert_fusion.3
  194.1 31.4 %backward.1 = (bf16[1024,1152]{1,0:T(8,128)(2,1)}, bf16[1024,1152]{1,0:T(8,128)(2,1)}, bf16[1024,384]{1,0:T(8,128)(2,1)}, bf16[1024,384]{1,0:T(8,128)(2,1)}, f32...) custom-call(bf16[1024,384]{1,0:T(8,128)(2,1)} %get-tuple-element.104.tok_own, bf16[1024,384]{1,0:T(8,128)(2,1)} %collective-permute-done.tok_oth, ...), custom_call_target="tpu_custom_call" | custom-call | flops 24999999488 | bytes 20000000 | tf_op jit(solution)/shard_map/backward/pallas_call | solution.py:343
  230.9 1.8 collective-permute-done.20
  234.7 2.6 collective-permute-done.41
  238.5 5.1 %convolution_convert_fusion.2 = bf16[768,1152]{1,0:T(8,128)(2,1)} fusion(bf16[1024,768]{1,0:T(8,128)(2,1)S(1)} %copy-done.30, bf16[1024,1152]{1,0:T(8,128)(2,1)} %get-tuple-element.57), kind=kOutput, calls=%fused_computation.5 | convolution fusion | flops 1812824064 | bytes 5701632 | tf_op jit(solution)/shard_map/dot_general | solution.py:37
  243.6 2.7 collective-permute-start.43
  246.9 1.5 collective-permute-start.23
  248.5 1.5 collective-permute-start.22
  250.6 1.7 collective-permute-done.22
  256.6 3.8 collective-permute-done.24
  260.6 3.6 collective-permute-done.27
  264.2 2.8 collective-permute-start.25
  267.1 13.5 %collective-permute-done.25 = bf16[64,6,384]{2,1,0:T(8,128)(2,1)S(1)} collective-permute-done((bf16[64,6,384]{2,1,0:T(8,128)(2,1)S(1)}, bf16[64,6,384]{2,1,0:T(8,128)(2,1)S(1)}, u32[]{:S(2)}, u32[]{:S(2)}) %collective-permute-start.25) | collective-permute-done | bytes 294944 | tf_op jit(solution)/shard_map/ppermute | solution.py:377
  280.6 1.5 collective-permute-start.19
  282.4 1.9 convolution_add_fusion.1
  287.9 2.5 convolution_bitcast_fusion
  290.4 5.3 %copy.37 = f32[6,384,384]{2,1,0:T(8,128)} copy(f32[6,384,384]{1,2,0:T(8,128)} %convolution_bitcast_fusion) | data formatting | bytes 7077888
  295.8 10.7 %collective-permute-done.45 = bf16[384,384]{1,0:T(8,128)(2,1)} collective-permute-done((bf16[384,384]{1,0:T(8,128)(2,1)}, bf16[384,384]{1,0:T(8,128)(2,1)}, u32[]{:S(2)}, u32[]{:S(2)}) %collective-permute-start.45) | collective-permute-done | bytes 294944 | tf_op jit(solution)/shard_map/ppermute | solution.py:368
  309.4 3.6 collective-permute-done.46
  313.0 1.5 collective-permute-start.18
  314.9 4.2 collective-permute-done.47
  319.4 10.8 %collective-permute-done.18 = bf16[1024,384]{1,0:T(8,128)(2,1)S(1)} collective-permute-done((bf16[1024,384]{1,0:T(8,128)(2,1)S(1)}, bf16[1024,384]{1,0:T(8,128)(2,1)S(1)}, u32[]{:S(2)}, u32[]{:S(2)}) %collective-permute-start.18) | collective-permute-done | bytes 786464 | tf_op jit(solution)/shard_map/ppermute | solution.py:368
  330.5 3.8 convolution_add_fusion
  334.4 1.6 collective-permute-start.30
  336.0 1.4 collective-permute-start.50
  338.8 1.7 collective-permute-done.50
  341.4 11.5 %collective-permute-done.30 = bf16[384,1152]{1,0:T(8,128)(2,1)S(1)} collective-permute-done((bf16[384,1152]{1,0:T(8,128)(2,1)S(1)}, bf16[384,1152]{1,0:T(8,128)(2,1)S(1)}, u32[]{:S(2)}, u32[]{:S(2)}) %collective-permute-start.30) | collective-permute-done | bytes 884768 | tf_op jit(solution)/shard_map/ppermute | solution.py:368
  356.2 5.3 %collective-permute-done.31 = bf16[192,1152]{1,0:T(8,128)(2,1)S(1)} collective-permute-done((bf16[192,1152]{1,0:T(8,128)(2,1)S(1)}, bf16[192,1152]{1,0:T(8,128)(2,1)S(1)}, u32[]{:S(2)}, u32[]{:S(2)}) %collective-permute-start.31) | collective-permute-done | bytes 442400 | tf_op jit(solution)/shard_map/ppermute | solution.py:377
  362.0 4.6 convert_add_fusion
  366.8 1.6 collective-permute-start.61
  368.9 2.7 collective-permute-start.33
  371.5 4.3 convert_add_fusion.1
  378.0 17.7 %collective-permute-done.61 = bf16[1536,384]{1,0:T(8,128)(2,1)S(1)} collective-permute-done((bf16[1536,384]{1,0:T(8,128)(2,1)S(1)}, bf16[1536,384]{1,0:T(8,128)(2,1)S(1)}, u32[]{:S(2)}, u32[]{:S(2)}) %collective-permute-start.61) | collective-permute-done | bytes 1179680 | tf_op jit(solution)/shard_map/ppermute | solution.py:368
  396.7 2.0 collective-permute-start.35
  398.7 15.8 %collective-permute-done.53 = bf16[384,1536]{1,0:T(8,128)(2,1)S(1)} collective-permute-done((bf16[384,1536]{1,0:T(8,128)(2,1)S(1)}, bf16[384,1536]{1,0:T(8,128)(2,1)S(1)}, u32[]{:S(2)}, u32[]{:S(2)}) %collective-permute-start.53) | collective-permute-done | bytes 1179680 | tf_op jit(solution)/shard_map/ppermute | solution.py:368
  418.1 1.7 collective-permute-start.63
  419.8 8.8 %collective-permute-done.54 = bf16[192,1536]{1,0:T(8,128)(2,1)S(1)} collective-permute-done((bf16[192,1536]{1,0:T(8,128)(2,1)S(1)}, bf16[192,1536]{1,0:T(8,128)(2,1)S(1)}, u32[]{:S(2)}, u32[]{:S(2)}) %collective-permute-start.54) | collective-permute-done | bytes 589856 | tf_op jit(solution)/shard_map/ppermute | solution.py:377
  430.5 1.7 collective-permute-start.55
  434.6 1.4 concatenate.130
  436.1 2.1 concatenate.131
  439.4 2.3 collective-permute-start.64
  443.5 9.5 %collective-permute-done.64 = bf16[192,384]{1,0:T(8,128)(2,1)S(1)} collective-permute-done((bf16[192,384]{1,0:T(8,128)(2,1)S(1)}, bf16[192,384]{1,0:T(8,128)(2,1)S(1)}, u32[]{:S(2)}, u32[]{:S(2)}) %collective-permute-start.64) | collective-permute-done | bytes 147488 | tf_op jit(solution)/shard_map/ppermute | solution.py:377
  453.1 2.2 collective-permute-done.56
  456.1 4.6 collective-permute-done.65
  460.8 2.7 collective-permute-done.57
  463.8 4.0 collective-permute-done.66
  468.9 2.1 collective-permute-done.58
  474.0 7.0 %collective-permute-done.67 = bf16[768,384]{1,0:T(8,128)(2,1)S(1)} collective-permute-done((bf16[768,384]{1,0:T(8,128)(2,1)S(1)}, bf16[768,384]{1,0:T(8,128)(2,1)S(1)}, u32[]{:S(2)}, u32[]{:S(2)}) %collective-permute-start.67) | collective-permute-done | bytes 589856 | tf_op jit(solution)/shard_map/ppermute | solution.py:377
  481.3 1.6 maximum_convert_fusion.1
  482.8 4.5 collective-permute-done.59
  487.6 1.7 maximum_convert_fusion
  (283 shorter events, 72.2 us)
Async XLA Ops:
  3.5 20.9 %collective-permute-start = (bf16[1024,384]{1,0:T(8,128)(2,1)}, bf16[1024,384]{1,0:T(8,128)(2,1)}, u32[]{:S(2)}, u32[]{:S(2)}) collective-permute-start(bf16[1024,384]{1,0:T(8,128)(2,1)} %get-tuple-element.103), channel_id=1, source_target_pairs={{0,2},{2,0},{1,3},{3,1},{4,6},{6,4},{5,7},{7,5},{8,10},{10,8},{9,1... | collective-permute-start | bytes 2359304 | tf_op jit(solution)/shard_map/ppermute | solution.py:368
  7.6 40.0 %collective-permute-start.3 = (f32[8,6,384]{2,1,0:T(8,128)}, f32[8,6,384]{2,1,0:T(8,128)S(1)}, u32[]{:S(2)}, u32[]{:S(2)}) collective-permute-start(f32[8,6,384]{2,1,0:T(8,128)} %copy.40), channel_id=1, source_target_pairs={{0,1},{1,0},{2,3},{3,2},{4,5},{5,4},{6,7},{7,6},{8,9},{9,8},{10,11... | collective-permute-start | bytes 221192 | tf_op jit(solution)/shard_map/ppermute | solution.py:372
  7.6 41.5 %collective-permute-start.5 = (f32[2304]{0:T(1024)S(1)}, f32[2304]{0:T(1024)}, u32[]{:S(2)}, u32[]{:S(2)}) collective-permute-start(f32[2304]{0:T(1024)S(1)} %maximum_convert_fusion.3), channel_id=1, source_target_pairs={{0,1},{1,0},{2,3},{3,2},{4,5},{5,4},{6,7},{7,6},{8,9},{9,8},{10,11... | collective-permute-start | bytes 27656 | tf_op jit(solution)/shard_map/ppermute | solution.py:372
  8.9 21.9 %collective-permute-start.8 = (f32[768]{0:T(1024)S(1)}, f32[768]{0:T(1024)S(1)}, u32[]{:S(2)}, u32[]{:S(2)}) collective-permute-start(f32[768]{0:T(1024)S(1)} %maximum_convert_fusion.4), channel_id=1, source_target_pairs={{0,2},{2,0},{1,3},{3,1},{4,6},{6,4},{5,7},{7,5},{8,10},{10,8},{9,1... | collective-permute-start | bytes 9224 | tf_op jit(solution)/shard_map/ppermute | solution.py:368
  24.4 21.1 %collective-permute-start.1 = (bf16[3,384,384]{2,1,0:T(8,128)(2,1)}, bf16[3,384,384]{2,1,0:T(8,128)(2,1)}, u32[]{:S(2)}, u32[]{:S(2)}) collective-permute-start(bf16[3,384,384]{2,1,0:T(8,128)(2,1)} %w0.1), channel_id=1, source_target_pairs={{0,2},{2,0},{1,3},{3,1},{4,6},{6,4},{5,7},{7,5},{8,10},{10,8},{9,1... | collective-permute-start | bytes 2654216 | tf_op jit(solution)/shard_map/ppermute | solution.py:368
  30.8 71.2 %collective-permute-start.6 = (bf16[3,384,384]{2,1,0:T(8,128)(2,1)}, bf16[3,384,384]{2,1,0:T(8,128)(2,1)S(1)}, u32[]{:S(2)}, u32[]{:S(2)}) collective-permute-start(bf16[3,384,384]{2,1,0:T(8,128)(2,1)} %w0.1), channel_id=1, source_target_pairs={{0,1},{1,0},{2,3},{3,2},{4,5},{5,4},{6,7},{7,6},{8,9},{9,8},{10,11... | collective-permute-start | bytes 2654216 | tf_op jit(solution)/shard_map/ppermute | solution.py:372
  45.5 66.0 %collective-permute-start.12 = (bf16[384,1536]{1,0:T(8,128)(2,1)}, bf16[384,1536]{1,0:T(8,128)(2,1)S(1)}, u32[]{:S(2)}, u32[]{:S(2)}) collective-permute-start(bf16[384,1536]{1,0:T(8,128)(2,1)} %x0), channel_id=1, source_target_pairs={{0,2},{2,0},{1,3},{3,1},{4,6},{6,4},{5,7},{7,5},{8,10},{10,8},{9,1... | collective-permute-start | bytes 3538952 | tf_op jit(solution)/shard_map/ppermute | solution.py:368
  47.0 64.8 %collective-permute-start.15 = (bf16[1536,384]{1,0:T(8,128)(2,1)}, bf16[1536,384]{1,0:T(8,128)(2,1)}, u32[]{:S(2)}, u32[]{:S(2)}) collective-permute-start(bf16[1536,384]{1,0:T(8,128)(2,1)} %s0), channel_id=1, source_target_pairs={{0,2},{2,0},{1,3},{3,1},{4,6},{6,4},{5,7},{7,5},{8,10},{10,8},{9,1... | collective-permute-start | bytes 3538952 | tf_op jit(solution)/shard_map/ppermute | solution.py:368
  47.6 50.6 %collective-permute-start.4 = (f32[4,6,384]{2,1,0:T(8,128)S(1)}, f32[4,6,384]{2,1,0:T(8,128)S(1)}, u32[]{:S(2)}, u32[]{:S(2)}) collective-permute-start(f32[4,6,384]{2,1,0:T(8,128)S(1)} %get-tuple-element.130), channel_id=1, source_target_pairs={{0,2},{2,0},{1,3},{3,1},{4,6},{6,4},{5,7},{7,5},{8,10},{10,8},{9,1... | collective-permute-start | bytes 110600 | tf_op jit(solution)/shard_map/ppermute | solution.py:368
  49.1 61.3 %collective-permute-start.7 = (bf16[3,384,384]{2,1,0:T(8,128)(2,1)}, bf16[3,384,384]{2,1,0:T(8,128)(2,1)S(1)}, u32[]{:S(2)}, u32[]{:S(2)}) collective-permute-start(bf16[3,384,384]{2,1,0:T(8,128)(2,1)} %collective-permute-done.1.w1), channel_id=1, source_target_pairs={{0,1},{1,0},{2,3},{3,2},{4,5},{5,4},{6,7},{7,6},{8,9},{9,8},{10,11... | collective-permute-start | bytes 2654216 | tf_op jit(solution)/shard_map/ppermute | solution.py:372
  98.3 6.9 %collective-permute-start.9 = (bf16[384,384]{1,0:T(8,128)(2,1)}, bf16[384,384]{1,0:T(8,128)(2,1)S(1)}, u32[]{:S(2)}, u32[]{:S(2)}) collective-permute-start(bf16[384,384]{1,0:T(8,128)(2,1)} %o0), channel_id=1, source_target_pairs={{0,2},{2,0},{1,3},{3,1},{4,6},{6,4},{5,7},{7,5},{8,10},{10,8},{9,1... | collective-permute-start | bytes 884744 | tf_op jit(solution)/shard_map/ppermute | solution.py:368
  102.0 7.8 %collective-permute-start.10 = (bf16[384,384]{1,0:T(8,128)(2,1)}, bf16[384,384]{1,0:T(8,128)(2,1)S(1)}, u32[]{:S(2)}, u32[]{:S(2)}) collective-permute-start(bf16[384,384]{1,0:T(8,128)(2,1)} %o0), channel_id=1, source_target_pairs={{0,1},{1,0},{2,3},{3,2},{4,5},{5,4},{6,7},{7,6},{8,9},{9,8},{10,11... | collective-permute-start | bytes 884744 | tf_op jit(solution)/shard_map/ppermute | solution.py:372
  105.2 5.1 %collective-permute-start.11 = (bf16[384,384]{1,0:T(8,128)(2,1)S(1)}, bf16[384,384]{1,0:T(8,128)(2,1)S(1)}, u32[]{:S(2)}, u32[]{:S(2)}) collective-permute-start(bf16[384,384]{1,0:T(8,128)(2,1)S(1)} %collective-permute-done.9.o1), channel_id=1, source_target_pairs={{0,1},{1,0},{2,3},{3,2},{4,5},{5,4},{6,7},{7,6},{8,9},{9,8},{10,11... | collective-permute-start | bytes 884744 | tf_op jit(solution)/shard_map/ppermute | solution.py:372
  109.8 20.8 %collective-permute-start.13 = (bf16[384,1536]{1,0:T(8,128)(2,1)}, bf16[384,1536]{1,0:T(8,128)(2,1)}, u32[]{:S(2)}, u32[]{:S(2)}) collective-permute-start(bf16[384,1536]{1,0:T(8,128)(2,1)} %x0), channel_id=1, source_target_pairs={{0,1},{1,0},{2,3},{3,2},{4,5},{5,4},{6,7},{7,6},{8,9},{9,8},{10,11... | collective-permute-start | bytes 3538952 | tf_op jit(solution)/shard_map/ppermute | solution.py:372
  110.3 20.3 %collective-permute-start.16 = (bf16[1536,384]{1,0:T(8,128)(2,1)}, bf16[1536,384]{1,0:T(8,128)(2,1)}, u32[]{:S(2)}, u32[]{:S(2)}) collective-permute-start(bf16[1536,384]{1,0:T(8,128)(2,1)} %s0), channel_id=1, source_target_pairs={{0,1},{1,0},{2,3},{3,2},{4,5},{5,4},{6,7},{7,6},{8,9},{9,8},{10,11... | collective-permute-start | bytes 3538952 | tf_op jit(solution)/shard_map/ppermute | solution.py:372
  110.4 20.2 %collective-permute-start.2 = (bf16[1024,384]{1,0:T(8,128)(2,1)}, bf16[1024,384]{1,0:T(8,128)(2,1)}, u32[]{:S(2)}, u32[]{:S(2)}) collective-permute-start(bf16[1024,384]{1,0:T(8,128)(2,1)} %get-tuple-element.41), channel_id=1, source_target_pairs={{0,2},{2,0},{1,3},{3,1},{4,6},{6,4},{5,7},{7,5},{8,10},{10,8},{9,1... | collective-permute-start | bytes 2359304 | tf_op jit(solution)/shard_map/ppermute | solution.py:368
  111.5 19.1 %collective-permute-start.14 = (bf16[384,1536]{1,0:T(8,128)(2,1)S(1)}, bf16[384,1536]{1,0:T(8,128)(2,1)}, u32[]{:S(2)}, u32[]{:S(2)}) collective-permute-start(bf16[384,1536]{1,0:T(8,128)(2,1)S(1)} %collective-permute-done.12.x1), channel_id=1, source_target_pairs={{0,1},{1,0},{2,3},{3,2},{4,5},{5,4},{6,7},{7,6},{8,9},{9,8},{10,11... | collective-permute-start | bytes 3538952 | tf_op jit(solution)/shard_map/ppermute | solution.py:372
  111.7 18.9 %collective-permute-start.17 = (bf16[1536,384]{1,0:T(8,128)(2,1)}, bf16[1536,384]{1,0:T(8,128)(2,1)}, u32[]{:S(2)}, u32[]{:S(2)}) collective-permute-start(bf16[1536,384]{1,0:T(8,128)(2,1)} %collective-permute-done.15.s1), channel_id=1, source_target_pairs={{0,1},{1,0},{2,3},{3,2},{4,5},{5,4},{6,7},{7,6},{8,9},{9,8},{10,11... | collective-permute-start | bytes 3538952 | tf_op jit(solution)/shard_map/ppermute | solution.py:372
  186.6 175.3 %collective-permute-start.60 = (bf16[1536,768]{1,0:T(8,128)(2,1)}, bf16[1536,768]{1,0:T(8,128)(2,1)}, u32[]{:S(2)}, u32[]{:S(2)}) collective-permute-start(bf16[1536,768]{1,0:T(8,128)(2,1)} %convolution_convert_fusion), channel_id=1, source_target_pairs={{0,1},{1,0},{2,3},{3,2},{4,5},{5,4},{6,7},{7,6},{8,9},{9,8},{10,11... | collective-permute-start | bytes 7077896 | tf_op jit(solution)/shard_map/ppermute | solution.py:372
  190.7 180.8 %collective-permute-start.52 = (bf16[768,1536]{1,0:T(8,128)(2,1)}, bf16[768,1536]{1,0:T(8,128)(2,1)}, u32[]{:S(2)}, u32[]{:S(2)}) collective-permute-start(bf16[768,1536]{1,0:T(8,128)(2,1)} %convolution_convert_fusion.1), channel_id=1, source_target_pairs={{0,1},{1,0},{2,3},{3,2},{4,5},{5,4},{6,7},{7,6},{8,9},{9,8},{10,11... | collective-permute-start | bytes 7077896 | tf_op jit(solution)/shard_map/ppermute | solution.py:372
  192.8 89.4 %collective-permute-start.44 = (bf16[384,768]{1,0:T(8,128)(2,1)}, bf16[384,768]{1,0:T(8,128)(2,1)}, u32[]{:S(2)}, u32[]{:S(2)}) collective-permute-start(bf16[384,768]{1,0:T(8,128)(2,1)} %convolution_convert_fusion.3), channel_id=1, source_target_pairs={{0,1},{1,0},{2,3},{3,2},{4,5},{5,4},{6,7},{7,6},{8,9},{9,8},{10,11... | collective-permute-start | bytes 1769480 | tf_op jit(solution)/shard_map/ppermute | solution.py:372
  193.0 34.5 %collective-permute-start.37 = (f32[2,384]{1,0:T(2,128)S(1)}, f32[2,384]{1,0:T(2,128)S(1)}, u32[]{:S(2)}, u32[]{:S(2)}) collective-permute-start(f32[2,384]{1,0:T(2,128)S(1)} %slice.166), channel_id=1, source_target_pairs={{0,2},{2,0},{1,3},{3,1},{4,6},{6,4},{5,7},{7,5},{8,10},{10,8},{9,1... | collective-permute-start | bytes 9224 | tf_op jit(solution)/shard_map/ppermute | solution.py:368
  228.7 4.0 collective-permute-start.20
  233.4 3.8 collective-permute-start.41
  234.6 11.7 %collective-permute-start.21 = (bf16[8,6,384]{2,1,0:T(8,128)(2,1)S(1)}, bf16[8,6,384]{2,1,0:T(8,128)(2,1)S(1)}, u32[]{:S(2)}, u32[]{:S(2)}) collective-permute-start(bf16[8,6,384]{2,1,0:T(8,128)(2,1)S(1)} %pad_maximum_fusion.14), channel_id=1, source_target_pairs={{0,1},{1,0},{2,3},{3,2},{4,5},{5,4},{6,7},{7,6},{8,9},{9,8},{10,11... | collective-permute-start | bytes 110600 | tf_op jit(solution)/shard_map/ppermute | solution.py:372
  237.3 6.4 %collective-permute-start.42 = (f32[3456]{0:T(1024)S(1)}, f32[3456]{0:T(1024)S(1)}, u32[]{:S(2)}, u32[]{:S(2)}) collective-permute-start(f32[3456]{0:T(1024)S(1)} %fusion.22), channel_id=1, source_target_pairs={{0,8},{4,12},{8,0},{12,4},{16,24},{20,28},{24,16},{28,20},{1,9},{5... | collective-permute-start | bytes 41480 | tf_op jit(solution)/shard_map/ppermute | solution.py:377
  243.6 4.9 collective-permute-start.43
  246.9 7.4 %collective-permute-start.23 = (bf16[16,6,384]{2,1,0:T(8,128)(2,1)S(1)}, bf16[16,6,384]{2,1,0:T(8,128)(2,1)S(1)}, u32[]{:S(2)}, u32[]{:S(2)}) collective-permute-start(bf16[16,6,384]{2,1,0:T(8,128)(2,1)S(1)} %pad_maximum_fusion.12), channel_id=1, source_target_pairs={{0,4},{4,0},{8,12},{12,8},{16,20},{20,16},{24,28},{28,24},{1,5},{5... | collective-permute-start | bytes 221192 | tf_op jit(solution)/shard_map/ppermute | solution.py:377
  248.5 3.8 collective-permute-start.22
  254.4 6.0 %collective-permute-start.24 = (bf16[32,6,384]{2,1,0:T(8,128)(2,1)S(1)}, bf16[32,6,384]{2,1,0:T(8,128)(2,1)S(1)}, u32[]{:S(2)}, u32[]{:S(2)}) collective-permute-start(bf16[32,6,384]{2,1,0:T(8,128)(2,1)S(1)} %pad_maximum_fusion.9), channel_id=1, source_target_pairs={{0,8},{4,12},{8,0},{12,4},{16,24},{20,28},{24,16},{28,20},{1,9},{5... | collective-permute-start | bytes 442376 | tf_op jit(solution)/shard_map/ppermute | solution.py:377
  256.6 73.9 %collective-permute-start.29 = (bf16[768,1152]{1,0:T(8,128)(2,1)}, bf16[768,1152]{1,0:T(8,128)(2,1)}, u32[]{:S(2)}, u32[]{:S(2)}) collective-permute-start(bf16[768,1152]{1,0:T(8,128)(2,1)} %convolution_convert_fusion.2), channel_id=1, source_target_pairs={{0,1},{1,0},{2,3},{3,2},{4,5},{5,4},{6,7},{7,6},{8,9},{9,8},{10,11... | collective-permute-start | bytes 5308424 | tf_op jit(solution)/shard_map/ppermute | solution.py:372
  260.4 3.9 collective-permute-start.27
  264.2 16.4 %collective-permute-start.25 = (bf16[64,6,384]{2,1,0:T(8,128)(2,1)S(1)}, bf16[64,6,384]{2,1,0:T(8,128)(2,1)S(1)}, u32[]{:S(2)}, u32[]{:S(2)}) collective-permute-start(bf16[64,6,384]{2,1,0:T(8,128)(2,1)S(1)} %pad_maximum_fusion.5), channel_id=1, source_target_pairs={{0,16},{4,20},{8,24},{12,28},{16,0},{20,4},{24,8},{28,12},{1,17},{... | collective-permute-start | bytes 884744 | tf_op jit(solution)/shard_map/ppermute | solution.py:377
  280.6 33.9 %collective-permute-start.19 = (bf16[1024,384]{1,0:T(8,128)(2,1)}, bf16[1024,384]{1,0:T(8,128)(2,1)S(1)}, u32[]{:S(2)}, u32[]{:S(2)}) collective-permute-start(bf16[1024,384]{1,0:T(8,128)(2,1)} %get-tuple-element.52), channel_id=1, source_target_pairs={{0,2},{2,0},{1,3},{3,1},{4,6},{6,4},{5,7},{7,5},{8,10},{10,8},{9,1... | collective-permute-start | bytes 2359304 | tf_op jit(solution)/shard_map/ppermute | solution.py:368
  282.3 5.2 %collective-permute-start.28 = (bf16[64,384]{1,0:T(8,128)(2,1)S(1)}, bf16[64,384]{1,0:T(8,128)(2,1)S(1)}, u32[]{:S(2)}, u32[]{:S(2)}) collective-permute-start(bf16[64,384]{1,0:T(8,128)(2,1)S(1)} %pad_maximum_fusion.15), channel_id=1, source_target_pairs={{0,16},{4,20},{8,24},{12,28},{16,0},{20,4},{24,8},{28,12},{1,17},{... | collective-permute-start | bytes 147464 | tf_op jit(solution)/shard_map/ppermute | solution.py:377
  287.4 19.1 %collective-permute-start.45 = (bf16[384,384]{1,0:T(8,128)(2,1)}, bf16[384,384]{1,0:T(8,128)(2,1)}, u32[]{:S(2)}, u32[]{:S(2)}) collective-permute-start(bf16[384,384]{1,0:T(8,128)(2,1)} %slice.216), channel_id=1, source_target_pairs={{0,2},{2,0},{1,3},{3,1},{4,6},{6,4},{5,7},{7,5},{8,10},{10,8},{9,1... | collective-permute-start | bytes 884744 | tf_op jit(solution)/shard_map/ppermute | solution.py:368
  307.8 5.2 %collective-permute-start.46 = (bf16[192,384]{1,0:T(8,128)(2,1)S(1)}, bf16[192,384]{1,0:T(8,128)(2,1)S(1)}, u32[]{:S(2)}, u32[]{:S(2)}) collective-permute-start(bf16[192,384]{1,0:T(8,128)(2,1)S(1)} %dynamic-slice_convert_fusion.8), channel_id=1, source_target_pairs={{0,4},{4,0},{8,12},{12,8},{16,20},{20,16},{24,28},{28,24},{1,5},{5... | collective-permute-start | bytes 442376 | tf_op jit(solution)/shard_map/ppermute | solution.py:377
  313.0 17.2 %collective-permute-start.18 = (bf16[1024,384]{1,0:T(8,128)(2,1)S(1)}, bf16[1024,384]{1,0:T(8,128)(2,1)S(1)}, u32[]{:S(2)}, u32[]{:S(2)}) collective-permute-start(bf16[1024,384]{1,0:T(8,128)(2,1)S(1)} %copy-done.20), channel_id=1, source_target_pairs={{0,2},{2,0},{1,3},{3,1},{4,6},{6,4},{5,7},{7,5},{8,10},{10,8},{9,1... | collective-permute-start | bytes 2359304 | tf_op jit(solution)/shard_map/ppermute | solution.py:368
  314.6 4.4 collective-permute-start.47
  319.1 11.3 %collective-permute-start.48 = (bf16[48,384]{1,0:T(8,128)(2,1)S(1)}, bf16[48,384]{1,0:T(8,128)(2,1)S(1)}, u32[]{:S(2)}, u32[]{:S(2)}) collective-permute-start(bf16[48,384]{1,0:T(8,128)(2,1)S(1)} %dynamic-slice_convert_fusion.11), channel_id=1, source_target_pairs={{0,16},{4,20},{8,24},{12,28},{16,0},{20,4},{24,8},{28,12},{1,17},{... | collective-permute-start | bytes 110600 | tf_op jit(solution)/shard_map/ppermute | solution.py:377
  330.4 5.6 %collective-permute-start.49 = (bf16[48,384]{1,0:T(8,128)(2,1)S(1)}, bf16[48,384]{1,0:T(8,128)(2,1)S(1)}, u32[]{:S(2)}, u32[]{:S(2)}) collective-permute-start(bf16[48,384]{1,0:T(8,128)(2,1)S(1)} %add_convert_fusion.3), channel_id=1, source_target_pairs={{0,16},{4,20},{8,24},{12,28},{16,0},{20,4},{24,8},{28,12},{1,17},{... | collective-permute-start | bytes 110600 | tf_op jit(solution)/shard_map/ppermute | solution.py:377
  334.4 18.5 %collective-permute-start.30 = (bf16[384,1152]{1,0:T(8,128)(2,1)S(1)}, bf16[384,1152]{1,0:T(8,128)(2,1)S(1)}, u32[]{:S(2)}, u32[]{:S(2)}) collective-permute-start(bf16[384,1152]{1,0:T(8,128)(2,1)S(1)} %slice.215), channel_id=1, source_target_pairs={{0,2},{2,0},{1,3},{3,1},{4,6},{6,4},{5,7},{7,5},{8,10},{10,8},{9,1... | collective-permute-start | bytes 2654216 | tf_op jit(solution)/shard_map/ppermute | solution.py:368
  336.0 4.4 collective-permute-start.50
  340.5 14.7 %collective-permute-start.51 = (bf16[192,384]{1,0:T(8,128)(2,1)S(1)}, bf16[192,384]{1,0:T(8,128)(2,1)S(1)}, u32[]{:S(2)}, u32[]{:S(2)}) collective-permute-start(bf16[192,384]{1,0:T(8,128)(2,1)S(1)} %pad_maximum_fusion.10), channel_id=1, source_target_pairs={{0,4},{4,0},{8,12},{12,8},{16,20},{20,16},{24,28},{28,24},{1,5},{5... | collective-permute-start | bytes 442376 | tf_op jit(solution)/shard_map/ppermute | solution.py:377
  353.1 8.4 %collective-permute-start.31 = (bf16[192,1152]{1,0:T(8,128)(2,1)S(1)}, bf16[192,1152]{1,0:T(8,128)(2,1)S(1)}, u32[]{:S(2)}, u32[]{:S(2)}) collective-permute-start(bf16[192,1152]{1,0:T(8,128)(2,1)S(1)} %dynamic-slice_convert_fusion.2), channel_id=1, source_target_pairs={{0,4},{4,0},{8,12},{12,8},{16,20},{20,16},{24,28},{28,24},{1,5},{5... | collective-permute-start | bytes 1327112 | tf_op jit(solution)/shard_map/ppermute | solution.py:377
  361.6 7.2 %collective-permute-start.32 = (bf16[96,1152]{1,0:T(8,128)(2,1)S(1)}, bf16[96,1152]{1,0:T(8,128)(2,1)S(1)}, u32[]{:S(2)}, u32[]{:S(2)}) collective-permute-start(bf16[96,1152]{1,0:T(8,128)(2,1)S(1)} %dynamic-slice_convert_fusion.5), channel_id=1, source_target_pairs={{0,8},{4,12},{8,0},{12,4},{16,24},{20,28},{24,16},{28,20},{1,9},{5... | collective-permute-start | bytes 663560 | tf_op jit(solution)/shard_map/ppermute | solution.py:377
  366.8 29.0 %collective-permute-start.61 = (bf16[1536,384]{1,0:T(8,128)(2,1)S(1)}, bf16[1536,384]{1,0:T(8,128)(2,1)S(1)}, u32[]{:S(2)}, u32[]{:S(2)}) collective-permute-start(bf16[1536,384]{1,0:T(8,128)(2,1)S(1)} %slice.213), channel_id=1, source_target_pairs={{0,2},{2,0},{1,3},{3,1},{4,6},{6,4},{5,7},{7,5},{8,10},{10,8},{9,1... | collective-permute-start | bytes 3538952 | tf_op jit(solution)/shard_map/ppermute | solution.py:368
  368.9 9.1 %collective-permute-start.33 = (bf16[48,1152]{1,0:T(8,128)(2,1)S(1)}, bf16[48,1152]{1,0:T(8,128)(2,1)S(1)}, u32[]{:S(2)}, u32[]{:S(2)}) collective-permute-start(bf16[48,1152]{1,0:T(8,128)(2,1)S(1)} %dynamic-slice_convert_fusion.9), channel_id=1, source_target_pairs={{0,16},{4,20},{8,24},{12,28},{16,0},{20,4},{24,8},{28,12},{1,17},{... | collective-permute-start | bytes 331784 | tf_op jit(solution)/shard_map/ppermute | solution.py:377
  376.0 38.5 %collective-permute-start.53 = (bf16[384,1536]{1,0:T(8,128)(2,1)S(1)}, bf16[384,1536]{1,0:T(8,128)(2,1)S(1)}, u32[]{:S(2)}, u32[]{:S(2)}) collective-permute-start(bf16[384,1536]{1,0:T(8,128)(2,1)S(1)} %slice.214), channel_id=1, source_target_pairs={{0,2},{2,0},{1,3},{3,1},{4,6},{6,4},{5,7},{7,5},{8,10},{10,8},{9,1... | collective-permute-start | bytes 3538952 | tf_op jit(solution)/shard_map/ppermute | solution.py:368
  377.9 18.7 %collective-permute-start.34 = (bf16[48,1152]{1,0:T(8,128)(2,1)S(1)}, bf16[48,1152]{1,0:T(8,128)(2,1)S(1)}, u32[]{:S(2)}, u32[]{:S(2)}) collective-permute-start(bf16[48,1152]{1,0:T(8,128)(2,1)S(1)} %add_convert_fusion.2), channel_id=1, source_target_pairs={{0,16},{4,20},{8,24},{12,28},{16,0},{20,4},{24,8},{28,12},{1,17},{... | collective-permute-start | bytes 331784 | tf_op jit(solution)/shard_map/ppermute | solution.py:377
  396.0 21.2 %collective-permute-start.62 = (bf16[768,384]{1,0:T(8,128)(2,1)S(1)}, bf16[768,384]{1,0:T(8,128)(2,1)S(1)}, u32[]{:S(2)}, u32[]{:S(2)}) collective-permute-start(bf16[768,384]{1,0:T(8,128)(2,1)S(1)} %dynamic-slice_convert_fusion), channel_id=1, source_target_pairs={{0,4},{4,0},{8,12},{12,8},{16,20},{20,16},{24,28},{28,24},{1,5},{5... | collective-permute-start | bytes 1769480 | tf_op jit(solution)/shard_map/ppermute | solution.py:377
  396.7 19.0 %collective-permute-start.35 = (bf16[96,1152]{1,0:T(8,128)(2,1)S(1)}, bf16[96,1152]{1,0:T(8,128)(2,1)S(1)}, u32[]{:S(2)}, u32[]{:S(2)}) collective-permute-start(bf16[96,1152]{1,0:T(8,128)(2,1)S(1)} %pad_maximum_fusion.8), channel_id=1, source_target_pairs={{0,8},{4,12},{8,0},{12,4},{16,24},{20,28},{24,16},{28,20},{1,9},{5... | collective-permute-start | bytes 663560 | tf_op jit(solution)/shard_map/ppermute | solution.py:377
  414.9 13.7 %collective-permute-start.54 = (bf16[192,1536]{1,0:T(8,128)(2,1)S(1)}, bf16[192,1536]{1,0:T(8,128)(2,1)S(1)}, u32[]{:S(2)}, u32[]{:S(2)}) collective-permute-start(bf16[192,1536]{1,0:T(8,128)(2,1)S(1)} %dynamic-slice_convert_fusion.1), channel_id=1, source_target_pairs={{0,4},{4,0},{8,12},{12,8},{16,20},{20,16},{24,28},{28,24},{1,5},{5... | collective-permute-start | bytes 1769480 | tf_op jit(solution)/shard_map/ppermute | solution.py:377
  415.9 17.4 %collective-permute-start.36 = (bf16[192,1152]{1,0:T(8,128)(2,1)S(1)}, bf16[192,1152]{1,0:T(8,128)(2,1)S(1)}, u32[]{:S(2)}, u32[]{:S(2)}) collective-permute-start(bf16[192,1152]{1,0:T(8,128)(2,1)S(1)} %pad_maximum_fusion.4), channel_id=1, source_target_pairs={{0,4},{4,0},{8,12},{12,8},{16,20},{20,16},{24,28},{28,24},{1,5},{5... | collective-permute-start | bytes 1327112 | tf_op jit(solution)/shard_map/ppermute | solution.py:377
  418.1 20.1 %collective-permute-start.63 = (bf16[384,384]{1,0:T(8,128)(2,1)}, bf16[384,384]{1,0:T(8,128)(2,1)}, u32[]{:S(2)}, u32[]{:S(2)}) collective-permute-start(bf16[384,384]{1,0:T(8,128)(2,1)} %dynamic-slice_convert_fusion.3), channel_id=1, source_target_pairs={{0,8},{4,12},{8,0},{12,4},{16,24},{20,28},{24,16},{28,20},{1,9},{5... | collective-permute-start | bytes 884744 | tf_op jit(solution)/shard_map/ppermute | solution.py:377
  430.5 11.2 %collective-permute-start.55 = (bf16[96,1536]{1,0:T(8,128)(2,1)}, bf16[96,1536]{1,0:T(8,128)(2,1)}, u32[]{:S(2)}, u32[]{:S(2)}) collective-permute-start(bf16[96,1536]{1,0:T(8,128)(2,1)} %dynamic-slice_convert_fusion.4), channel_id=1, source_target_pairs={{0,8},{4,12},{8,0},{12,4},{16,24},{20,28},{24,16},{28,20},{1,9},{5... | collective-permute-start | bytes 884744 | tf_op jit(solution)/shard_map/ppermute | solution.py:377
  439.4 13.6 %collective-permute-start.64 = (bf16[192,384]{1,0:T(8,128)(2,1)S(1)}, bf16[192,384]{1,0:T(8,128)(2,1)S(1)}, u32[]{:S(2)}, u32[]{:S(2)}) collective-permute-start(bf16[192,384]{1,0:T(8,128)(2,1)S(1)} %dynamic-slice_convert_fusion.6), channel_id=1, source_target_pairs={{0,16},{4,20},{8,24},{12,28},{16,0},{20,4},{24,8},{28,12},{1,17},{... | collective-permute-start | bytes 442376 | tf_op jit(solution)/shard_map/ppermute | solution.py:377
  442.8 12.5 %collective-permute-start.56 = (bf16[48,1536]{1,0:T(8,128)(2,1)S(1)}, bf16[48,1536]{1,0:T(8,128)(2,1)S(1)}, u32[]{:S(2)}, u32[]{:S(2)}) collective-permute-start(bf16[48,1536]{1,0:T(8,128)(2,1)S(1)} %dynamic-slice_convert_fusion.7), channel_id=1, source_target_pairs={{0,16},{4,20},{8,24},{12,28},{16,0},{20,4},{24,8},{28,12},{1,17},{... | collective-permute-start | bytes 442376 | tf_op jit(solution)/shard_map/ppermute | solution.py:377
  453.0 7.7 %collective-permute-start.65 = (bf16[192,384]{1,0:T(8,128)(2,1)S(1)}, bf16[192,384]{1,0:T(8,128)(2,1)S(1)}, u32[]{:S(2)}, u32[]{:S(2)}) collective-permute-start(bf16[192,384]{1,0:T(8,128)(2,1)S(1)} %add_convert_fusion), channel_id=1, source_target_pairs={{0,16},{4,20},{8,24},{12,28},{16,0},{20,4},{24,8},{28,12},{1,17},{... | collective-permute-start | bytes 442376 | tf_op jit(solution)/shard_map/ppermute | solution.py:377
  455.3 8.3 %collective-permute-start.57 = (bf16[48,1536]{1,0:T(8,128)(2,1)S(1)}, bf16[48,1536]{1,0:T(8,128)(2,1)S(1)}, u32[]{:S(2)}, u32[]{:S(2)}) collective-permute-start(bf16[48,1536]{1,0:T(8,128)(2,1)S(1)} %add_convert_fusion.1), channel_id=1, source_target_pairs={{0,16},{4,20},{8,24},{12,28},{16,0},{20,4},{24,8},{28,12},{1,17},{... | collective-permute-start | bytes 442376 | tf_op jit(solution)/shard_map/ppermute | solution.py:377
  460.8 7.0 %collective-permute-start.66 = (bf16[384,384]{1,0:T(8,128)(2,1)S(1)}, bf16[384,384]{1,0:T(8,128)(2,1)S(1)}, u32[]{:S(2)}, u32[]{:S(2)}) collective-permute-start(bf16[384,384]{1,0:T(8,128)(2,1)S(1)} %pad_maximum_fusion.7), channel_id=1, source_target_pairs={{0,8},{4,12},{8,0},{12,4},{16,24},{20,28},{24,16},{28,20},{1,9},{5... | collective-permute-start | bytes 884744 | tf_op jit(solution)/shard_map/ppermute | solution.py:377
  463.6 7.3 %collective-permute-start.58 = (bf16[96,1536]{1,0:T(8,128)(2,1)S(1)}, bf16[96,1536]{1,0:T(8,128)(2,1)S(1)}, u32[]{:S(2)}, u32[]{:S(2)}) collective-permute-start(bf16[96,1536]{1,0:T(8,128)(2,1)S(1)} %pad_maximum_fusion.6), channel_id=1, source_target_pairs={{0,8},{4,12},{8,0},{12,4},{16,24},{20,28},{24,16},{28,20},{1,9},{5... | collective-permute-start | bytes 884744 | tf_op jit(solution)/shard_map/ppermute | solution.py:377
  468.0 13.0 %collective-permute-start.67 = (bf16[768,384]{1,0:T(8,128)(2,1)S(1)}, bf16[768,384]{1,0:T(8,128)(2,1)S(1)}, u32[]{:S(2)}, u32[]{:S(2)}) collective-permute-start(bf16[768,384]{1,0:T(8,128)(2,1)S(1)} %pad_maximum_fusion.3), channel_id=1, source_target_pairs={{0,4},{4,0},{8,12},{12,8},{16,20},{20,16},{24,28},{28,24},{1,5},{5... | collective-permute-start | bytes 1769480 | tf_op jit(solution)/shard_map/ppermute | solution.py:377
  471.1 16.2 %collective-permute-start.59 = (bf16[192,1536]{1,0:T(8,128)(2,1)S(1)}, bf16[192,1536]{1,0:T(8,128)(2,1)S(1)}, u32[]{:S(2)}, u32[]{:S(2)}) collective-permute-start(bf16[192,1536]{1,0:T(8,128)(2,1)S(1)} %pad_maximum_fusion.2), channel_id=1, source_target_pairs={{0,4},{4,0},{8,12},{12,8},{16,20},{20,16},{24,28},{28,24},{1,5},{5... | collective-permute-start | bytes 1769480 | tf_op jit(solution)/shard_map/ppermute | solution.py:377
  (38 other events, 439.9 us)

commit v2 on v1

--- a/solution.py
+++ b/solution.py
@@ -406,28 +406,54 @@
     )
 
 
-def reduce_grid(own, other, row_dim):
-    arrived = swap_col(other().astype(B16))
-    total = own() + arrived.astype(F32)
-    mine, theirs = halves(total, row_dim)
-    return mine + swap_row(theirs.astype(B16)).astype(F32)
-
-
-def sum_dp(values):
-    me = lax.axis_index("dp")
-    for distance in distances():
-        kept, sent = pick(values, (me // distance) % 2)
-        values = kept + swap_dp(sent.astype(B16), distance).astype(F32)
-    values = values.astype(B16)
+def x_place():
+    return lax.axis_index("dp") % 2
+
+
+def scatter_stage(values, distance, axis=0):
+    place = (lax.axis_index("dp") // distance) % 2
+    size = values.shape[axis] // 2
+    kept = lax.dynamic_slice_in_dim(values, place * size, size, axis)
+    sent = lax.dynamic_slice_in_dim(values, (1 - place) * size, size, axis)
+    return kept + swap_dp(sent.astype(B16), distance).astype(F32)
+
+
+def gather_dp(values):
     for distance in reversed(distances()):
-        values = in_order((me // distance) % 2, values, swap_dp(values, distance))
-    return values.astype(F32)
-
-
-def gather_dp(values):
-    for distance in distances():
         values = jnp.concatenate([values, swap_dp(values, distance)], axis=0)
     return values
+
+
+def sum_order():
+    me, mine = lax.axis_index("dp"), 0
+    for distance in distances():
+        mine = mine * 2 + (me // distance) % 2
+    return jnp.full((1,), mine, jnp.int32)
+
+
+def order_grid_kernel(mine, values, shr_out, out_out, exp_out):
+    shr_rows, out_rows, exp_rows = shr_out.shape[1], out_out.shape[1], exp_out.shape[1]
+    for block in range(values.shape[0]):
+        place = mine[0] ^ block
+        shr_out[place] = values[block, :shr_rows].astype(F32)
+        out_out[place] = values[block, shr_rows : shr_rows + out_rows].astype(F32)
+        for part in range(exp_out.shape[2] // HALF):
+            at = shr_rows + out_rows + part * exp_rows
+            exp_out[place, :, part * HALF : (part + 1) * HALF] = values[
+                block, at : at + exp_rows
+            ].astype(F32)
+
+
+def order(kernel, values, shapes):
+    whole = [pl.BlockSpec(memory_space=pltpu.VMEM)]
+    return pl.pallas_call(
+        kernel,
+        in_specs=[pl.BlockSpec(memory_space=pltpu.SMEM)] + whole,
+        out_specs=whole * len(shapes),
+        out_shape=[jax.ShapeDtypeStruct(shape, F32) for shape in shapes],
+        compiler_params=pltpu.CompilerParams(vmem_limit_bytes=VMEM_BYTES),
+        name="order",
+    )(sum_order(), values)
 
 
 def shards(
@@ -437,43 +463,68 @@
     row = lax.axis_index("row")
     col = lax.axis_index("col")
 
+    tok_own, sent = pick(tokens, row)
+    tok_oth = swap_row(sent)
+    tok = (tok_own, tok_oth)
+
     raw_condition = condition.astype(F32)
     act_cond = jax.nn.silu(raw_condition).astype(B16)
     mod_terms = jnp.einsum("ld,kde->lke", act_cond, adaptive, preferred_element_type=F32)
     kept, sent = pick(mod_terms, col)
-    mod_rows = kept + swap_col(sent) + adabias.astype(F32)
+    group = kept.shape[0]
+    latents = group // 2
+    col_bias = jnp.concatenate([attbias.reshape(-1), expbias]).astype(F32).reshape(-1, 1, HALF)
+    got = swap_col(
+        jnp.concatenate([sent.reshape(-1, HALF), col_bias.reshape(-1, HALF)], axis=0)
+    )
+    mod_rows = kept + got[: 6 * group].reshape(group, 6, HALF) + adabias.astype(F32)
+    col_other = got[6 * group :]
     kept, sent = pick(mod_rows, row)
-    modulation = jnp.concatenate([kept, swap_row(sent)], axis=2)
-
-    tok_own, sent = pick(tokens, row)
-    tok_oth = swap_row(sent)
-    tok = (tok_own, tok_oth)
-
-    def pieces(values):
-        over = swap_row(values)
-        return values, over, swap_col(values), swap_col(over)
-
-    attend_pieces = pieces(after(attend, tok_oth))
-    ready = attend_pieces[1]
-    out_pieces = pieces(after(outproj, ready))
-    exp_pieces = pieces(after(expand, ready))
-    shr_pieces = pieces(after(shrink, ready))
-    cot_own, sent = pick(cotangent, row)
-    cot_oth = swap_row(after(sent, ready))
-
-    by_col = jnp.concatenate([attbias.reshape(-1), expbias]).astype(F32)
-    by_row = jnp.concatenate([outbias, shrbias]).astype(F32)
-    by_col = (by_col, swap_col(by_col))
-    by_row = (by_row, swap_row(by_row))
+    row_bias = jnp.stack([outbias, shrbias]).astype(F32)
+    got = swap_row(jnp.concatenate([sent.reshape(-1, HALF), row_bias], axis=0))
+    modulation = jnp.concatenate([kept, got[: 6 * latents].reshape(latents, 6, HALF)], axis=2)
+    row_other = got[6 * latents :]
+    col_bias = col_bias.reshape(-1, HALF)
     blank = jnp.zeros((HALF,), F32)
     bias = jnp.concatenate(
-        [piece for part in by_col for piece in (part[:HALF], blank, part[HALF:D])]
+        [piece for part in (col_bias, col_other) for piece in (part[0], blank, part[1])]
     )[None]
-    exp_bias = jnp.concatenate([part[D:] for part in by_col])[None]
-    out_bias = jnp.concatenate([part[:HALF] for part in by_row])[None]
-    shr_bias = jnp.concatenate([part[HALF:] for part in by_row])[None]
-
+    exp_bias = jnp.concatenate([col_bias[2:], col_other[2:]], axis=0).reshape(1, FF)
+    out_bias = jnp.concatenate([row_bias[:1], row_other[:1]], axis=1)
+    shr_bias = jnp.concatenate([row_bias[1:], row_other[1:]], axis=1)
+
+    def pieces(values, over):
+        return values, over, swap_col(values), swap_col(over)
+
+    def near(values):
+        return pick(values, x_place())[0]
+
+    def relayed(half):
+        return in_order(x_place(), half, swap_dp(half, 1))
+
+    flat_attend = attend.reshape(-1, attend.shape[2])
+    att_half = swap_row(after(near(flat_attend), tok_oth, got))
+    att_half, exp_half = lax.optimization_barrier((att_half, near(expand)))
+    exp_half = swap_row(exp_half)
+    attend_pieces = pieces(attend, relayed(att_half).reshape(attend.shape))
+    cond_all = gather_dp(act_cond)
+    *attend_pieces, exp_half, shr_half, outproj, cond_all = lax.optimization_barrier(
+        (*attend_pieces, exp_half, near(shrink), outproj, cond_all)
+    )
+    shr_half, out_over = swap_row(shr_half), swap_row(outproj)
+    exp_far = swap_dp(exp_half, 1)
+    cot_own, cot_sent = pick(cotangent, row)
     first, qkv, attended = call_forward(tok_own, tok_oth, modulation, bias, attend_pieces)
+    attended, exp_half, exp_far, shr_half, out_over, cot_sent = lax.optimization_barrier(
+        (attended, exp_half, exp_far, shr_half, out_over, cot_sent)
+    )
+    cot_oth = swap_row(cot_sent)
+    shr_far = swap_dp(shr_half, 1)
+    exp_over = in_order(x_place(), exp_half, exp_far)
+    out_pieces = pieces(outproj, out_over)
+    exp_pieces = pieces(expand, exp_over)
+    shr_over = in_order(x_place(), shr_half, shr_far)
+    shr_pieces = pieces(shrink, shr_over)
     (
         res_own, res_oth, second, act_own, act_oth, dh_own, dh_oth, e_one, e_two,
         d_middle, d_attended, mod_late, sums_late,
@@ -481,50 +532,120 @@
         tok, (cot_own, cot_oth), attended, modulation, (out_bias, exp_bias, shr_bias),
         out_pieces, exp_pieces, shr_pieces,
     )
-    result = in_order(row, res_own, swap_row(res_oth))
-    shrink_part = reduce_grid(lambda: dot_tn(act_own, e_two), lambda: dot_tn(act_oth, e_two), 1)
-    expand_part = reduce_grid(lambda: dot_tn(second, dh_own), lambda: dot_tn(second, dh_oth), 0)
     att_own, att_oth = halves(attended, 1)
-    outproj_part = reduce_grid(lambda: dot_tn(att_own, e_one), lambda: dot_tn(att_oth, e_one), 1)
+    depth = act_oth.shape[1]
+    shr_got = swap_col(
+        jnp.concatenate(
+            [dot_tn(act_oth, e_two).astype(B16), dot_tn(att_oth, e_one).astype(B16)], axis=0
+        )
+    )
+    exp_got = swap_col(dot_tn(second, dh_oth).astype(B16))
+    shr_total = dot_tn(act_own, e_two) + shr_got[:depth].astype(F32)
+    out_total = dot_tn(att_own, e_one) + shr_got[depth:].astype(F32)
+    exp_total = dot_tn(second, dh_own) + exp_got.astype(F32)
+    d_attended, shr_total, out_total, exp_total = lax.optimization_barrier(
+        (d_attended, shr_total, out_total, exp_total)
+    )
+    near_step, *far_steps = distances()
+    size = lax.axis_size("dp")
+    shr_mine, shr_theirs = [
+        jnp.concatenate(
+            [part.reshape(size, -1, HALF) for part in parts], axis=1
+        )
+        for parts in zip(halves(shr_total, 1), halves(out_total, 1))
+    ]
+    shr_part = shr_mine + swap_row(shr_theirs.astype(B16)).astype(F32)
+    exp_part = scatter_stage(exp_total.reshape(2, HALF, -1), near_step, 1)
+
     dqkv_own, dqkv_oth, grad_own, grad_oth, mod_early, sums_early = call_backward(
         tok, modulation, qkv, d_attended, d_middle, attend_pieces
     )
-    attend_part = reduce_grid(lambda: dot_tn(first, dqkv_own), lambda: dot_tn(first, dqkv_oth), 0)
+    dqkv_own, dqkv_oth, shr_part, exp_part = lax.optimization_barrier(
+        (dqkv_own, dqkv_oth, shr_part, exp_part)
+    )
+    exp_part = exp_part[0] + swap_row(exp_part[1].astype(B16)).astype(F32)
+    shr_part = scatter_stage(shr_part, near_step)
+    att_got = swap_col(dot_tn(first, dqkv_oth).astype(B16)).astype(F32)
+    att_total = dot_tn(first, dqkv_own) + att_got
+    att_total, shr_part, exp_part, mod_early, res_oth = lax.optimization_barrier(
+        (att_total, shr_part, exp_part, mod_early, res_oth)
+    )
+    att_mine, att_theirs = halves(att_total, 0)
+    att_part = att_mine + swap_row(att_theirs.astype(B16)).astype(F32)
+    exp_part = exp_part.reshape(size // 2, HALF // size, -1)
+    grid_part = jnp.concatenate(
+        [shr_part]
+        + [
+            exp_part[:, :, at : at + HALF] for at in range(0, exp_part.shape[2], HALF)
+        ],
+        axis=1,
+    )
+    grid_part = scatter_stage(grid_part, far_steps[0])
+
+    d_modulation = jnp.concatenate([mod_early, mod_late], axis=1).astype(B16).astype(F32)
+    sums_late = jnp.sum(sums_late, axis=(0, 1))
+    sums_early = jnp.sum(sums_early, axis=(0, 1)).reshape(6, HALF)
+    row_sums = sums_late[: 2 * D].reshape(2, 2, HALF)
+    wide = sums_late[2 * D :].reshape(2, -1, HALF)
+    col_sums = jnp.concatenate(
+        [sums_early[0:3:2], wide[0], sums_early[3:6:2], wide[1]], axis=0
+    )
+    mine = d_modulation[:, :, :HALF].reshape(-1, HALF)
+    theirs = d_modulation[:, :, HALF:].reshape(-1, HALF)
+    got = swap_row(jnp.concatenate([theirs, row_sums[:, 1], col_sums], axis=0))
+    rows = mine.shape[0]
+    block = in_order(row, mine, got[:rows]).astype(B16)
+    sums = jnp.concatenate([row_sums[:, 0], col_sums], axis=0) + got[rows:]
+    high = sums.astype(B16)
+    low = (sums - high.astype(F32)).astype(B16)
+    width = block.shape[0] + 2 * sums.shape[0]
+    packed = jnp.concatenate([block, high, low], axis=0)[None]
+    att_part, packed, grid_part, grad_oth, res_oth = lax.optimization_barrier(
+        (att_part, packed, grid_part, grad_oth, res_oth)
+    )
+    attend_grad = lax.psum(att_part.astype(B16), "dp").astype(F32)
+    attend_grad = attend_grad.reshape(HALF, 3, HALF).transpose(1, 0, 2)
+    packed_all = gather_dp(packed)
+    for distance in far_steps[1:]:
+        grid_part = scatter_stage(grid_part, distance)
+    block_all = packed_all[:, : block.shape[0]].reshape(-1, HALF)
+    both_sums = jnp.sum(packed_all[:, block.shape[0] :].astype(F32), axis=0)
+    sums = both_sums[: sums.shape[0]] + both_sums[sums.shape[0] :]
+    count = col_sums.shape[0] // 2
+    given = jnp.concatenate([sums[:2], sums[2 + count :]], axis=0)
+    high = given.astype(B16)
+    low = (given - high.astype(F32)).astype(B16)
+    got = swap_col(jnp.concatenate([block_all, high, low], axis=0))
+    other_all = got[: block_all.shape[0]]
+    got = got[block_all.shape[0] :].astype(F32)
+    sums = sums[: 2 + count] + got[: 2 + count] + got[2 + count :]
+    outbias_grad, shrbias_grad = sums[0], sums[1]
+    attbias_grad = sums[2:4]
+    expbias_grad = sums[4:].reshape(-1)
+
+    result = in_order(row, res_own, swap_row(res_oth))
     input_gradient = in_order(row, grad_own, swap_row(grad_oth))
-    shrink_grad = sum_dp(shrink_part)
-    expand_grad = sum_dp(expand_part)
-    outproj_grad = sum_dp(outproj_part)
-    attend_grad = sum_dp(attend_part).reshape(HALF, 3, HALF).transpose(1, 0, 2)
-
-    d_modulation = jnp.concatenate([mod_early, mod_late], axis=1).astype(B16)
-    mine, theirs = halves(d_modulation, 2)
-    mod_block = in_order(row, mine, swap_row(theirs))
-    mod_group = in_order(col, mod_block, swap_col(mod_block))
-    mod_all = gather_dp(mod_group)
-    cond_all = gather_dp(act_cond)
+    exp_width = expand.shape[1]
+    shrink_grad, outproj_grad, expand_grad = order(
+        order_grid_kernel,
+        gather_dp(grid_part.astype(B16)),
+        [(size, depth // size, HALF), (size, HALF // size, HALF), (size, HALF // size, exp_width)],
+    )
+    shrink_grad, outproj_grad = [part.reshape(-1, HALF) for part in (shrink_grad, outproj_grad)]
+    expand_grad = expand_grad.reshape(HALF, exp_width)
+    mod_all = jnp.concatenate([block_all, other_all], axis=0).reshape(-1, 6, HALF)
+    cond_mine, cond_theirs = pick(
+        cond_all.reshape(-1, 2 * group, HALF).transpose(1, 0, 2), col
+    )
+    cond_all = jnp.concatenate(
+        [part.transpose(1, 0, 2).reshape(-1, HALF) for part in (cond_mine, cond_theirs)], axis=0
+    )
     adabias_grad = jnp.sum(mod_all, axis=0, dtype=F32)
     adaptive_grad = jnp.einsum("ld,lke->kde", cond_all, mod_all, preferred_element_type=F32)
+    mod_group = in_order(col, block, other_all[: block.shape[0]]).reshape(-1, 6, HALF)
     d_act = jnp.einsum("lke,kde->ld", mod_group, adaptive, preferred_element_type=F32)
     d_act = d_act + swap_row(d_act)
     condition_gradient = jax.vjp(jax.nn.silu, raw_condition)[1](d_act)[0].astype(B16)
-
-    sums_late = jnp.sum(sums_late, axis=(0, 1))
-    sums_early = jnp.sum(sums_early, axis=(0, 1))
-    mine, theirs = halves(sums_late[: 2 * D].reshape(2, D), 1)
-    row_sums = mine + swap_row(theirs)
-    row_sums = row_sums + swap_col(row_sums)
-    wide = halves(sums_late[2 * D :], 0)
-    narrow = halves(sums_early, 0)
-    mine, theirs = [jnp.concatenate([narrow[side], wide[side]]) for side in range(2)]
-    col_sums = mine + swap_col(theirs)
-    col_sums = col_sums + swap_row(col_sums)
-    sums = jnp.concatenate([row_sums.reshape(-1), col_sums])
-    for distance in distances():
-        sums = sums + swap_dp(sums, distance)
-    outbias_grad = sums[:HALF]
-    shrbias_grad = sums[HALF:D]
-    attbias_grad = jnp.stack([sums[D : D + HALF], sums[2 * D : 2 * D + HALF]])
-    expbias_grad = sums[D + SIDE :]
     return (
         result, input_gradient, condition_gradient, adaptive_grad, adabias_grad, attend_grad,
         attbias_grad, outproj_grad, outbias_grad, expand_grad, expbias_grad, shrink_grad,

time: 495 us -> 451 us (0.911)
  waiting for transfers between devices: 242 us -> 157 us
  other arithmetic: 21.4 us -> 40.3 us
  local copies, waits for them, and re-layouts: 32.5 us -> 51 us
  starting transfers between devices: 58.8 us -> 42.2 us
  between operations: 2.08 us -> 15.5 us
    ppermute x18 -> x14, waiting for transfers between devices: 153 us -> 67.9 us  [swap_row(): return lax.ppermute(values, 'row', SWAP)]
    ppermute x33 -> x16, waiting for transfers between devices: 88.4 us -> 51.4 us  [swap_dp(): lax.ppermute(values, 'dp', [(place, place ^ distance) for place in range(...]
    psum x0 -> x1, waiting for transfers between devices: none -> 36.1 us  [shards(): attend_grad = lax.psum(att_part.astype(B16), 'dp').astype(F32)]
    ppermute x33 -> x16, starting transfers between devices: 33.1 us -> 21.2 us  [swap_dp(): lax.ppermute(values, 'dp', [(place, place ^ distance) for place in range(...]
    add x20 -> x9, other arithmetic: 4.46 us -> 11.8 us  [the longest x3 4.3 us: scatter_stage(): return kept + swap_dp(sent.astype(B16), distance).astype(F32)]
    concatenate x4 -> x8, other arithmetic: 0.18 us -> 6.8 us  [gather_dp(): values = jnp.concatenate([values, swap_dp(values, distance)], axis=0)]
    dynamic_slice x2 -> x5, local copies, waits for them, and re-layouts: 0.03 us -> 6.59 us  [pick(): kept = lax.dynamic_slice_in_dim(values, place * size, size, 0)]
    ppermute x18 -> x14, starting transfers between devices: 22.8 us -> 18.7 us  [swap_row(): return lax.ppermute(values, 'row', SWAP)]
  transfers between devices with their start and end apart: 68 -> 44, of which waited for: 36 -> 18; matrix products, arithmetic and copies ran while one was open for 16% -> 19% of each run, Pallas kernels for 10% -> 11%
where the time goes in v2:
time: 451 us; the launch traced here: 444 us
  waiting for transfers between devices  157 us (35%)
  Pallas kernels  102 us (23%)
  local copies, waits for them, and re-layouts  51 us (11%)
  starting transfers between devices  42.2 us (9%)
  other arithmetic  40.3 us (9%)
  matrix products  36.3 us (8%)
  between operations  15.5 us (3%)
    ppermute x14, waiting for transfers between devices, swap_row(): return lax.ppermute(values, 'row', SWAP)  67.9 us
    ppermute x16, waiting for transfers between devices, swap_dp(): lax.ppermute(values, 'dp', [(place, place ^ distance) for place in range(...  51.4 us
    pallas_call x1, Pallas kernels, call_middle(): pl.pallas_call(middle_kernel, grid=(steps,), in_specs=halves + halves + [...  49.2 us
    psum x1, waiting for transfers between devices, shards(): attend_grad = lax.psum(att_part.astype(B16), 'dp').astype(F32)  36.1 us
    dot_general x8, matrix products, dot_tn(): lax.dot_general(left, right, (((0,), (0,)), ((), ())), preferred_element_...  32.3 us
    pallas_call x1, Pallas kernels, call_backward(): pl.pallas_call(backward_kernel, grid=(latents,), in_specs=[tiles(SEQ, HAL...  31.5 us
    ppermute x16, starting transfers between devices, swap_dp(): lax.ppermute(values, 'dp', [(place, place ^ distance) for place in range(...  21.2 us
    ppermute x14, starting transfers between devices, swap_row(): return lax.ppermute(values, 'row', SWAP)  18.7 us
  transfers between devices with their start and end apart: 44, of which 18 were waited for; matrix products, arithmetic and copies ran while one was open for 19% of the time, Pallas kernels for 11%

profile of v2, /device:TPU:0, one launch (start us, length us, event | category | flops | bytes accessed | tf_op | source)
XLA Modules:
  0.0 443.6 jit_solution(13543943367808312437)
XLA Ops:
  7.3 1.4 copy-done
  11.0 1.3 constant_dynamic-slice_fusion.9
  12.4 2.6 collective-permute-start
  15.0 2.7 collective-permute-start.8
  22.6 1.8 constant_dynamic-slice_fusion.3
  24.4 10.0 %collective-permute-done.2 = f32[26,384]{1,0:T(8,128)S(1)} collective-permute-done((f32[26,384]{1,0:T(8,128)S(1)}, f32[26,384]{1,0:T(8,128)S(1)}, u32[]{:S(2)}, u32[]{:S(2)}) %collective-permute-start.2) | collective-permute-done | bytes 39968 | tf_op jit(solution)/shard_map/ppermute | solution.py:368
  34.4 1.7 collective-permute-start.3
  36.1 1.9 constant_dynamic-slice_fusion.2
  38.0 8.6 %collective-permute-done.3 = bf16[576,384]{1,0:T(8,128)(2,1)} collective-permute-done((bf16[576,384]{1,0:T(8,128)(2,1)}, bf16[576,384]{1,0:T(8,128)(2,1)}, u32[]{:S(2)}, u32[]{:S(2)}) %collective-permute-start.3) | collective-permute-done | bytes 442400 | tf_op jit(solution)/shard_map/ppermute | solution.py:368
  46.7 1.5 collective-permute-start.4
  49.5 1.6 collective-permute-start.9
  51.2 6.9 %collective-permute-done.4 = bf16[576,384]{1,0:T(8,128)(2,1)} collective-permute-done((bf16[576,384]{1,0:T(8,128)(2,1)}, bf16[576,384]{1,0:T(8,128)(2,1)}, u32[]{:S(2)}, u32[]{:S(2)}) %collective-permute-start.4) | collective-permute-done | bytes 442400 | tf_op jit(solution)/shard_map/ppermute | solution.py:377
  59.5 2.2 constant_dynamic-slice_fusion.1
  63.0 1.5 collective-permute-start.7
  67.3 11.1 %collective-permute-done.7 = bf16[192,1536]{1,0:T(8,128)(2,1)S(1)} collective-permute-done((bf16[192,1536]{1,0:T(8,128)(2,1)}, bf16[192,1536]{1,0:T(8,128)(2,1)S(1)}, u32[]{:S(2)}, u32[]{:S(2)}) %collective-permute-start.7) | collective-permute-done | bytes 589856 | tf_op jit(solution)/shard_map/ppermute | solution.py:368
  81.3 16.5 %forward.1 = (bf16[1024,768]{1,0:T(8,128)(2,1)}, bf16[1024,2304]{1,0:T(8,128)(2,1)}, bf16[1024,768]{1,0:T(8,128)(2,1)}) custom-call(bf16[1024,384]{1,0:T(8,128)(2,1)} %get-tuple-element.172.tok_own, bf16[1024,384]{1,0:T(8,128)(2,1)} %collective-permute-done.tok_oth, f32[4,6,768]{2,1,0:T(8,128)} %pad_maximum_fusion.14.mod, f32[1,2304]{1,0:T(1,128)} %broadcast_in_dim.14.bias, ...), custom_call_target="tpu_custom_call" | custom-call | flops 14000000000 | bytes 16000000 | tf_op jit(solution)/shard_map/forward/pallas_call | solution.py:275
  97.8 2.0 collective-permute-done.13.o1
  102.5 10.8 %collective-permute-done.19 = bf16[768,384]{1,0:T(8,128)(2,1)S(1)} collective-permute-done((bf16[768,384]{1,0:T(8,128)(2,1)}, bf16[768,384]{1,0:T(8,128)(2,1)S(1)}, u32[]{:S(2)}, u32[]{:S(2)}) %collective-permute-start.19) | collective-permute-done | bytes 589856 | tf_op jit(solution)/shard_map/ppermute | solution.py:377
  120.5 15.4 %collective-permute-done.14.cot_oth = bf16[1024,384]{1,0:T(8,128)(2,1)} collective-permute-done((bf16[1024,384]{1,0:T(8,128)(2,1)}, bf16[1024,384]{1,0:T(8,128)(2,1)}, u32[]{:S(2)}, u32[]{:S(2)}) %collective-permute-start.14) | collective-permute-done | bytes 786464 | tf_op jit(solution)/shard_map/ppermute | solution.py:368
  135.9 49.2 %middle.1 = (bf16[1024,384]{1,0:T(8,128)(2,1)}, bf16[1024,384]{1,0:T(8,128)(2,1)}, bf16[1024,768]{1,0:T(8,128)(2,1)}, bf16[1024,1536]{1,0:T(8,128)(2,1)}, bf16[1...) custom-call(bf16[1024,384]{1,0:T(8,128)(2,1)} %get-tuple-element.172, ...), custom_call_target="tpu_custom_call" | custom-call | flops 30000001024 | bytes 50000000 | tf_op jit(solution)/shard_map/middle/pallas_call | solution.py:305
  185.1 6.6 %convolution_convert_fusion = bf16[768,1536]{1,0:T(8,128)(2,1)} fusion(bf16[1024,768]{1,0:T(8,128)(2,1)} %get-tuple-element.98, bf16[1024,1536]{1,0:T(8,128)(2,1)} %get-tuple-element.100), kind=kOutput, calls=%fused_computation.3 | convolution fusion | flops 2417098752 | bytes 7077888 | tf_op jit(solution)/shard_map/dot_general | solution.py:37
  194.0 2.9 convolution_convert_fusion.1
  197.0 1.8 pad_maximum_fusion
  199.3 5.5 %convert_add_fusion = f32[768,1536]{1,0:T(8,128)S(1)} fusion(bf16[768,1536]{1,0:T(8,128)(2,1)} %collective-permute-done.23, bf16[1024,768]{1,0:T(8,128)(2,1)S(1)} %copy-done.10, bf16[1024,1536]{1,0:T(8,128)(2,1)} %get-tuple-element.99), kind=kOutput, calls=%fused_computation | convolution fusion | flops 2418278400 | bytes 11796480 | tf_op jit(solution)/shard_map/dot_general | solution.py:37
  204.8 2.5 convolution_add_fusion.1
  207.4 1.6 copy-done.44
  209.4 4.5 %convert_add_fusion.1 = f32[1536,768]{1,0:T(8,128)S(1)} fusion(bf16[1024,1536]{1,0:T(8,128)(2,1)S(1)} %copy-done.44, bf16[1024,768]{1,0:T(8,128)(2,1)S(1)} %copy-done.48, bf16[1920,768]{1,0:T(8,128)(2,1)} %collective-permute-done.22), kind=kOutput, calls=%fused_computation.1 | convolution fusion | flops 2418278400 | bytes 11796480 | tf_op jit(solution)/shard_map/dot_general | solution.py:37
  218.7 31.5 %backward.1 = (bf16[1024,1152]{1,0:T(8,128)(2,1)}, bf16[1024,1152]{1,0:T(8,128)(2,1)}, bf16[1024,384]{1,0:T(8,128)(2,1)}, bf16[1024,384]{1,0:T(8,128)(2,1)}, f32...) custom-call(bf16[1024,384]{1,0:T(8,128)(2,1)} %get-tuple-element.172.tok_own, bf16[1024,384]{1,0:T(8,128)(2,1)} %collective-permute-done.tok_oth, ...), custom_call_target="tpu_custom_call" | custom-call | flops 24999999488 | bytes 20000000 | tf_op jit(solution)/shard_map/backward/pallas_call | solution.py:343
  250.3 2.5 convert_add_fusion.2
  253.1 3.8 maximum_add_fusion
  256.9 3.5 convolution_convert_fusion.2
  262.1 1.5 dynamic-slice_convert_fusion.1
  265.7 11.7 %collective-permute-done.28 = bf16[192,1536]{1,0:T(8,128)(2,1)} collective-permute-done((bf16[192,1536]{1,0:T(8,128)(2,1)}, bf16[192,1536]{1,0:T(8,128)(2,1)}, u32[]{:S(2)}, u32[]{:S(2)}) %collective-permute-start.28) | collective-permute-done | bytes 589856 | tf_op jit(solution)/shard_map/ppermute | solution.py:368
  277.3 1.6 bitcast_add_fusion
  278.9 3.4 collective-permute-done.27
  282.5 6.0 %convolution_add_fusion = f32[768,1152]{1,0:T(8,128)} fusion(bf16[1024,768]{1,0:T(8,128)(2,1)} %get-tuple-element.91, bf16[1024,1152]{1,0:T(8,128)(2,1)S(1)} %copy-done.42, bf16[768,1152]{1,0:T(8,128)(2,1)} %collective-permute-done.26), kind=kOutput, calls=%fused_computation.2 | convolution fusion | flops 1813708800 | bytes 9240576 | tf_op jit(solution)/shard_map/dot_general | solution.py:37
  288.8 1.5 copy-done.5
  291.1 1.4 collective-permute-start.31
  293.2 1.8 concatenate.139
  295.1 1.5 collective-permute-start.30
  296.6 1.6 slice.368
  300.0 2.6 concatenate.140
  302.6 1.4 slice.296
  304.0 1.4 reshape.168
  307.9 1.6 convert_add_fusion.5
  309.5 9.1 %collective-permute-done.29 = bf16[384,1152]{1,0:T(8,128)(2,1)S(1)} collective-permute-done((bf16[384,1152]{1,0:T(8,128)(2,1)S(1)}, bf16[384,1152]{1,0:T(8,128)(2,1)S(1)}, u32[]{:S(2)}, u32[]{:S(2)}) %collective-permute-start.29) | collective-permute-done | bytes 884768 | tf_op jit(solution)/shard_map/ppermute | solution.py:368
  319.7 2.6 collective-permute-start.34
  322.4 3.2 collective-permute-done.34
  325.6 2.6 collective-permute-start.39
  328.2 2.2 collective-permute-done.35
  330.5 1.5 collective-permute-start.36
  332.1 8.2 %collective-permute-done.39 = bf16[1,432,384]{2,1,0:T(8,128)(2,1)S(1)} collective-permute-done((bf16[1,432,384]{2,1,0:T(8,128)(2,1)S(1)}, bf16[1,432,384]{2,1,0:T(8,128)(2,1)S(1)}, u32[]{:S(2)}, u32[]{:S(2)}) %collective-permute-start.39) | collective-permute-done | bytes 331808 | tf_op jit(solution)/shard_map/ppermute | solution.py:377
  340.8 1.9 collective-permute-start.33
  342.9 2.2 copy.35
  345.1 15.1 %collective-permute-done.40 = bf16[1,432,384]{2,1,0:T(8,128)(2,1)S(1)} collective-permute-done((bf16[1,432,384]{2,1,0:T(8,128)(2,1)S(1)}, bf16[1,432,384]{2,1,0:T(8,128)(2,1)S(1)}, u32[]{:S(2)}, u32[]{:S(2)}) %collective-permute-start.40) | collective-permute-done | bytes 331808 | tf_op jit(solution)/shard_map/ppermute | solution.py:377
  364.3 2.5 convolution_bitcast_fusion
  369.5 5.2 %copy.36 = f32[6,384,384]{2,1,0:T(8,128)} copy(f32[6,384,384]{1,2,0:T(8,128)} %convolution_bitcast_fusion) | data formatting | bytes 7077888
  375.3 2.8 collective-permute-start.38
  379.5 1.6 collective-permute-done.41
  381.1 2.3 pad_maximum_fusion.5
  390.4 36.1 %all-reduce.2.cloned.1.call-done = bf16[3,384,384]{1,2,0:T(8,128)(2,1)} async-done(((bf16[3,384,384]{1,2,0:T(8,128)(2,1)}), bf16[3,384,384]{1,2,0:T(8,128)(2,1)}) %all-reduce.2.cloned.1.call-update) | async-done | bytes 884752 | tf_op jit(solution)/shard_map/psum | solution.py:606
  426.6 2.5 copy.37
  429.1 2.8 pad_maximum_fusion.1.values
  431.9 4.4 order.1
  (279 shorter events, 63.0 us)
Async XLA Ops:
  7.2 419.3 %all-reduce.2.cloned.1.call-start = ((), (), s32[]{:S(2)}) async-start(), calls=%async_computation | async-start | bytes 1769472 | tf_op jit(solution)/shard_map/psum | solution.py:606
  10.4 9.0 %copy-start.33 = (bf16[384]{0:T(512)(128)(2,1)S(1)}, bf16[384]{0:T(512)(128)(2,1)}, u32[]{:S(2)}) copy-start(bf16[384]{0:T(512)(128)(2,1)} %param.24) | copy-start | bytes 2308
  10.5 9.6 %collective-permute-start.1 = (f32[54,384]{1,0:T(8,128)S(1)}, f32[54,384]{1,0:T(8,128)}, u32[]{:S(2)}, u32[]{:S(2)}) collective-permute-start(f32[54,384]{1,0:T(8,128)S(1)} %pad_maximum_fusion.16), channel_id=1, source_target_pairs={{0,1},{1,0},{2,3},{3,2},{4,5},{5,4},{6,7},{7,6},{8,9},{9,8},{10,11... | collective-permute-start | bytes 248840 | tf_op jit(solution)/shard_map/ppermute | solution.py:372
  12.4 35.8 %copy-start.9 = (bf16[2048,384]{1,0:T(8,128)(2,1)S(1)}, bf16[2048,384]{1,0:T(8,128)(2,1)}, u32[]{:S(2)}) copy-start(bf16[2048,384]{1,0:T(8,128)(2,1)} %param.25) | copy-start | bytes 4718596
  12.4 22.0 %collective-permute-start = (bf16[1024,384]{1,0:T(8,128)(2,1)}, bf16[1024,384]{1,0:T(8,128)(2,1)}, u32[]{:S(2)}, u32[]{:S(2)}) collective-permute-start(bf16[1024,384]{1,0:T(8,128)(2,1)} %get-tuple-element.171), channel_id=1, source_target_pairs={{0,2},{2,0},{1,3},{3,1},{4,6},{6,4},{5,7},{7,5},{8,10},{10,8},{9,1... | collective-permute-start | bytes 2359304 | tf_op jit(solution)/shard_map/ppermute | solution.py:368
  15.0 34.6 %collective-permute-start.8 = (bf16[16,384]{1,0:T(8,128)(2,1)S(1)}, bf16[16,384]{1,0:T(8,128)(2,1)S(1)}, u32[]{:S(2)}, u32[]{:S(2)}) collective-permute-start(bf16[16,384]{1,0:T(8,128)(2,1)S(1)} %fusion.11), channel_id=1, source_target_pairs={{0,16},{4,20},{8,24},{12,28},{16,0},{20,4},{24,8},{28,12},{1,17},{... | collective-permute-start | bytes 36872 | tf_op jit(solution)/shard_map/ppermute | solution.py:377
  17.6 49.7 %collective-permute-start.5 = (bf16[3,384,384]{2,1,0:T(8,128)(2,1)}, bf16[3,384,384]{2,1,0:T(8,128)(2,1)}, u32[]{:S(2)}, u32[]{:S(2)}) collective-permute-start(bf16[3,384,384]{2,1,0:T(8,128)(2,1)} %w0.1), channel_id=1, source_target_pairs={{0,1},{1,0},{2,3},{3,2},{4,5},{5,4},{6,7},{7,6},{8,9},{9,8},{10,11... | collective-permute-start | bytes 2654216 | tf_op jit(solution)/shard_map/ppermute | solution.py:372
  17.6 100.7 %collective-permute-start.17 = (bf16[384,1536]{1,0:T(8,128)(2,1)}, bf16[384,1536]{1,0:T(8,128)(2,1)}, u32[]{:S(2)}, u32[]{:S(2)}) collective-permute-start(bf16[384,1536]{1,0:T(8,128)(2,1)} %x0.1), channel_id=1, source_target_pairs={{0,1},{1,0},{2,3},{3,2},{4,5},{5,4},{6,7},{7,6},{8,9},{9,8},{10,11... | collective-permute-start | bytes 3538952 | tf_op jit(solution)/shard_map/ppermute | solution.py:372
  22.0 12.4 %collective-permute-start.2 = (f32[26,384]{1,0:T(8,128)S(1)}, f32[26,384]{1,0:T(8,128)S(1)}, u32[]{:S(2)}, u32[]{:S(2)}) collective-permute-start(f32[26,384]{1,0:T(8,128)S(1)} %pad_maximum_fusion.18), channel_id=1, source_target_pairs={{0,2},{2,0},{1,3},{3,1},{4,6},{6,4},{5,7},{7,5},{8,10},{10,8},{9,1... | collective-permute-start | bytes 119816 | tf_op jit(solution)/shard_map/ppermute | solution.py:368
  34.4 12.3 %collective-permute-start.3 = (bf16[576,384]{1,0:T(8,128)(2,1)}, bf16[576,384]{1,0:T(8,128)(2,1)}, u32[]{:S(2)}, u32[]{:S(2)}) collective-permute-start(bf16[576,384]{1,0:T(8,128)(2,1)} %constant_dynamic-slice_fusion.3), channel_id=1, source_target_pairs={{0,2},{2,0},{1,3},{3,1},{4,6},{6,4},{5,7},{7,5},{8,10},{10,8},{9,1... | collective-permute-start | bytes 1327112 | tf_op jit(solution)/shard_map/ppermute | solution.py:368
  46.7 11.4 %collective-permute-start.4 = (bf16[576,384]{1,0:T(8,128)(2,1)}, bf16[576,384]{1,0:T(8,128)(2,1)}, u32[]{:S(2)}, u32[]{:S(2)}) collective-permute-start(bf16[576,384]{1,0:T(8,128)(2,1)} %collective-permute-done.3), channel_id=1, source_target_pairs={{0,4},{4,0},{8,12},{12,8},{16,20},{20,16},{24,28},{28,24},{1,5},{5... | collective-permute-start | bytes 1327112 | tf_op jit(solution)/shard_map/ppermute | solution.py:377
  49.5 12.2 %collective-permute-start.9 = (bf16[32,384]{1,0:T(8,128)(2,1)S(1)}, bf16[32,384]{1,0:T(8,128)(2,1)S(1)}, u32[]{:S(2)}, u32[]{:S(2)}) collective-permute-start(bf16[32,384]{1,0:T(8,128)(2,1)S(1)} %pad_maximum_fusion.21), channel_id=1, source_target_pairs={{0,8},{4,12},{8,0},{12,4},{16,24},{20,28},{24,16},{28,20},{1,9},{5... | collective-permute-start | bytes 73736 | tf_op jit(solution)/shard_map/ppermute | solution.py:377
  59.3 6.0 %copy-start.30 = (f32[2304]{0:T(1024)S(1)}, f32[2304]{0:T(1024)}, u32[]{:S(2)}) copy-start(f32[2304]{0:T(1024)} %copy-done.29) | copy-start | bytes 27652
  59.4 21.8 %copy-start.12 = (bf16[1152,384]{1,0:T(8,128)(2,1)}, bf16[1152,384]{1,0:T(8,128)(2,1)S(1)}, u32[]{:S(2)}) copy-start(bf16[1152,384]{1,0:T(8,128)(2,1)S(1)} %pad_maximum_fusion.8) | copy-start | bytes 2654212
  59.4 19.0 %collective-permute-start.6 = (bf16[3,384,384]{2,1,0:T(8,128)(2,1)S(1)}, bf16[3,384,384]{2,1,0:T(8,128)(2,1)}, u32[]{:S(2)}, u32[]{:S(2)}) collective-permute-start(bf16[3,384,384]{2,1,0:T(8,128)(2,1)S(1)} %bitcast.76), channel_id=1, source_target_pairs={{0,1},{1,0},{2,3},{3,2},{4,5},{5,4},{6,7},{7,6},{8,9},{9,8},{10,11... | collective-permute-start | bytes 2654216 | tf_op jit(solution)/shard_map/ppermute | solution.py:372
  61.7 4.3 collective-permute-start.10
  63.0 15.4 %collective-permute-start.7 = (bf16[192,1536]{1,0:T(8,128)(2,1)}, bf16[192,1536]{1,0:T(8,128)(2,1)S(1)}, u32[]{:S(2)}, u32[]{:S(2)}) collective-permute-start(bf16[192,1536]{1,0:T(8,128)(2,1)} %constant_dynamic-slice_fusion.2), channel_id=1, source_target_pairs={{0,2},{2,0},{1,3},{3,1},{4,6},{6,4},{5,7},{7,5},{8,10},{10,8},{9,1... | collective-permute-start | bytes 1769480 | tf_op jit(solution)/shard_map/ppermute | solution.py:368
  66.0 52.5 %collective-permute-start.20 = (bf16[1536,384]{1,0:T(8,128)(2,1)}, bf16[1536,384]{1,0:T(8,128)(2,1)}, u32[]{:S(2)}, u32[]{:S(2)}) collective-permute-start(bf16[1536,384]{1,0:T(8,128)(2,1)} %s0.1), channel_id=1, source_target_pairs={{0,1},{1,0},{2,3},{3,2},{4,5},{5,4},{6,7},{7,6},{8,9},{9,8},{10,11... | collective-permute-start | bytes 3538952 | tf_op jit(solution)/shard_map/ppermute | solution.py:372
  78.5 21.4 %collective-permute-start.11 = (bf16[192,1536]{1,0:T(8,128)(2,1)S(1)}, bf16[192,1536]{1,0:T(8,128)(2,1)}, u32[]{:S(2)}, u32[]{:S(2)}) collective-permute-start(bf16[192,1536]{1,0:T(8,128)(2,1)S(1)} %collective-permute-done.7), channel_id=1, source_target_pairs={{0,4},{4,0},{8,12},{12,8},{16,20},{20,16},{24,28},{28,24},{1,5},{5... | collective-permute-start | bytes 1769480 | tf_op jit(solution)/shard_map/ppermute | solution.py:377
  79.2 20.6 %collective-permute-start.12 = (bf16[768,384]{1,0:T(8,128)(2,1)}, bf16[768,384]{1,0:T(8,128)(2,1)}, u32[]{:S(2)}, u32[]{:S(2)}) collective-permute-start(bf16[768,384]{1,0:T(8,128)(2,1)} %constant_dynamic-slice_fusion.1), channel_id=1, source_target_pairs={{0,2},{2,0},{1,3},{3,1},{4,6},{6,4},{5,7},{7,5},{8,10},{10,8},{9,1... | collective-permute-start | bytes 1769480 | tf_op jit(solution)/shard_map/ppermute | solution.py:368
  80.5 19.3 %collective-permute-start.13 = (bf16[384,384]{1,0:T(8,128)(2,1)}, bf16[384,384]{1,0:T(8,128)(2,1)S(1)}, u32[]{:S(2)}, u32[]{:S(2)}) collective-permute-start(bf16[384,384]{1,0:T(8,128)(2,1)} %o0), channel_id=1, source_target_pairs={{0,2},{2,0},{1,3},{3,1},{4,6},{6,4},{5,7},{7,5},{8,10},{10,8},{9,1... | collective-permute-start | bytes 884744 | tf_op jit(solution)/shard_map/ppermute | solution.py:368
  99.8 13.4 %collective-permute-start.19 = (bf16[768,384]{1,0:T(8,128)(2,1)}, bf16[768,384]{1,0:T(8,128)(2,1)S(1)}, u32[]{:S(2)}, u32[]{:S(2)}) collective-permute-start(bf16[768,384]{1,0:T(8,128)(2,1)} %collective-permute-done.12), channel_id=1, source_target_pairs={{0,4},{4,0},{8,12},{12,8},{16,20},{20,16},{24,28},{28,24},{1,5},{5... | collective-permute-start | bytes 1769480 | tf_op jit(solution)/shard_map/ppermute | solution.py:377
  102.4 13.2 %copy-start.11 = (bf16[384,1536]{1,0:T(8,128)(2,1)}, bf16[384,1536]{1,0:T(8,128)(2,1)S(1)}, u32[]{:S(2)}) copy-start(bf16[384,1536]{1,0:T(8,128)(2,1)S(1)} %pad_maximum_fusion.6.x1) | copy-start | bytes 3538948
  102.4 33.5 %collective-permute-start.18 = (bf16[384,1536]{1,0:T(8,128)(2,1)S(1)}, bf16[384,1536]{1,0:T(8,128)(2,1)}, u32[]{:S(2)}, u32[]{:S(2)}) collective-permute-start(bf16[384,1536]{1,0:T(8,128)(2,1)S(1)} %pad_maximum_fusion.6.x1), channel_id=1, source_target_pairs={{0,1},{1,0},{2,3},{3,2},{4,5},{5,4},{6,7},{7,6},{8,9},{9,8},{10,11... | collective-permute-start | bytes 3538952 | tf_op jit(solution)/shard_map/ppermute | solution.py:372
  115.6 20.3 %collective-permute-start.21 = (bf16[1536,384]{1,0:T(8,128)(2,1)}, bf16[1536,384]{1,0:T(8,128)(2,1)}, u32[]{:S(2)}, u32[]{:S(2)}) collective-permute-start(bf16[1536,384]{1,0:T(8,128)(2,1)} %pad_maximum_fusion.7.s1), channel_id=1, source_target_pairs={{0,1},{1,0},{2,3},{3,2},{4,5},{5,4},{6,7},{7,6},{8,9},{9,8},{10,11... | collective-permute-start | bytes 3538952 | tf_op jit(solution)/shard_map/ppermute | solution.py:372
  115.6 20.3 %collective-permute-start.14 = (bf16[1024,384]{1,0:T(8,128)(2,1)}, bf16[1024,384]{1,0:T(8,128)(2,1)}, u32[]{:S(2)}, u32[]{:S(2)}) collective-permute-start(bf16[1024,384]{1,0:T(8,128)(2,1)} %get-tuple-element.84), channel_id=1, source_target_pairs={{0,2},{2,0},{1,3},{3,1},{4,6},{6,4},{5,7},{7,5},{8,10},{10,8},{9,1... | collective-permute-start | bytes 2359304 | tf_op jit(solution)/shard_map/ppermute | solution.py:368
  118.3 1.6 collective-permute-start.15
  118.5 2.0 collective-permute-start.16
  119.8 16.0 %copy-start.36 = (bf16[384,384]{1,0:T(8,128)(2,1)}, bf16[384,384]{1,0:T(8,128)(2,1)S(1)}, u32[]{:S(2)}) copy-start(bf16[384,384]{1,0:T(8,128)(2,1)S(1)} %collective-permute-done.15.o2) | copy-start | bytes 884740
  120.5 15.4 %copy-start.37 = (bf16[384,384]{1,0:T(8,128)(2,1)}, bf16[384,384]{1,0:T(8,128)(2,1)S(1)}, u32[]{:S(2)}) copy-start(bf16[384,384]{1,0:T(8,128)(2,1)S(1)} %collective-permute-done.16.o3) | copy-start | bytes 884740
  185.1 6.6 %copy-start.38 = (bf16[1024,768]{1,0:T(8,128)(2,1)S(1)}, bf16[1024,768]{1,0:T(8,128)(2,1)}, u32[]{:S(2)}) copy-start(bf16[1024,768]{1,0:T(8,128)(2,1)} %get-tuple-element.85.att) | copy-start | bytes 4718596
  185.1 6.6 %copy-start.40 = (bf16[1024,768]{1,0:T(8,128)(2,1)S(1)}, bf16[1024,768]{1,0:T(8,128)(2,1)}, u32[]{:S(2)}) copy-start(bf16[1024,768]{1,0:T(8,128)(2,1)} %get-tuple-element.97) | copy-start | bytes 4718596
  191.6 7.6 %collective-permute-start.23 = (bf16[768,1536]{1,0:T(8,128)(2,1)}, bf16[768,1536]{1,0:T(8,128)(2,1)}, u32[]{:S(2)}, u32[]{:S(2)}) collective-permute-start(bf16[768,1536]{1,0:T(8,128)(2,1)} %convolution_convert_fusion), channel_id=1, source_target_pairs={{0,1},{1,0},{2,3},{3,2},{4,5},{5,4},{6,7},{7,6},{8,9},{9,8},{10,11... | collective-permute-start | bytes 7077896 | tf_op jit(solution)/shard_map/ppermute | solution.py:372
  198.7 6.1 %collective-permute-start.22 = (bf16[1920,768]{1,0:T(8,128)(2,1)}, bf16[1920,768]{1,0:T(8,128)(2,1)}, u32[]{:S(2)}, u32[]{:S(2)}) collective-permute-start(bf16[1920,768]{1,0:T(8,128)(2,1)} %pad_maximum_fusion), channel_id=1, source_target_pairs={{0,1},{1,0},{2,3},{3,2},{4,5},{5,4},{6,7},{7,6},{8,9},{9,8},{10,11... | collective-permute-start | bytes 8847368 | tf_op jit(solution)/shard_map/ppermute | solution.py:372
  199.3 5.6 %copy-start.41 = (bf16[1024,768]{1,0:T(8,128)(2,1)S(1)}, bf16[1024,768]{1,0:T(8,128)(2,1)}, u32[]{:S(2)}) copy-start(bf16[1024,768]{1,0:T(8,128)(2,1)} %get-tuple-element.97) | copy-start | bytes 4718596
  204.8 9.2 %copy-start.1 = (f32[768,1536]{1,0:T(8,128)}, f32[768,1536]{1,0:T(8,128)S(1)}, u32[]{:S(2)}) copy-start(f32[768,1536]{1,0:T(8,128)S(1)} %convert_add_fusion) | copy-start | bytes 14155780
  207.4 42.9 %copy-start.6 = (f32[384,768]{1,0:T(8,128)}, f32[384,768]{1,0:T(8,128)S(1)}, u32[]{:S(2)}) copy-start(f32[384,768]{1,0:T(8,128)S(1)} %convolution_add_fusion.1) | copy-start | bytes 3538948
  214.1 36.2 %collective-permute-start.25 = (bf16[2,192,1536]{2,1,0:T(8,128)(2,1)S(1)}, bf16[2,192,1536]{2,1,0:T(8,128)(2,1)}, u32[]{:S(2)}, u32[]{:S(2)}) collective-permute-start(bf16[2,192,1536]{2,1,0:T(8,128)(2,1)S(1)} %dynamic-slice_convert_fusion), channel_id=1, source_target_pairs={{0,4},{4,0},{8,12},{12,8},{16,20},{20,16},{24,28},{28,24},{1,5},{5... | collective-permute-start | bytes 3538952 | tf_op jit(solution)/shard_map/ppermute | solution.py:377
  217.4 35.4 %collective-permute-start.24 = (bf16[8,240,384]{2,1,0:T(8,128)(2,1)}, bf16[8,240,384]{2,1,0:T(8,128)(2,1)}, u32[]{:S(2)}, u32[]{:S(2)}) collective-permute-start(bf16[8,240,384]{2,1,0:T(8,128)(2,1)} %pad_maximum_fusion.4), channel_id=1, source_target_pairs={{0,2},{2,0},{1,3},{3,1},{4,6},{6,4},{5,7},{7,5},{8,10},{10,8},{9,1... | collective-permute-start | bytes 4423688 | tf_op jit(solution)/shard_map/ppermute | solution.py:368
  252.8 7.6 %copy-start.4 = (f32[2,192,1536]{2,1,0:T(8,128)}, f32[2,192,1536]{2,1,0:T(8,128)S(1)}, u32[]{:S(2)}) copy-start(f32[2,192,1536]{2,1,0:T(8,128)S(1)} %convert_add_fusion.2) | copy-start | bytes 7077892
  260.4 22.1 %collective-permute-start.26 = (bf16[768,1152]{1,0:T(8,128)(2,1)}, bf16[768,1152]{1,0:T(8,128)(2,1)}, u32[]{:S(2)}, u32[]{:S(2)}) collective-permute-start(bf16[768,1152]{1,0:T(8,128)(2,1)} %convolution_convert_fusion.2), channel_id=1, source_target_pairs={{0,1},{1,0},{2,3},{3,2},{4,5},{5,4},{6,7},{7,6},{8,9},{9,8},{10,11... | collective-permute-start | bytes 5308424 | tf_op jit(solution)/shard_map/ppermute | solution.py:372
  261.3 16.1 %collective-permute-start.28 = (bf16[192,1536]{1,0:T(8,128)(2,1)}, bf16[192,1536]{1,0:T(8,128)(2,1)}, u32[]{:S(2)}, u32[]{:S(2)}) collective-permute-start(bf16[192,1536]{1,0:T(8,128)(2,1)} %fusion.2), channel_id=1, source_target_pairs={{0,2},{2,0},{1,3},{3,1},{4,6},{6,4},{5,7},{7,5},{8,10},{10,8},{9,1... | collective-permute-start | bytes 1769480 | tf_op jit(solution)/shard_map/ppermute | solution.py:368
  263.6 18.7 %collective-permute-start.27 = (bf16[4,240,384]{2,1,0:T(8,128)(2,1)S(1)}, bf16[4,240,384]{2,1,0:T(8,128)(2,1)S(1)}, u32[]{:S(2)}, u32[]{:S(2)}) collective-permute-start(bf16[4,240,384]{2,1,0:T(8,128)(2,1)S(1)} %dynamic-slice_convert_fusion.1), channel_id=1, source_target_pairs={{0,4},{4,0},{8,12},{12,8},{16,20},{20,16},{24,28},{28,24},{1,5},{5... | collective-permute-start | bytes 2211848 | tf_op jit(solution)/shard_map/ppermute | solution.py:377
  265.6 27.6 %copy-start.26 = (f32[2,384]{1,0:T(2,128)}, f32[2,384]{1,0:T(2,128)S(1)}, u32[]{:S(2)}) copy-start(f32[2,384]{1,0:T(2,128)S(1)} %slice.249) | copy-start | bytes 9220
  265.7 27.6 %copy-start.27 = (f32[2,384]{1,0:T(2,128)}, f32[2,384]{1,0:T(2,128)S(1)}, u32[]{:S(2)}) copy-start(f32[2,384]{1,0:T(2,128)S(1)} %slice.252) | copy-start | bytes 9220
  265.7 16.6 %copy-start.3 = (f32[8,240,384]{2,1,0:T(8,128)S(1)}, f32[8,240,384]{2,1,0:T(8,128)}, u32[]{:S(2)}) copy-start(f32[8,240,384]{2,1,0:T(8,128)} %maximum_add_fusion) | copy-start | bytes 8847364
  291.1 16.7 %collective-permute-start.31 = (bf16[2,432,384]{2,1,0:T(8,128)(2,1)}, bf16[2,432,384]{2,1,0:T(8,128)(2,1)}, u32[]{:S(2)}, u32[]{:S(2)}) collective-permute-start(bf16[2,432,384]{2,1,0:T(8,128)(2,1)} %dynamic-slice_convert_fusion.2), channel_id=1, source_target_pairs={{0,8},{4,12},{8,0},{12,4},{16,24},{20,28},{24,16},{28,20},{1,9},{5... | collective-permute-start | bytes 1990664 | tf_op jit(solution)/shard_map/ppermute | solution.py:377
  295.1 10.3 %collective-permute-start.30 = (f32[38,384]{1,0:T(8,128)}, f32[38,384]{1,0:T(8,128)}, u32[]{:S(2)}, u32[]{:S(2)}) collective-permute-start(f32[38,384]{1,0:T(8,128)} %concatenate.139), channel_id=1, source_target_pairs={{0,2},{2,0},{1,3},{3,1},{4,6},{6,4},{5,7},{7,5},{8,10},{10,8},{9,1... | collective-permute-start | bytes 175112 | tf_op jit(solution)/shard_map/ppermute | solution.py:368
  298.2 20.5 %collective-permute-start.29 = (bf16[384,1152]{1,0:T(8,128)(2,1)S(1)}, bf16[384,1152]{1,0:T(8,128)(2,1)S(1)}, u32[]{:S(2)}, u32[]{:S(2)}) collective-permute-start(bf16[384,1152]{1,0:T(8,128)(2,1)S(1)} %slice.368), channel_id=1, source_target_pairs={{0,2},{2,0},{1,3},{3,1},{4,6},{6,4},{5,7},{7,5},{8,10},{10,8},{9,1... | collective-permute-start | bytes 2654216 | tf_op jit(solution)/shard_map/ppermute | solution.py:368
  305.4 13.3 %copy-start.7 = (f32[768,1152]{1,0:T(8,128)S(1)}, f32[768,1152]{1,0:T(8,128)}, u32[]{:S(2)}) copy-start(f32[768,1152]{1,0:T(8,128)} %convolution_add_fusion) | copy-start | bytes 10616836
  319.7 5.8 %collective-permute-start.34 = (bf16[1,76,384]{2,1,0:T(8,128)(2,1)S(1)}, bf16[1,76,384]{2,1,0:T(8,128)(2,1)S(1)}, u32[]{:S(2)}, u32[]{:S(2)}) collective-permute-start(bf16[1,76,384]{2,1,0:T(8,128)(2,1)S(1)} %maximum_bitcast_fusion.2), channel_id=1, source_target_pairs={{0,16},{4,20},{8,24},{12,28},{16,0},{20,4},{24,8},{28,12},{1,17},{... | collective-permute-start | bytes 175112 | tf_op jit(solution)/shard_map/ppermute | solution.py:377
  325.5 4.9 %collective-permute-start.35 = (bf16[2,76,384]{2,1,0:T(8,128)(2,1)S(1)}, bf16[2,76,384]{2,1,0:T(8,128)(2,1)S(1)}, u32[]{:S(2)}, u32[]{:S(2)}) collective-permute-start(bf16[2,76,384]{2,1,0:T(8,128)(2,1)S(1)} %pad_maximum_fusion.13), channel_id=1, source_target_pairs={{0,8},{4,12},{8,0},{12,4},{16,24},{20,28},{24,16},{28,20},{1,9},{5... | collective-permute-start | bytes 350216 | tf_op jit(solution)/shard_map/ppermute | solution.py:377
  325.6 14.6 %collective-permute-start.39 = (bf16[1,432,384]{2,1,0:T(8,128)(2,1)S(1)}, bf16[1,432,384]{2,1,0:T(8,128)(2,1)S(1)}, u32[]{:S(2)}, u32[]{:S(2)}) collective-permute-start(bf16[1,432,384]{2,1,0:T(8,128)(2,1)S(1)} %dynamic-slice_convert_fusion.3), channel_id=1, source_target_pairs={{0,16},{4,20},{8,24},{12,28},{16,0},{20,4},{24,8},{28,12},{1,17},{... | collective-permute-start | bytes 995336 | tf_op jit(solution)/shard_map/ppermute | solution.py:377
  330.5 9.9 %collective-permute-start.36 = (bf16[4,76,384]{2,1,0:T(8,128)(2,1)S(1)}, bf16[4,76,384]{2,1,0:T(8,128)(2,1)S(1)}, u32[]{:S(2)}, u32[]{:S(2)}) collective-permute-start(bf16[4,76,384]{2,1,0:T(8,128)(2,1)S(1)} %pad_maximum_fusion.12), channel_id=1, source_target_pairs={{0,4},{4,0},{8,12},{12,8},{16,20},{20,16},{24,28},{28,24},{1,5},{5... | collective-permute-start | bytes 700424 | tf_op jit(solution)/shard_map/ppermute | solution.py:377
  332.1 8.7 %copy-start.15 = (bf16[128,384]{1,0:T(8,128)(2,1)S(1)}, bf16[128,384]{1,0:T(8,128)(2,1)}, u32[]{:S(2)}) copy-start(bf16[128,384]{1,0:T(8,128)(2,1)} %pad_maximum_fusion.15) | copy-start | bytes 294916
  340.3 19.9 %collective-permute-start.40 = (bf16[1,432,384]{2,1,0:T(8,128)(2,1)S(1)}, bf16[1,432,384]{2,1,0:T(8,128)(2,1)S(1)}, u32[]{:S(2)}, u32[]{:S(2)}) collective-permute-start(bf16[1,432,384]{2,1,0:T(8,128)(2,1)S(1)} %add_convert_fusion), channel_id=1, source_target_pairs={{0,16},{4,20},{8,24},{12,28},{16,0},{20,4},{24,8},{28,12},{1,17},{... | collective-permute-start | bytes 995336 | tf_op jit(solution)/shard_map/ppermute | solution.py:377
  340.7 20.5 %collective-permute-start.37 = (bf16[400,384]{1,0:T(8,128)(2,1)S(1)}, bf16[400,384]{1,0:T(8,128)(2,1)}, u32[]{:S(2)}, u32[]{:S(2)}) collective-permute-start(bf16[400,384]{1,0:T(8,128)(2,1)S(1)} %pad_maximum_fusion.11), channel_id=1, source_target_pairs={{0,1},{1,0},{2,3},{3,2},{4,5},{5,4},{6,7},{7,6},{8,9},{9,8},{10,11... | collective-permute-start | bytes 921608 | tf_op jit(solution)/shard_map/ppermute | solution.py:372
  340.8 44.4 %collective-permute-start.33 = (bf16[1024,384]{1,0:T(8,128)(2,1)}, bf16[1024,384]{1,0:T(8,128)(2,1)}, u32[]{:S(2)}, u32[]{:S(2)}) collective-permute-start(bf16[1024,384]{1,0:T(8,128)(2,1)} %get-tuple-element.125), channel_id=1, source_target_pairs={{0,2},{2,0},{1,3},{3,1},{4,6},{6,4},{5,7},{7,5},{8,10},{10,8},{9,1... | collective-permute-start | bytes 2359304 | tf_op jit(solution)/shard_map/ppermute | solution.py:368
  342.7 45.1 %collective-permute-start.32 = (bf16[1024,384]{1,0:T(8,128)(2,1)}, bf16[1024,384]{1,0:T(8,128)(2,1)}, u32[]{:S(2)}, u32[]{:S(2)}) collective-permute-start(bf16[1024,384]{1,0:T(8,128)(2,1)} %get-tuple-element.123), channel_id=1, source_target_pairs={{0,2},{2,0},{1,3},{3,1},{4,6},{6,4},{5,7},{7,5},{8,10},{10,8},{9,1... | collective-permute-start | bytes 2359304 | tf_op jit(solution)/shard_map/ppermute | solution.py:368
  361.2 19.9 %collective-permute-start.41 = (bf16[2,432,384]{2,1,0:T(8,128)(2,1)}, bf16[2,432,384]{2,1,0:T(8,128)(2,1)}, u32[]{:S(2)}, u32[]{:S(2)}) collective-permute-start(bf16[2,432,384]{2,1,0:T(8,128)(2,1)} %pad_maximum_fusion.9), channel_id=1, source_target_pairs={{0,8},{4,12},{8,0},{12,4},{16,24},{20,28},{24,16},{28,20},{1,9},{5... | collective-permute-start | bytes 1990664 | tf_op jit(solution)/shard_map/ppermute | solution.py:377
  375.3 9.3 %copy-start.22 = (bf16[16,384]{1,0:T(8,128)(2,1)S(1)}, bf16[16,384]{1,0:T(8,128)(2,1)}, u32[]{:S(2)}) copy-start(bf16[16,384]{1,0:T(8,128)(2,1)} %param.14) | copy-start | bytes 36868
  375.3 9.9 %copy-start.14 = (bf16[1024,384]{1,0:T(8,128)(2,1)S(1)}, bf16[1024,384]{1,0:T(8,128)(2,1)}, u32[]{:S(2)}) copy-start(bf16[1024,384]{1,0:T(8,128)(2,1)} %get-tuple-element.124) | copy-start | bytes 2359300
  375.3 9.3 %collective-permute-start.38 = (f32[16,384]{1,0:T(8,128)S(1)}, f32[16,384]{1,0:T(8,128)S(1)}, u32[]{:S(2)}, u32[]{:S(2)}) collective-permute-start(f32[16,384]{1,0:T(8,128)S(1)} %convolution_bitcast_fusion.1), channel_id=1, source_target_pairs={{0,2},{2,0},{1,3},{3,1},{4,6},{6,4},{5,7},{7,5},{8,10},{10,8},{9,1... | collective-permute-start | bytes 73736 | tf_op jit(solution)/shard_map/ppermute | solution.py:368
  383.4 45.7 %collective-permute-start.42 = (bf16[4,432,384]{2,1,0:T(8,128)(2,1)}, bf16[4,432,384]{2,1,0:T(8,128)(2,1)}, u32[]{:S(2)}, u32[]{:S(2)}) collective-permute-start(bf16[4,432,384]{2,1,0:T(8,128)(2,1)} %pad_maximum_fusion.5), channel_id=1, source_target_pairs={{0,4},{4,0},{8,12},{12,8},{16,20},{20,16},{24,28},{28,24},{1,5},{5... | collective-permute-start | bytes 3981320 | tf_op jit(solution)/shard_map/ppermute | solution.py:377
  (31 other events, 94.3 us)
Sparse Core Ops, SparseCore 0:
  345.2 81.2 all-reduce.1

commit v3 on v2

--- a/solution.py
+++ b/solution.py
@@ -54,12 +54,18 @@
     return jnp.concatenate([own_ref[...], oth_ref[...]], axis=1).astype(F32)
 
 
-def spread_rows(mod_ref, number):
-    rows = [
-        jnp.broadcast_to(mod_ref[latent, number : number + 1, :], (SEQ, D))
-        for latent in range(mod_ref.shape[0])
-    ]
-    return rows[0] if len(rows) == 1 else jnp.concatenate(rows, axis=0)
+def line(ref, lead, number):
+    return ref[lead, number : number + 1, :]
+
+
+def spread_rows(mods, number, per_tile):
+    own, oth = mods
+    rows = []
+    for latent in range(per_tile):
+        at = pl.ds(pl.program_id(0) * per_tile + latent, 1)
+        pair = jnp.concatenate([own[number, at, :], oth[number, at, :]], axis=1)
+        rows.append(jnp.broadcast_to(pair, (SEQ, D)))
+    return rows[0] if per_tile == 1 else jnp.concatenate(rows, axis=0)
 
 
 def store_sums(out_ref, number, values):
@@ -84,25 +90,48 @@
     return copies
 
 
-def grid_copies(pieces, weight, sem, first_is_row):
+def grid_copies(pieces, weight, sem):
     copies = []
     for number, piece in enumerate(pieces):
         row, col = number % 2, number // 2
         across, down = piece.shape[1], piece.shape[0]
-        top, left = (row, col) if first_is_row else (col, row)
         copies.append(
             pltpu.make_async_copy(
                 piece,
-                weight.at[pl.ds(top * down, down), pl.ds(left * across, across)],
+                weight.at[pl.ds(col * down, down), pl.ds(row * across, across)],
                 sem.at[number],
             )
         )
     return copies
 
 
+def relay_copies(place, pieces, weight, sem, first_is_row):
+    copies = []
+    for col in range(2):
+        whole, near, far = pieces[3 * col : 3 * col + 3]
+        down, across = whole.shape
+        size = near.shape[0]
+        for piece, row, start in (
+            (whole, 0, 0),
+            (near, 1, place * size),
+            (far, 1, (1 - place) * size),
+        ):
+            top, left = (row, col) if first_is_row else (col, row)
+            rows = pl.ds(pl.multiple_of(top * down + start, 16), piece.shape[0])
+            copies.append(
+                pltpu.make_async_copy(
+                    piece, weight.at[rows, pl.ds(left * across, across)], sem.at[len(copies)]
+                )
+            )
+    return copies
+
+
 def forward_kernel(
-    tok_own, tok_oth, mod, bias, w0, w1, w2, w3, first_ref, qkv_ref, att_ref, weight, sem
+    tok_own, tok_oth, mod_own, mod_oth, col_own, col_oth, w0, w1, w2, w3,
+    first_ref, qkv_ref, att_ref, weight, sem,
 ):
+    mod = (mod_own, mod_oth)
+
     @pl.when(pl.program_id(0) == 0)
     def _():
         copies = attend_copies((w0, w1, w2, w3), weight, sem)
@@ -112,9 +141,16 @@
             copy.wait()
 
     normal, _ = normalize(both(tok_own, tok_oth))
-    first = (normal * (1.0 + spread_rows(mod, 1)) + spread_rows(mod, 0)).astype(B16)
+    first = (normal * (1.0 + spread_rows(mod, 1, 1)) + spread_rows(mod, 0, 1)).astype(B16)
     first_ref[...] = first
-    qkv_ref[...] = (dot(first, weight[...]) + bias[...]).astype(B16)
+    blank = jnp.zeros((1, HALF), F32)
+    last = col_oth.shape[0] - 1
+    bias = jnp.concatenate(
+        [line(col_own, 0, 0), blank, line(col_own, 0, 1)]
+        + [line(col_oth, last, 0), blank, line(col_oth, last, 1)],
+        axis=1,
+    )
+    qkv_ref[...] = (dot(first, weight[...]) + bias).astype(B16)
     low = lax.broadcasted_iota(jnp.int32, (SEQ, PAIR), 1) < HEAD_DIM
     for col in range(2):
         for pair in range(HALF // PAIR):
@@ -133,8 +169,8 @@
 
 
 def middle_kernel(
-    tok_own, tok_oth, cot_own, cot_oth, att, mod, outbias, expbias, shrbias,
-    o0, o1, o2, o3, x0, x1, x2, x3, s0, s1, s2, s3,
+    place, tok_own, tok_oth, cot_own, cot_oth, att, mod_own, mod_oth, col_own, col_oth, row_own,
+    o0, o1, o2, o3, x0, x1, x2, x3, x4, x5, s0, s1, s2, s3, s4, s5,
     res_own, res_oth, second_ref, act_own, act_oth, dh_own, dh_oth, e_one_ref, e_two_ref,
     d_mid_ref, d_att_ref, mod_ref, sum_ref,
     w_out, w_exp, w_shr, sem_out, sem_exp, sem_shr,
@@ -142,28 +178,39 @@
     @pl.when(pl.program_id(0) == 0)
     def _():
         copies = (
-            grid_copies((o0, o1, o2, o3), w_out, sem_out, False)
-            + grid_copies((x0, x1, x2, x3), w_exp, sem_exp, True)
-            + grid_copies((s0, s1, s2, s3), w_shr, sem_shr, False)
+            grid_copies((o0, o1, o2, o3), w_out, sem_out)
+            + relay_copies(place[0], (x0, x1, x2, x3, x4, x5), w_exp, sem_exp, True)
+            + relay_copies(place[0], (s0, s1, s2, s3, s4, s5), w_shr, sem_shr, False)
         )
         for copy in copies:
             copy.start()
         for copy in copies:
             copy.wait()
 
-    branch_one = dot(att[...], w_out[...]) + outbias[...]
-    middle = both(tok_own, tok_oth) + spread_rows(mod, 2) * branch_one
+    per_tile = mod_ref.shape[0]
+    last = mod_oth.shape[0] - 1
+    rows = functools.partial(spread_rows, (mod_own, mod_oth), per_tile=per_tile)
+    outbias = jnp.concatenate([line(row_own, 0, 0), line(mod_oth, last, 0)], axis=1)
+    shrbias = jnp.concatenate([line(row_own, 0, 1), line(mod_oth, last, 1)], axis=1)
+
+    branch_one = dot(att[...], w_out[...]) + outbias
+    middle = both(tok_own, tok_oth) + rows(2) * branch_one
     normal, inverse = normalize(middle)
-    second = (normal * (1.0 + spread_rows(mod, 4)) + spread_rows(mod, 3)).astype(B16)
+    second = (normal * (1.0 + rows(4)) + rows(3)).astype(B16)
     second_ref[...] = second
     upstream = both(cot_own, cot_oth)
-    e_two = (spread_rows(mod, 5) * upstream).astype(B16)
+    e_two = (rows(5) * upstream).astype(B16)
     e_two_ref[...] = e_two
-    branch_two = shrbias[...]
+    branch_two = shrbias
     d_second = 0.0
     for part in range(FF // D):
         at = part * D
-        hidden = dot(second, w_exp[:, at : at + D]) + expbias[:, at : at + D]
+        owner, lead = (col_own, 0) if 2 * at < FF else (col_oth, col_oth.shape[0] - 1)
+        number = 2 + 2 * (part % (FF // D // 2))
+        expbias = jnp.concatenate(
+            [line(owner, lead, number), line(owner, lead, number + 1)], axis=1
+        )
+        hidden = dot(second, w_exp[:, at : at + D]) + expbias
         square = hidden * hidden
         bend = jnp.tanh(hidden * (ROOT + (ROOT * CUBE) * square))
         share = 0.5 + 0.5 * bend
@@ -179,16 +226,16 @@
         sum_ref[0, :, 2 * D + at : 2 * D + at + D] = jnp.sum(
             d_hidden.astype(F32), axis=0, keepdims=True
         )
-    result = (middle + spread_rows(mod, 5) * branch_two).astype(B16)
+    result = (middle + rows(5) * branch_two).astype(B16)
     res_own[...] = result[:, :HALF]
     res_oth[...] = result[:, HALF:]
     store_sums(mod_ref, 3, upstream * branch_two)
     store_sums(mod_ref, 1, d_second)
     store_sums(mod_ref, 2, d_second * normal)
-    d_middle = upstream + norm_grad(d_second * (1.0 + spread_rows(mod, 4)), normal, inverse)
+    d_middle = upstream + norm_grad(d_second * (1.0 + rows(4)), normal, inverse)
     d_mid_ref[...] = d_middle
     store_sums(mod_ref, 0, d_middle * branch_one)
-    e_one = (spread_rows(mod, 2) * d_middle).astype(B16)
+    e_one = (rows(2) * d_middle).astype(B16)
     e_one_ref[...] = e_one
     d_att_ref[...] = dot_nt(e_one, w_out[...]).astype(B16)
     sum_ref[0, :, :D] = jnp.sum(e_one.astype(F32), axis=0, keepdims=True)
@@ -196,9 +243,11 @@
 
 
 def backward_kernel(
-    tok_own, tok_oth, mod, qkv, d_att, d_mid, w0, w1, w2, w3,
+    tok_own, tok_oth, mod_own, mod_oth, qkv, d_att, d_mid, w0, w1, w2, w3,
     dqkv_own, dqkv_oth, grad_own, grad_oth, mod_ref, sum_ref, weight, sem,
 ):
+    mod = (mod_own, mod_oth)
+
     @pl.when(pl.program_id(0) == 0)
     def _():
         copies = attend_copies((w0, w1, w2, w3), weight, sem)
@@ -241,7 +290,7 @@
     store_sums(mod_ref, 0, d_first)
     store_sums(mod_ref, 1, d_first * normal)
     grad = (
-        d_mid[...] + norm_grad(d_first * (1.0 + spread_rows(mod, 1)), normal, inverse)
+        d_mid[...] + norm_grad(d_first * (1.0 + spread_rows(mod, 1, 1)), normal, inverse)
     ).astype(B16)
     grad_own[...] = grad[:, :HALF]
     grad_oth[...] = grad[:, HALF:]
@@ -255,8 +304,8 @@
     return pl.BlockSpec((count, rows, width), lambda step: (step, 0, 0))
 
 
-def fixed(width):
-    return pl.BlockSpec((1, width), lambda step: (0, 0))
+def fixed(values):
+    return pl.BlockSpec(values.shape, lambda step: (0,) * values.ndim)
 
 
 def anywhere(count):
@@ -269,13 +318,13 @@
     )
 
 
-def call_forward(tok_own, tok_oth, modulation, bias, pieces):
+def call_forward(tok_own, tok_oth, vectors, pieces):
     count = tok_own.shape[0]
     latents = count // SEQ
     return pl.pallas_call(
         forward_kernel,
         grid=(latents,),
-        in_specs=[tiles(SEQ, HALF)] * 2 + [stacked(1, 6, D), fixed(2 * SIDE)] + anywhere(4),
+        in_specs=[tiles(SEQ, HALF)] * 2 + [fixed(values) for values in vectors] + anywhere(4),
         out_specs=[tiles(SEQ, D), tiles(SEQ, 2 * SIDE), tiles(SEQ, D)],
         out_shape=[
             jax.ShapeDtypeStruct((count, D), B16),
@@ -288,10 +337,10 @@
             flops=14 * 10**9, bytes_accessed=16 * 10**6, transcendentals=count * SEQ * 12
         ),
         name="forward",
-    )(tok_own, tok_oth, modulation, bias, *pieces)
-
-
-def call_middle(tok, cot, att, modulation, biases, out_pieces, exp_pieces, shr_pieces):
+    )(tok_own, tok_oth, *vectors, *pieces)
+
+
+def call_middle(place, tok, cot, att, vectors, out_pieces, exp_pieces, shr_pieces):
     count = att.shape[0]
     latents = count // SEQ
     per_tile = PER_TILE if latents % PER_TILE == 0 else 1
@@ -305,10 +354,12 @@
     return pl.pallas_call(
         middle_kernel,
         grid=(steps,),
-        in_specs=halves
+        in_specs=[pl.BlockSpec(memory_space=pltpu.SMEM)]
         + halves
-        + [tiles(rows, D), stacked(per_tile, 6, D), fixed(D), fixed(FF), fixed(D)]
-        + anywhere(12),
+        + halves
+        + [tiles(rows, D)]
+        + [fixed(values) for values in vectors]
+        + anywhere(16),
         out_specs=halves
         + [tiles(rows, D)]
         + [tiles(rows, FF // 2)] * 4
@@ -326,25 +377,26 @@
             pltpu.VMEM((D, FF), B16),
             pltpu.VMEM((FF, D), B16),
             pltpu.SemaphoreType.DMA((4,)),
-            pltpu.SemaphoreType.DMA((4,)),
-            pltpu.SemaphoreType.DMA((4,)),
+            pltpu.SemaphoreType.DMA((6,)),
+            pltpu.SemaphoreType.DMA((6,)),
         ],
         compiler_params=params(),
         cost_estimate=pl.CostEstimate(
             flops=30 * 10**9, bytes_accessed=50 * 10**6, transcendentals=count * FF
         ),
         name="middle",
-    )(*tok, *cot, att, modulation, *biases, *out_pieces, *exp_pieces, *shr_pieces)
-
-
-def call_backward(tok, modulation, qkv, d_att, d_mid, pieces):
+    )(place, *tok, *cot, att, *vectors, *out_pieces, *exp_pieces, *shr_pieces)
+
+
+def call_backward(tok, vectors, qkv, d_att, d_mid, pieces):
     count = d_att.shape[0]
     latents = count // SEQ
     return pl.pallas_call(
         backward_kernel,
         grid=(latents,),
         in_specs=[tiles(SEQ, HALF)] * 2
-        + [stacked(1, 6, D), tiles(SEQ, 2 * SIDE), tiles(SEQ, D), tiles(SEQ, D)]
+        + [fixed(values) for values in vectors]
+        + [tiles(SEQ, 2 * SIDE), tiles(SEQ, D), tiles(SEQ, D)]
         + anywhere(4),
         out_specs=[tiles(SEQ, SIDE)] * 2
         + [tiles(SEQ, HALF)] * 2
@@ -361,7 +413,7 @@
             flops=25 * 10**9, bytes_accessed=20 * 10**6, transcendentals=count * SEQ * 12
         ),
         name="backward",
-    )(*tok, modulation, qkv, d_att, d_mid, *pieces)
+    )(*tok, *vectors, qkv, d_att, d_mid, *pieces)
 
 
 def swap_row(values):
@@ -393,10 +445,10 @@
     )
 
 
-def pick(values, place):
-    size = values.shape[0] // 2
-    kept = lax.dynamic_slice_in_dim(values, place * size, size, 0)
-    sent = lax.dynamic_slice_in_dim(values, (1 - place) * size, size, 0)
+def pick(values, place, axis=0):
+    size = values.shape[axis] // 2
+    kept = lax.dynamic_slice_in_dim(values, place * size, size, axis)
+    sent = lax.dynamic_slice_in_dim(values, (1 - place) * size, size, axis)
     return kept, sent
 
 
@@ -424,36 +476,51 @@
     return values
 
 
-def sum_order():
+def near_place():
+    return jnp.full((1,), x_place(), jnp.int32)
+
+
+def sum_place():
     me, mine = lax.axis_index("dp"), 0
     for distance in distances():
         mine = mine * 2 + (me // distance) % 2
     return jnp.full((1,), mine, jnp.int32)
 
 
-def order_grid_kernel(mine, values, shr_out, out_out, exp_out):
+def order_grid_kernel(mine, near, far, shr_out, out_out, exp_out):
     shr_rows, out_rows, exp_rows = shr_out.shape[1], out_out.shape[1], exp_out.shape[1]
-    for block in range(values.shape[0]):
-        place = mine[0] ^ block
-        shr_out[place] = values[block, :shr_rows].astype(F32)
-        out_out[place] = values[block, shr_rows : shr_rows + out_rows].astype(F32)
-        for part in range(exp_out.shape[2] // HALF):
-            at = shr_rows + out_rows + part * exp_rows
-            exp_out[place, :, part * HALF : (part + 1) * HALF] = values[
-                block, at : at + exp_rows
-            ].astype(F32)
-
-
-def order(kernel, values, shapes):
+    count = near.shape[0]
+    for values, place in ((near, mine[0]), (far, 1 - mine[0])):
+        for block in range(count):
+            into = place * count + block
+            shr_out[into] = values[block, :shr_rows].astype(F32)
+            out_out[into] = values[block, shr_rows : shr_rows + out_rows].astype(F32)
+            for part in range(exp_out.shape[2] // HALF):
+                at = shr_rows + out_rows + part * exp_rows
+                exp_out[into, :, part * HALF : (part + 1) * HALF] = values[
+                    block, at : at + exp_rows
+                ].astype(F32)
+
+
+def order_attend_kernel(mine, near, far, out):
+    count = near.shape[0]
+    for number, values in enumerate((near, far)):
+        for block in range(count):
+            place = mine[0] ^ (number * count + block)
+            for kind in range(out.shape[0]):
+                out[kind, place] = values[block, :, kind * HALF : (kind + 1) * HALF].astype(F32)
+
+
+def order(kernel, place, values, shapes):
     whole = [pl.BlockSpec(memory_space=pltpu.VMEM)]
     return pl.pallas_call(
         kernel,
-        in_specs=[pl.BlockSpec(memory_space=pltpu.SMEM)] + whole,
+        in_specs=[pl.BlockSpec(memory_space=pltpu.SMEM)] + whole * len(values),
         out_specs=whole * len(shapes),
         out_shape=[jax.ShapeDtypeStruct(shape, F32) for shape in shapes],
         compiler_params=pltpu.CompilerParams(vmem_limit_bytes=VMEM_BYTES),
         name="order",
-    )(sum_order(), values)
+    )(place, *values)
 
 
 def shards(
@@ -467,31 +534,21 @@
     tok_oth = swap_row(sent)
     tok = (tok_own, tok_oth)
 
-    raw_condition = condition.astype(F32)
+    raw_condition = after(condition, sent).astype(F32)
     act_cond = jax.nn.silu(raw_condition).astype(B16)
-    mod_terms = jnp.einsum("ld,kde->lke", act_cond, adaptive, preferred_element_type=F32)
-    kept, sent = pick(mod_terms, col)
-    group = kept.shape[0]
+    mod_terms = jnp.einsum("ld,kde->kle", act_cond, adaptive, preferred_element_type=F32)
+    kept, sent = pick(mod_terms, col, 1)
+    group = kept.shape[1]
     latents = group // 2
-    col_bias = jnp.concatenate([attbias.reshape(-1), expbias]).astype(F32).reshape(-1, 1, HALF)
-    got = swap_col(
-        jnp.concatenate([sent.reshape(-1, HALF), col_bias.reshape(-1, HALF)], axis=0)
-    )
-    mod_rows = kept + got[: 6 * group].reshape(group, 6, HALF) + adabias.astype(F32)
-    col_other = got[6 * group :]
-    kept, sent = pick(mod_rows, row)
-    row_bias = jnp.stack([outbias, shrbias]).astype(F32)
-    got = swap_row(jnp.concatenate([sent.reshape(-1, HALF), row_bias], axis=0))
-    modulation = jnp.concatenate([kept, got[: 6 * latents].reshape(latents, 6, HALF)], axis=2)
-    row_other = got[6 * latents :]
-    col_bias = col_bias.reshape(-1, HALF)
-    blank = jnp.zeros((HALF,), F32)
-    bias = jnp.concatenate(
-        [piece for part in (col_bias, col_other) for piece in (part[0], blank, part[1])]
-    )[None]
-    exp_bias = jnp.concatenate([col_bias[2:], col_other[2:]], axis=0).reshape(1, FF)
-    out_bias = jnp.concatenate([row_bias[:1], row_other[:1]], axis=1)
-    shr_bias = jnp.concatenate([row_bias[1:], row_other[1:]], axis=1)
+    col_own = jnp.concatenate([attbias, expbias.reshape(-1, HALF)], axis=0).astype(F32)
+    col_own = jnp.pad(col_own, ((0, group - col_own.shape[0]), (0, 0)))[None]
+    col_oth = swap_col(jnp.concatenate([sent, col_own], axis=0))
+    mod_rows = kept + col_oth[:6] + adabias.astype(F32)[:, None]
+    mod_own, sent = pick(mod_rows, row, 1)
+    row_own = jnp.stack([outbias, shrbias]).astype(F32)
+    row_own = jnp.pad(row_own, ((0, latents - 2), (0, 0)))[None]
+    mod_oth = swap_row(jnp.concatenate([sent, row_own], axis=0))
+    mods = (mod_own, mod_oth)
 
     def pieces(values, over):
         return values, over, swap_col(values), swap_col(over)
@@ -499,37 +556,36 @@
     def near(values):
         return pick(values, x_place())[0]
 
-    def relayed(half):
-        return in_order(x_place(), half, swap_dp(half, 1))
-
-    flat_attend = attend.reshape(-1, attend.shape[2])
-    att_half = swap_row(after(near(flat_attend), tok_oth, got))
-    att_half, exp_half = lax.optimization_barrier((att_half, near(expand)))
-    exp_half = swap_row(exp_half)
-    attend_pieces = pieces(attend, relayed(att_half).reshape(attend.shape))
-    cond_all = gather_dp(act_cond)
-    *attend_pieces, exp_half, shr_half, outproj, cond_all = lax.optimization_barrier(
-        (*attend_pieces, exp_half, near(shrink), outproj, cond_all)
-    )
-    shr_half, out_over = swap_row(shr_half), swap_row(outproj)
-    exp_far = swap_dp(exp_half, 1)
     cot_own, cot_sent = pick(cotangent, row)
-    first, qkv, attended = call_forward(tok_own, tok_oth, modulation, bias, attend_pieces)
-    attended, exp_half, exp_far, shr_half, out_over, cot_sent = lax.optimization_barrier(
-        (attended, exp_half, exp_far, shr_half, out_over, cot_sent)
-    )
-    cot_oth = swap_row(cot_sent)
-    shr_far = swap_dp(shr_half, 1)
-    exp_over = in_order(x_place(), exp_half, exp_far)
+    attend, _, _, exp_near, shr_near, cot_sent = lax.optimization_barrier(
+        (attend, tok_oth, mod_oth, near(expand), near(shrink), cot_sent)
+    )
+    attend_pieces = pieces(attend, swap_row(attend))
+    *attend_pieces, exp_near, shr_near = lax.optimization_barrier(
+        (*attend_pieces, exp_near, shr_near)
+    )
+    exp_near, shr_near = swap_row(exp_near), swap_row(shr_near)
+    first, qkv, attended = call_forward(
+        tok_own, tok_oth, (*mods, col_own, col_oth), attend_pieces
+    )
+    attended, exp_near, shr_near, outproj, cot_sent, act_late = lax.optimization_barrier(
+        (attended, exp_near, shr_near, outproj, cot_sent, act_cond)
+    )
+    cot_oth, out_over = swap_row(cot_sent), swap_row(outproj)
+    exp_far, shr_far = swap_dp(exp_near, 1), swap_dp(shr_near, 1)
+    early = [swap_col(values) for values in (expand, shrink, exp_near, shr_near)]
+    cond_all = gather_dp(act_late)
+    cot_oth, out_over, exp_far, shr_far, cond_all, *early = lax.optimization_barrier(
+        (cot_oth, out_over, exp_far, shr_far, cond_all, *early)
+    )
+    exp_pieces = (expand, exp_near, exp_far, early[0], early[2], swap_col(exp_far))
+    shr_pieces = (shrink, shr_near, shr_far, early[1], early[3], swap_col(shr_far))
     out_pieces = pieces(outproj, out_over)
-    exp_pieces = pieces(expand, exp_over)
-    shr_over = in_order(x_place(), shr_half, shr_far)
-    shr_pieces = pieces(shrink, shr_over)
     (
         res_own, res_oth, second, act_own, act_oth, dh_own, dh_oth, e_one, e_two,
         d_middle, d_attended, mod_late, sums_late,
     ) = call_middle(
-        tok, (cot_own, cot_oth), attended, modulation, (out_bias, exp_bias, shr_bias),
+        near_place(), tok, (cot_own, cot_oth), attended, (*mods, col_own, col_oth, row_own),
         out_pieces, exp_pieces, shr_pieces,
     )
     att_own, att_oth = halves(attended, 1)
@@ -549,38 +605,40 @@
     near_step, *far_steps = distances()
     size = lax.axis_size("dp")
     shr_mine, shr_theirs = [
-        jnp.concatenate(
-            [part.reshape(size, -1, HALF) for part in parts], axis=1
-        )
+        jnp.concatenate([part.reshape(size, -1, HALF) for part in parts], axis=1)
         for parts in zip(halves(shr_total, 1), halves(out_total, 1))
     ]
-    shr_part = shr_mine + swap_row(shr_theirs.astype(B16)).astype(F32)
-    exp_part = scatter_stage(exp_total.reshape(2, HALF, -1), near_step, 1)
+    shr_got = swap_row(shr_theirs.astype(B16))
+    exp_kept, exp_sent = pick(exp_total.reshape(2, HALF, -1), x_place(), 1)
+    exp_got = swap_dp(exp_sent.astype(B16), near_step)
 
     dqkv_own, dqkv_oth, grad_own, grad_oth, mod_early, sums_early = call_backward(
-        tok, modulation, qkv, d_attended, d_middle, attend_pieces
-    )
-    dqkv_own, dqkv_oth, shr_part, exp_part = lax.optimization_barrier(
-        (dqkv_own, dqkv_oth, shr_part, exp_part)
-    )
-    exp_part = exp_part[0] + swap_row(exp_part[1].astype(B16)).astype(F32)
-    shr_part = scatter_stage(shr_part, near_step)
+        tok, mods, qkv, d_attended, d_middle, attend_pieces
+    )
+    dqkv_own, dqkv_oth, shr_got, exp_got = lax.optimization_barrier(
+        (dqkv_own, dqkv_oth, shr_got, exp_got)
+    )
     att_got = swap_col(dot_tn(first, dqkv_oth).astype(B16)).astype(F32)
+    exp_part = exp_kept + exp_got.astype(F32)
+    shr_kept, shr_sent = pick(shr_mine + shr_got.astype(F32), x_place())
+    exp_got = swap_row(exp_part[1].astype(B16))
+    shr_got = swap_dp(shr_sent.astype(B16), near_step)
     att_total = dot_tn(first, dqkv_own) + att_got
-    att_total, shr_part, exp_part, mod_early, res_oth = lax.optimization_barrier(
-        (att_total, shr_part, exp_part, mod_early, res_oth)
+    att_total, exp_got, shr_got, mod_early, grad_oth, res_oth = lax.optimization_barrier(
+        (att_total, exp_got, shr_got, mod_early, grad_oth, res_oth)
     )
     att_mine, att_theirs = halves(att_total, 0)
     att_part = att_mine + swap_row(att_theirs.astype(B16)).astype(F32)
+    exp_part = (exp_part[0] + exp_got.astype(F32)).astype(B16)
     exp_part = exp_part.reshape(size // 2, HALF // size, -1)
     grid_part = jnp.concatenate(
-        [shr_part]
-        + [
-            exp_part[:, :, at : at + HALF] for at in range(0, exp_part.shape[2], HALF)
-        ],
+        [(shr_kept + shr_got.astype(F32)).astype(B16)]
+        + [exp_part[:, :, at : at + HALF] for at in range(0, exp_part.shape[2], HALF)],
         axis=1,
     )
-    grid_part = scatter_stage(grid_part, far_steps[0])
+    grid_part = lax.psum(
+        grid_part, "dp", axis_index_groups=[list(range(place, size, 2)) for place in range(2)]
+    )
 
     d_modulation = jnp.concatenate([mod_early, mod_late], axis=1).astype(B16).astype(F32)
     sums_late = jnp.sum(sums_late, axis=(0, 1))
@@ -600,14 +658,32 @@
     low = (sums - high.astype(F32)).astype(B16)
     width = block.shape[0] + 2 * sums.shape[0]
     packed = jnp.concatenate([block, high, low], axis=0)[None]
-    att_part, packed, grid_part, grad_oth, res_oth = lax.optimization_barrier(
-        (att_part, packed, grid_part, grad_oth, res_oth)
-    )
-    attend_grad = lax.psum(att_part.astype(B16), "dp").astype(F32)
-    attend_grad = attend_grad.reshape(HALF, 3, HALF).transpose(1, 0, 2)
+    att_part, packed, grad_oth, res_oth = lax.optimization_barrier(
+        (att_part, packed, grad_oth, res_oth)
+    )
     packed_all = gather_dp(packed)
-    for distance in far_steps[1:]:
-        grid_part = scatter_stage(grid_part, distance)
+    att_part = att_part.reshape(size, HALF // size, -1)
+    for distance in distances():
+        att_part = scatter_stage(att_part, distance)
+    att_part, grid_part = lax.optimization_barrier((att_part.astype(B16), grid_part))
+    for distance in reversed(far_steps):
+        att_part = jnp.concatenate([att_part, swap_dp(att_part, distance)], axis=0)
+    exp_width = expand.shape[1]
+    shrink_grad, outproj_grad, expand_grad = order(
+        order_grid_kernel,
+        near_place(),
+        (grid_part, swap_dp(grid_part, near_step)),
+        [(size, depth // size, HALF), (size, HALF // size, HALF), (size, HALF // size, exp_width)],
+    )
+    shrink_grad, outproj_grad = [part.reshape(-1, HALF) for part in (shrink_grad, outproj_grad)]
+    expand_grad = expand_grad.reshape(HALF, exp_width)
+    (attend_grad,) = order(
+        order_attend_kernel,
+        sum_place(),
+        (att_part, swap_dp(att_part, near_step)),
+        [(3, size, HALF // size, HALF)],
+    )
+    attend_grad = attend_grad.reshape(3, HALF, HALF)
     block_all = packed_all[:, : block.shape[0]].reshape(-1, HALF)
     both_sums = jnp.sum(packed_all[:, block.shape[0] :].astype(F32), axis=0)
     sums = both_sums[: sums.shape[0]] + both_sums[sums.shape[0] :]
@@ -625,14 +701,6 @@
 
     result = in_order(row, res_own, swap_row(res_oth))
     input_gradient = in_order(row, grad_own, swap_row(grad_oth))
-    exp_width = expand.shape[1]
-    shrink_grad, outproj_grad, expand_grad = order(
-        order_grid_kernel,
-        gather_dp(grid_part.astype(B16)),
-        [(size, depth // size, HALF), (size, HALF // size, HALF), (size, HALF // size, exp_width)],
-    )
-    shrink_grad, outproj_grad = [part.reshape(-1, HALF) for part in (shrink_grad, outproj_grad)]
-    expand_grad = expand_grad.reshape(HALF, exp_width)
     mod_all = jnp.concatenate([block_all, other_all], axis=0).reshape(-1, 6, HALF)
     cond_mine, cond_theirs = pick(
         cond_all.reshape(-1, 2 * group, HALF).transpose(1, 0, 2), col

time: 451 us -> 422 us (0.936)
  other arithmetic: 40.3 us -> 23.3 us
  local copies, waits for them, and re-layouts: 51 us -> 37.1 us
  waiting for transfers between devices: 157 us -> 169 us
  Pallas kernels: 102 us -> 93.6 us
    psum x1, waiting for transfers between devices: 36.1 us -> 12.1 us  [shards(): lax.psum(grid_part, 'dp', axis_index_groups=[list(range(place, size, 2))...]
    ppermute x16 -> x17, waiting for transfers between devices: 51.4 us -> 67.1 us  [swap_dp(): lax.ppermute(values, 'dp', [(place, place ^ distance) for place in range(...]
    ppermute x14, waiting for transfers between devices: 67.9 us -> 83.6 us  [swap_row(): return lax.ppermute(values, 'row', SWAP)]
    pallas_call x1, Pallas kernels: 49.2 us -> 38.4 us  [call_middle(): pl.pallas_call(middle_kernel, grid=(steps,), in_specs=[pl.BlockSpec(memor...]
    concatenate x8 -> x5, other arithmetic: 6.8 us -> 1.79 us  [gather_dp(): values = jnp.concatenate([values, swap_dp(values, distance)], axis=0)]
    select_n x6 -> x2, other arithmetic: 6.91 us -> 1.93 us  [in_order(): jnp.where(place == 0, mine, theirs)]
    ppermute x13 -> x15, waiting for transfers between devices: 1.13 us -> 5.79 us  [swap_col(): return lax.ppermute(values, 'col', SWAP)]
    ppermute x16 -> x17, starting transfers between devices: 21.2 us -> 24 us  [swap_dp(): lax.ppermute(values, 'dp', [(place, place ^ distance) for place in range(...]
  transfers between devices with their start and end apart: 44 -> 47, of which waited for: 18 -> 23; matrix products, arithmetic and copies ran while one was open for 19% -> 14% of each run, Pallas kernels for 11% -> 12%
where the time goes in v3:
time: 422 us; the launch traced here: 417 us
  waiting for transfers between devices  169 us (40%)
  Pallas kernels  93.6 us (22%)
  starting transfers between devices  42.6 us (10%)
  local copies, waits for them, and re-layouts  37.1 us (9%)
  matrix products  36.1 us (9%)
  other arithmetic  23.3 us (6%)
  between operations  15.4 us (4%)
    ppermute x14, waiting for transfers between devices, swap_row(): return lax.ppermute(values, 'row', SWAP)  83.6 us
    ppermute x17, waiting for transfers between devices, swap_dp(): lax.ppermute(values, 'dp', [(place, place ^ distance) for place in range(...  67.1 us
    pallas_call x1, Pallas kernels, call_middle(): pl.pallas_call(middle_kernel, grid=(steps,), in_specs=[pl.BlockSpec(memor...  38.4 us
    dot_general x8, matrix products, dot_tn(): lax.dot_general(left, right, (((0,), (0,)), ((), ())), preferred_element_...  32.7 us
    pallas_call x1, Pallas kernels, call_backward(): pl.pallas_call(backward_kernel, grid=(latents,), in_specs=[tiles(SEQ, HAL...  31.7 us
    ppermute x17, starting transfers between devices, swap_dp(): lax.ppermute(values, 'dp', [(place, place ^ distance) for place in range(...  24 us
    unnamed x139, local copies, waits for them, and re-layouts  18.9 us
    pallas_call x1, Pallas kernels, call_forward(): pl.pallas_call(forward_kernel, grid=(latents,), in_specs=[tiles(SEQ, HALF...  16.7 us
  transfers between devices with their start and end apart: 47, of which 23 were waited for; matrix products, arithmetic and copies ran while one was open for 14% of the time, Pallas kernels for 12%

profile of v3, /device:TPU:0, one launch (start us, length us, event | category | flops | bytes accessed | tf_op | source)
XLA Modules:
  0.0 416.6 jit_solution(7700028892096938664)
XLA Ops:
  7.3 2.8 constant_dynamic-slice_fusion.6
  10.1 3.0 collective-permute-start
  14.3 1.9 constant_dynamic-slice_fusion.2
  16.2 1.3 constant_dynamic-slice_fusion.5
  20.5 11.3 %collective-permute-done.2.mod_oth = f32[7,4,384]{2,1,0:T(4,128)S(1)} collective-permute-done((f32[7,4,384]{2,1,0:T(4,128)S(1)}, f32[7,4,384]{2,1,0:T(4,128)S(1)}, u32[]{:S(2)}, u32[]{:S(2)}) %collective-permute-start.2) | collective-permute-done | bytes 43040 | tf_op jit(solution)/shard_map/ppermute | solution.py:420
  32.4 1.7 collective-permute-start.3
  34.2 19.2 %collective-permute-done.3.w1 = bf16[3,384,384]{2,1,0:T(8,128)(2,1)S(1)} collective-permute-done((bf16[3,384,384]{2,1,0:T(8,128)(2,1)S(1)}, bf16[3,384,384]{2,1,0:T(8,128)(2,1)S(1)}, u32[]{:S(2)}, u32[]{:S(2)}) %collective-permute-start.3) | collective-permute-done | bytes 884768 | tf_op jit(solution)/shard_map/ppermute | solution.py:420
  53.9 3.1 collective-permute-done.5.w3
  57.0 1.4 collective-permute-start.6
  59.1 16.7 %forward.1 = (bf16[1024,768]{1,0:T(8,128)(2,1)}, bf16[1024,2304]{1,0:T(8,128)(2,1)}, bf16[1024,768]{1,0:T(8,128)(2,1)}) custom-call(bf16[1024,384]{1,0:T(8,128)(2,1)} %get-tuple-element.192.tok_own, bf16[1024,384]{1,0:T(8,128)(2,1)} %collective-permute-done.tok_oth, f32[6,4,384]{2,1,0:T(4,128)} %get-tuple-element.200.mod_own, f32[7,4,384]{2,1,0:T(4,128)} %copy-done.51, ...), custom_call_target="tpu_custom_call" | custom-call | flops 14000000000 | bytes 16000000 | tf_op jit(solution)/shard_map/forward/pallas_call | solution.py:324
  75.8 9.5 %collective-permute-done.7.s1 = bf16[768,384]{1,0:T(8,128)(2,1)} collective-permute-done((bf16[768,384]{1,0:T(8,128)(2,1)S(1)}, bf16[768,384]{1,0:T(8,128)(2,1)}, u32[]{:S(2)}, u32[]{:S(2)}) %collective-permute-start.7) | collective-permute-done | bytes 589856 | tf_op jit(solution)/shard_map/ppermute | solution.py:420
  85.3 2.5 collective-permute-start.12
  87.8 1.5 collective-permute-start.8
  89.9 1.5 collective-permute-start.13
  91.5 2.3 collective-permute-done.13
  93.8 1.4 collective-permute-start.14
  95.8 2.6 collective-permute-done.14
  98.5 1.4 collective-permute-start.11
  99.9 12.8 %collective-permute-done.9.o1 = bf16[384,384]{1,0:T(8,128)(2,1)S(1)} collective-permute-done((bf16[384,384]{1,0:T(8,128)(2,1)}, bf16[384,384]{1,0:T(8,128)(2,1)S(1)}, u32[]{:S(2)}, u32[]{:S(2)}) %collective-permute-start.9) | collective-permute-done | bytes 294944 | tf_op jit(solution)/shard_map/ppermute | solution.py:420
  112.7 8.2 %collective-permute-done.11.s2 = bf16[768,384]{1,0:T(8,128)(2,1)S(1)} collective-permute-done((bf16[768,384]{1,0:T(8,128)(2,1)}, bf16[768,384]{1,0:T(8,128)(2,1)S(1)}, u32[]{:S(2)}, u32[]{:S(2)}) %collective-permute-start.11) | collective-permute-done | bytes 589856 | tf_op jit(solution)/shard_map/ppermute | solution.py:429
  123.0 2.0 collective-permute-done.19.o2
  126.8 38.4 %middle.1 = (bf16[1024,384]{1,0:T(8,128)(2,1)}, bf16[1024,384]{1,0:T(8,128)(2,1)}, bf16[1024,768]{1,0:T(8,128)(2,1)}, bf16[1024,1536]{1,0:T(8,128)(2,1)}, bf16[1...) custom-call(s32[1]{0:T(128)} %bitcast.place.mine, ...), custom_call_target="tpu_custom_call" | custom-call | flops 30000001024 | bytes 50000000 | tf_op jit(solution)/shard_map/middle/pallas_call | solution.py:354
  165.2 6.6 %convolution_convert_fusion = bf16[768,1536]{1,0:T(8,128)(2,1)} fusion(bf16[1024,768]{1,0:T(8,128)(2,1)} %get-tuple-element.118, bf16[1024,1536]{1,0:T(8,128)(2,1)} %get-tuple-element.120), kind=kOutput, calls=%fused_computation.3 | convolution fusion | flops 2417098752 | bytes 7077888 | tf_op jit(solution)/shard_map/dot_general | solution.py:37
  174.2 2.9 convolution_convert_fusion.1
  177.2 1.8 pad_maximum_fusion
  180.2 5.5 %convert_add_fusion = f32[768,1536]{1,0:T(8,128)S(1)} fusion(bf16[768,1536]{1,0:T(8,128)(2,1)} %collective-permute-done.24, bf16[1024,768]{1,0:T(8,128)(2,1)S(1)} %copy-done.6, bf16[1024,1536]{1,0:T(8,128)(2,1)} %get-tuple-element.119), kind=kOutput, calls=%fused_computation | convolution fusion | flops 2418278400 | bytes 11796480 | tf_op jit(solution)/shard_map/dot_general | solution.py:37
  185.7 2.5 convolution_add_fusion.1
  188.2 1.6 copy-done.58
  190.3 4.5 %convert_add_fusion.1 = f32[1536,768]{1,0:T(8,128)S(1)} fusion(bf16[1024,1536]{1,0:T(8,128)(2,1)S(1)} %copy-done.58, bf16[1024,768]{1,0:T(8,128)(2,1)S(1)} %copy-done.61, bf16[1920,768]{1,0:T(8,128)(2,1)} %collective-permute-done.23), kind=kOutput, calls=%fused_computation.1 | convolution fusion | flops 2418278400 | bytes 11796480 | tf_op jit(solution)/shard_map/dot_general | solution.py:37
  195.0 1.5 pad_maximum_fusion.3
  197.4 1.5 collective-permute-start.25
  200.6 31.7 %backward.1 = (bf16[1024,1152]{1,0:T(8,128)(2,1)}, bf16[1024,1152]{1,0:T(8,128)(2,1)}, bf16[1024,384]{1,0:T(8,128)(2,1)}, bf16[1024,384]{1,0:T(8,128)(2,1)}, f32...) custom-call(bf16[1024,384]{1,0:T(8,128)(2,1)} %get-tuple-element.192.tok_own, bf16[1024,384]{1,0:T(8,128)(2,1)} %collective-permute-done.tok_oth, ...), custom_call_target="tpu_custom_call" | custom-call | flops 24999999488 | bytes 20000000 | tf_op jit(solution)/shard_map/backward/pallas_call | solution.py:394
  232.3 6.1 %convolution_convert_fusion.2 = bf16[768,1152]{1,0:T(8,128)(2,1)} fusion(bf16[1024,768]{1,0:T(8,128)(2,1)} %get-tuple-element.111, bf16[1024,1152]{1,0:T(8,128)(2,1)} %get-tuple-element.129), kind=kOutput, calls=%fused_computation.5 | convolution fusion | flops 1812824064 | bytes 5701632 | tf_op jit(solution)/shard_map/dot_general | solution.py:37
  238.6 3.3 slice.180
  242.1 2.5 maximum_add_fusion
  244.8 1.5 collective-permute-start.29
  246.3 1.6 convert_add_fusion.2
  248.6 3.8 convolution_add_fusion
  252.5 10.9 %collective-permute-done.28 = bf16[192,1536]{1,0:T(8,128)(2,1)S(1)} collective-permute-done((bf16[192,1536]{1,0:T(8,128)(2,1)S(1)}, bf16[192,1536]{1,0:T(8,128)(2,1)S(1)}, u32[]{:S(2)}, u32[]{:S(2)}) %collective-permute-start.28) | collective-permute-done | bytes 589856 | tf_op jit(solution)/shard_map/ppermute | solution.py:420
  269.3 19.8 %collective-permute-done.31 = f32[38,384]{1,0:T(8,128)} collective-permute-done((f32[38,384]{1,0:T(8,128)S(1)}, f32[38,384]{1,0:T(8,128)}, u32[]{:S(2)}, u32[]{:S(2)}) %collective-permute-start.31) | collective-permute-done | bytes 58400 | tf_op jit(solution)/shard_map/ppermute | solution.py:420
  291.3 1.9 convert_add_fusion.3
  293.2 2.6 collective-permute-start.34
  295.8 1.6 slice_dynamic-update-slice_fusion
  297.4 1.3 collective-permute-done.34
  299.6 1.6 collective-permute-start.35
  301.3 10.3 %collective-permute-done.35 = bf16[2,76,384]{2,1,0:T(8,128)(2,1)S(1)} collective-permute-done((bf16[2,76,384]{2,1,0:T(8,128)(2,1)S(1)}, bf16[2,76,384]{2,1,0:T(8,128)(2,1)S(1)}, u32[]{:S(2)}, u32[]{:S(2)}) %collective-permute-start.35) | collective-permute-done | bytes 116768 | tf_op jit(solution)/shard_map/ppermute | solution.py:429
  312.5 1.5 collective-permute-start.36
  315.5 2.0 collective-permute-start.33
  319.6 4.0 collective-permute-done.39
  323.9 7.0 %collective-permute-done.40 = bf16[2,48,1152]{2,1,0:T(8,128)(2,1)S(1)} collective-permute-done((bf16[2,48,1152]{2,1,0:T(8,128)(2,1)S(1)}, bf16[2,48,1152]{2,1,0:T(8,128)(2,1)S(1)}, u32[]{:S(2)}, u32[]{:S(2)}) %collective-permute-start.40) | collective-permute-done | bytes 221216 | tf_op jit(solution)/shard_map/ppermute | solution.py:429
  331.7 2.9 collective-permute-start.41
  337.4 2.4 convolution_bitcast_fusion
  341.7 5.3 %copy.31 = f32[6,384,384]{2,1,0:T(8,128)} copy(f32[6,384,384]{1,2,0:T(8,128)} %convolution_bitcast_fusion) | data formatting | bytes 7077888
  348.5 12.1 %all-reduce.4.cloned.1.call-done.near = bf16[4,432,384]{2,1,0:T(8,128)(2,1)} async-done(((bf16[4,432,384]{2,1,0:T(8,128)(2,1)}), bf16[4,432,384]{2,1,0:T(8,128)(2,1)}) %all-reduce.4.cloned.1.call-update) | async-done | bytes 1327120 | tf_op jit(solution)/shard_map/psum | solution.py:639
  360.6 1.5 collective-permute-start.45
  362.0 2.1 collective-permute-start.42
  364.2 1.9 broadcast_select_fusion.1
  366.1 3.5 collective-permute-done.42
  370.1 5.5 %collective-permute-done.43 = bf16[2,48,1152]{2,1,0:T(8,128)(2,1)S(1)} collective-permute-done((bf16[2,48,1152]{2,1,0:T(8,128)(2,1)S(1)}, bf16[2,48,1152]{2,1,0:T(8,128)(2,1)S(1)}, u32[]{:S(2)}, u32[]{:S(2)}) %collective-permute-start.43) | collective-permute-done | bytes 221216 | tf_op jit(solution)/shard_map/ppermute | solution.py:429
  376.8 1.3 pad_maximum_fusion.2
  378.1 1.3 pad_maximum_fusion.1
  379.4 21.5 %collective-permute-done.44.far = bf16[4,48,1152]{2,1,0:T(8,128)(2,1)S(1)} collective-permute-done((bf16[4,48,1152]{2,1,0:T(8,128)(2,1)S(1)}, bf16[4,48,1152]{2,1,0:T(8,128)(2,1)S(1)}, u32[]{:S(2)}, u32[]{:S(2)}) %collective-permute-start.44) | collective-permute-done | bytes 442400 | tf_op jit(solution)/shard_map/ppermute | solution.py:429
  401.7 2.5 order.2
  405.2 4.3 %order.3 = (f32[8,192,384]{2,1,0:T(8,128)}, f32[8,48,384]{2,1,0:T(8,128)}, f32[8,48,1536]{2,1,0:T(8,128)}) custom-call(s32[1]{0:T(128)} %bitcast.place.mine, bf16[4,432,384]{2,1,0:T(8,128)(2,1)} %all-reduce.4.cloned.1.call-done.near, bf16[4,432,384]{2,1,0:T(8,128)(2,1)} %copy-done.10), custom_call_target="tpu_custom_call" | custom-call | tf_op jit(solution)/shard_map/order/pallas_call | solution.py:516
  (281 shorter events, 42.9 us)
Async XLA Ops:
  7.2 6.0 %copy-start = (bf16[6,384,384]{2,1,0:T(8,128)(2,1)S(1)}, bf16[6,384,384]{2,1,0:T(8,128)(2,1)}, u32[]{:S(2)}) copy-start(bf16[6,384,384]{2,1,0:T(8,128)(2,1)} %param.15) | copy-start | bytes 5308420
  7.2 6.0 %copy-start.25 = (bf16[16,384]{1,0:T(8,128)(2,1)S(1)}, bf16[16,384]{1,0:T(8,128)(2,1)}, u32[]{:S(2)}) copy-start(bf16[16,384]{1,0:T(8,128)(2,1)} %param.14) | copy-start | bytes 36868
  7.2 5.9 %copy-start.33 = (bf16[1536]{0:T(1024)(128)(2,1)S(1)}, bf16[1536]{0:T(1024)(128)(2,1)}, u32[]{:S(2)}) copy-start(bf16[1536]{0:T(1024)(128)(2,1)} %param.22) | copy-start | bytes 9220
  7.2 353.4 %all-reduce.4.cloned.1.call-start = ((), (), s32[]{:S(2)}) async-start(), calls=%async_computation | async-start | bytes 2654208 | tf_op jit(solution)/shard_map/psum | solution.py:639
  10.1 21.7 %collective-permute-start = (bf16[1024,384]{1,0:T(8,128)(2,1)}, bf16[1024,384]{1,0:T(8,128)(2,1)}, u32[]{:S(2)}, u32[]{:S(2)}) collective-permute-start(bf16[1024,384]{1,0:T(8,128)(2,1)} %get-tuple-element.191), channel_id=1, source_target_pairs={{0,2},{2,0},{1,3},{3,1},{4,6},{6,4},{5,7},{7,5},{8,10},{10,8},{9,1... | collective-permute-start | bytes 2359304 | tf_op jit(solution)/shard_map/ppermute | solution.py:420
  14.2 3.3 collective-permute-start.1
  16.2 16.2 %copy-start.37 = (bf16[3,384,384]{2,1,0:T(8,128)(2,1)S(1)}, bf16[3,384,384]{2,1,0:T(8,128)(2,1)}, u32[]{:S(2)}) copy-start(bf16[3,384,384]{2,1,0:T(8,128)(2,1)} %w0.1) | copy-start | bytes 2654212
  17.5 58.3 %copy-start.31 = (f32[1,4,384]{2,1,0:T(4,128)}, f32[1,4,384]{2,1,0:T(4,128)S(1)}, u32[]{:S(2)}) copy-start(f32[1,4,384]{2,1,0:T(4,128)S(1)} %fusion.31.row_own) | copy-start | bytes 18436
  19.1 12.7 %collective-permute-start.2 = (f32[7,4,384]{2,1,0:T(4,128)S(1)}, f32[7,4,384]{2,1,0:T(4,128)S(1)}, u32[]{:S(2)}, u32[]{:S(2)}) collective-permute-start(f32[7,4,384]{2,1,0:T(4,128)S(1)} %pad_maximum_fusion.13), channel_id=1, source_target_pairs={{0,2},{2,0},{1,3},{3,1},{4,6},{6,4},{5,7},{7,5},{8,10},{10,8},{9,1... | collective-permute-start | bytes 129032 | tf_op jit(solution)/shard_map/ppermute | solution.py:420
  32.4 20.9 %collective-permute-start.3 = (bf16[3,384,384]{2,1,0:T(8,128)(2,1)S(1)}, bf16[3,384,384]{2,1,0:T(8,128)(2,1)S(1)}, u32[]{:S(2)}, u32[]{:S(2)}) collective-permute-start(bf16[3,384,384]{2,1,0:T(8,128)(2,1)S(1)} %copy-done.37), channel_id=1, source_target_pairs={{0,2},{2,0},{1,3},{3,1},{4,6},{6,4},{5,7},{7,5},{8,10},{10,8},{9,1... | collective-permute-start | bytes 2654216 | tf_op jit(solution)/shard_map/ppermute | solution.py:420
  34.2 19.7 %collective-permute-start.4 = (bf16[3,384,384]{2,1,0:T(8,128)(2,1)S(1)}, bf16[3,384,384]{2,1,0:T(8,128)(2,1)S(1)}, u32[]{:S(2)}, u32[]{:S(2)}) collective-permute-start(bf16[3,384,384]{2,1,0:T(8,128)(2,1)S(1)} %copy-done.37), channel_id=1, source_target_pairs={{0,1},{1,0},{2,3},{3,2},{4,5},{5,4},{6,7},{7,6},{8,9},{9,8},{10,11... | collective-permute-start | bytes 2654216 | tf_op jit(solution)/shard_map/ppermute | solution.py:424
  53.4 3.7 collective-permute-start.5
  53.4 41.8 %collective-permute-start.15 = (bf16[384,1536]{1,0:T(8,128)(2,1)}, bf16[384,1536]{1,0:T(8,128)(2,1)}, u32[]{:S(2)}, u32[]{:S(2)}) collective-permute-start(bf16[384,1536]{1,0:T(8,128)(2,1)} %x0.1), channel_id=1, source_target_pairs={{0,1},{1,0},{2,3},{3,2},{4,5},{5,4},{6,7},{7,6},{8,9},{9,8},{10,11... | collective-permute-start | bytes 3538952 | tf_op jit(solution)/shard_map/ppermute | solution.py:424
  53.9 41.9 %collective-permute-start.16 = (bf16[1536,384]{1,0:T(8,128)(2,1)}, bf16[1536,384]{1,0:T(8,128)(2,1)}, u32[]{:S(2)}, u32[]{:S(2)}) collective-permute-start(bf16[1536,384]{1,0:T(8,128)(2,1)} %s0.1), channel_id=1, source_target_pairs={{0,1},{1,0},{2,3},{3,2},{4,5},{5,4},{6,7},{7,6},{8,9},{9,8},{10,11... | collective-permute-start | bytes 3538952 | tf_op jit(solution)/shard_map/ppermute | solution.py:424
  57.0 18.8 %collective-permute-start.6 = (bf16[192,1536]{1,0:T(8,128)(2,1)}, bf16[192,1536]{1,0:T(8,128)(2,1)}, u32[]{:S(2)}, u32[]{:S(2)}) collective-permute-start(bf16[192,1536]{1,0:T(8,128)(2,1)} %constant_dynamic-slice_fusion.2), channel_id=1, source_target_pairs={{0,2},{2,0},{1,3},{3,1},{4,6},{6,4},{5,7},{7,5},{8,10},{10,8},{9,1... | collective-permute-start | bytes 1769480 | tf_op jit(solution)/shard_map/ppermute | solution.py:420
  58.4 26.9 %collective-permute-start.7 = (bf16[768,384]{1,0:T(8,128)(2,1)S(1)}, bf16[768,384]{1,0:T(8,128)(2,1)}, u32[]{:S(2)}, u32[]{:S(2)}) collective-permute-start(bf16[768,384]{1,0:T(8,128)(2,1)S(1)} %constant_dynamic-slice_fusion.1), channel_id=1, source_target_pairs={{0,2},{2,0},{1,3},{3,1},{4,6},{6,4},{5,7},{7,5},{8,10},{10,8},{9,1... | collective-permute-start | bytes 1769480 | tf_op jit(solution)/shard_map/ppermute | solution.py:420
  59.1 28.8 %copy-start.12 = (bf16[1024,384]{1,0:T(8,128)(2,1)S(1)}, bf16[1024,384]{1,0:T(8,128)(2,1)}, u32[]{:S(2)}) copy-start(bf16[1024,384]{1,0:T(8,128)(2,1)} %get-tuple-element.96) | copy-start | bytes 2359300
  85.3 4.6 %collective-permute-start.12 = (bf16[16,384]{1,0:T(8,128)(2,1)S(1)}, bf16[16,384]{1,0:T(8,128)(2,1)S(1)}, u32[]{:S(2)}, u32[]{:S(2)}) collective-permute-start(bf16[16,384]{1,0:T(8,128)(2,1)S(1)} %fusion.14), channel_id=1, source_target_pairs={{0,16},{4,20},{8,24},{12,28},{16,0},{20,4},{24,8},{28,12},{1,17},{... | collective-permute-start | bytes 36872 | tf_op jit(solution)/shard_map/ppermute | solution.py:429
  87.8 33.0 %collective-permute-start.8 = (bf16[1024,384]{1,0:T(8,128)(2,1)S(1)}, bf16[1024,384]{1,0:T(8,128)(2,1)S(1)}, u32[]{:S(2)}, u32[]{:S(2)}) collective-permute-start(bf16[1024,384]{1,0:T(8,128)(2,1)S(1)} %copy-done.12), channel_id=1, source_target_pairs={{0,2},{2,0},{1,3},{3,1},{4,6},{6,4},{5,7},{7,5},{8,10},{10,8},{9,1... | collective-permute-start | bytes 2359304 | tf_op jit(solution)/shard_map/ppermute | solution.py:420
  89.4 23.3 %collective-permute-start.9 = (bf16[384,384]{1,0:T(8,128)(2,1)}, bf16[384,384]{1,0:T(8,128)(2,1)S(1)}, u32[]{:S(2)}, u32[]{:S(2)}) collective-permute-start(bf16[384,384]{1,0:T(8,128)(2,1)} %o0), channel_id=1, source_target_pairs={{0,2},{2,0},{1,3},{3,1},{4,6},{6,4},{5,7},{7,5},{8,10},{10,8},{9,1... | collective-permute-start | bytes 884744 | tf_op jit(solution)/shard_map/ppermute | solution.py:420
  89.9 3.8 collective-permute-start.13
  93.8 4.7 %collective-permute-start.14 = (bf16[64,384]{1,0:T(8,128)(2,1)S(1)}, bf16[64,384]{1,0:T(8,128)(2,1)S(1)}, u32[]{:S(2)}, u32[]{:S(2)}) collective-permute-start(bf16[64,384]{1,0:T(8,128)(2,1)S(1)} %pad_maximum_fusion.12), channel_id=1, source_target_pairs={{0,4},{4,0},{8,12},{12,8},{16,20},{20,16},{24,28},{28,24},{1,5},{5... | collective-permute-start | bytes 147464 | tf_op jit(solution)/shard_map/ppermute | solution.py:429
  95.2 17.5 %collective-permute-start.10 = (bf16[192,1536]{1,0:T(8,128)(2,1)}, bf16[192,1536]{1,0:T(8,128)(2,1)S(1)}, u32[]{:S(2)}, u32[]{:S(2)}) collective-permute-start(bf16[192,1536]{1,0:T(8,128)(2,1)} %collective-permute-done.6.x1), channel_id=1, source_target_pairs={{0,4},{4,0},{8,12},{12,8},{16,20},{20,16},{24,28},{28,24},{1,5},{5... | collective-permute-start | bytes 1769480 | tf_op jit(solution)/shard_map/ppermute | solution.py:429
  95.8 25.0 %collective-permute-start.17 = (bf16[192,1536]{1,0:T(8,128)(2,1)}, bf16[192,1536]{1,0:T(8,128)(2,1)S(1)}, u32[]{:S(2)}, u32[]{:S(2)}) collective-permute-start(bf16[192,1536]{1,0:T(8,128)(2,1)} %collective-permute-done.6.x1), channel_id=1, source_target_pairs={{0,1},{1,0},{2,3},{3,2},{4,5},{5,4},{6,7},{7,6},{8,9},{9,8},{10,11... | collective-permute-start | bytes 1769480 | tf_op jit(solution)/shard_map/ppermute | solution.py:424
  98.5 22.4 %collective-permute-start.11 = (bf16[768,384]{1,0:T(8,128)(2,1)}, bf16[768,384]{1,0:T(8,128)(2,1)S(1)}, u32[]{:S(2)}, u32[]{:S(2)}) collective-permute-start(bf16[768,384]{1,0:T(8,128)(2,1)} %collective-permute-done.7.s1), channel_id=1, source_target_pairs={{0,4},{4,0},{8,12},{12,8},{16,20},{20,16},{24,28},{28,24},{1,5},{5... | collective-permute-start | bytes 1769480 | tf_op jit(solution)/shard_map/ppermute | solution.py:429
  112.6 13.1 %copy-start.48 = (bf16[384,384]{1,0:T(8,128)(2,1)}, bf16[384,384]{1,0:T(8,128)(2,1)S(1)}, u32[]{:S(2)}) copy-start(bf16[384,384]{1,0:T(8,128)(2,1)S(1)} %collective-permute-done.9.o1) | copy-start | bytes 884740
  112.6 8.2 %collective-permute-start.18 = (bf16[768,384]{1,0:T(8,128)(2,1)}, bf16[768,384]{1,0:T(8,128)(2,1)S(1)}, u32[]{:S(2)}, u32[]{:S(2)}) collective-permute-start(bf16[768,384]{1,0:T(8,128)(2,1)} %collective-permute-done.7.s1), channel_id=1, source_target_pairs={{0,1},{1,0},{2,3},{3,2},{4,5},{5,4},{6,7},{7,6},{8,9},{9,8},{10,11... | collective-permute-start | bytes 1769480 | tf_op jit(solution)/shard_map/ppermute | solution.py:424
  112.7 13.7 %copy-start.42 = (bf16[192,1536]{1,0:T(8,128)(2,1)}, bf16[192,1536]{1,0:T(8,128)(2,1)S(1)}, u32[]{:S(2)}) copy-start(bf16[192,1536]{1,0:T(8,128)(2,1)S(1)} %collective-permute-done.10.x2) | copy-start | bytes 1769476
  122.0 3.7 collective-permute-start.21
  122.0 3.7 collective-permute-start.22
  122.5 2.5 collective-permute-start.19
  122.5 3.2 collective-permute-start.20
  165.2 6.7 %copy-start.52 = (bf16[1024,768]{1,0:T(8,128)(2,1)S(1)}, bf16[1024,768]{1,0:T(8,128)(2,1)}, u32[]{:S(2)}) copy-start(bf16[1024,768]{1,0:T(8,128)(2,1)} %get-tuple-element.102.att) | copy-start | bytes 4718596
  165.2 6.7 %copy-start.54 = (bf16[1024,768]{1,0:T(8,128)(2,1)S(1)}, bf16[1024,768]{1,0:T(8,128)(2,1)}, u32[]{:S(2)}) copy-start(bf16[1024,768]{1,0:T(8,128)(2,1)} %get-tuple-element.117) | copy-start | bytes 4718596
  171.8 8.4 %collective-permute-start.24 = (bf16[768,1536]{1,0:T(8,128)(2,1)}, bf16[768,1536]{1,0:T(8,128)(2,1)}, u32[]{:S(2)}, u32[]{:S(2)}) collective-permute-start(bf16[768,1536]{1,0:T(8,128)(2,1)} %convolution_convert_fusion), channel_id=1, source_target_pairs={{0,1},{1,0},{2,3},{3,2},{4,5},{5,4},{6,7},{7,6},{8,9},{9,8},{10,11... | collective-permute-start | bytes 7077896 | tf_op jit(solution)/shard_map/ppermute | solution.py:424
  179.0 6.7 %collective-permute-start.23 = (bf16[1920,768]{1,0:T(8,128)(2,1)}, bf16[1920,768]{1,0:T(8,128)(2,1)}, u32[]{:S(2)}, u32[]{:S(2)}) collective-permute-start(bf16[1920,768]{1,0:T(8,128)(2,1)} %pad_maximum_fusion), channel_id=1, source_target_pairs={{0,1},{1,0},{2,3},{3,2},{4,5},{5,4},{6,7},{7,6},{8,9},{9,8},{10,11... | collective-permute-start | bytes 8847368 | tf_op jit(solution)/shard_map/ppermute | solution.py:424
  185.6 13.2 %copy-start.1 = (f32[768,1536]{1,0:T(8,128)}, f32[768,1536]{1,0:T(8,128)S(1)}, u32[]{:S(2)}) copy-start(f32[768,1536]{1,0:T(8,128)S(1)} %convert_add_fusion) | copy-start | bytes 14155780
  188.2 6.7 %copy-start.14 = (f32[384,768]{1,0:T(8,128)}, f32[384,768]{1,0:T(8,128)S(1)}, u32[]{:S(2)}) copy-start(f32[384,768]{1,0:T(8,128)S(1)} %convolution_add_fusion.1) | copy-start | bytes 3538948
  197.4 35.0 %collective-permute-start.25 = (bf16[8,240,384]{2,1,0:T(8,128)(2,1)}, bf16[8,240,384]{2,1,0:T(8,128)(2,1)S(1)}, u32[]{:S(2)}, u32[]{:S(2)}) collective-permute-start(bf16[8,240,384]{2,1,0:T(8,128)(2,1)} %pad_maximum_fusion.3), channel_id=1, source_target_pairs={{0,2},{2,0},{1,3},{3,1},{4,6},{6,4},{5,7},{7,5},{8,10},{10,8},{9,1... | collective-permute-start | bytes 4423688 | tf_op jit(solution)/shard_map/ppermute | solution.py:420
  200.0 32.3 %collective-permute-start.26 = (bf16[2,192,1536]{2,1,0:T(8,128)(2,1)}, bf16[2,192,1536]{2,1,0:T(8,128)(2,1)}, u32[]{:S(2)}, u32[]{:S(2)}) collective-permute-start(bf16[2,192,1536]{2,1,0:T(8,128)(2,1)} %dynamic-slice_convert_fusion), channel_id=1, source_target_pairs={{0,4},{4,0},{8,12},{12,8},{16,20},{20,16},{24,28},{28,24},{1,5},{5... | collective-permute-start | bytes 3538952 | tf_op jit(solution)/shard_map/ppermute | solution.py:429
  232.3 6.2 %copy-start.7 = (bf16[8,240,384]{2,1,0:T(8,128)(2,1)}, bf16[8,240,384]{2,1,0:T(8,128)(2,1)S(1)}, u32[]{:S(2)}) copy-start(bf16[8,240,384]{2,1,0:T(8,128)(2,1)S(1)} %collective-permute-done.25) | copy-start | bytes 4423684
  232.3 6.2 %copy-start.26 = (f32[4,4,768]{2,1,0:T(4,128)S(1)}, f32[4,4,768]{2,1,0:T(4,128)}, u32[]{:S(2)}) copy-start(f32[4,4,768]{2,1,0:T(4,128)} %get-tuple-element.137) | copy-start | bytes 147460
  238.5 10.1 %collective-permute-start.27 = (bf16[768,1152]{1,0:T(8,128)(2,1)}, bf16[768,1152]{1,0:T(8,128)(2,1)}, u32[]{:S(2)}, u32[]{:S(2)}) collective-permute-start(bf16[768,1152]{1,0:T(8,128)(2,1)} %convolution_convert_fusion.2), channel_id=1, source_target_pairs={{0,1},{1,0},{2,3},{3,2},{4,5},{5,4},{6,7},{7,6},{8,9},{9,8},{10,11... | collective-permute-start | bytes 5308424 | tf_op jit(solution)/shard_map/ppermute | solution.py:424
  244.8 19.0 %collective-permute-start.29 = (bf16[4,240,384]{2,1,0:T(8,128)(2,1)S(1)}, bf16[4,240,384]{2,1,0:T(8,128)(2,1)S(1)}, u32[]{:S(2)}, u32[]{:S(2)}) collective-permute-start(bf16[4,240,384]{2,1,0:T(8,128)(2,1)S(1)} %dynamic-slice_convert_fusion.1), channel_id=1, source_target_pairs={{0,4},{4,0},{8,12},{12,8},{16,20},{20,16},{24,28},{28,24},{1,5},{5... | collective-permute-start | bytes 2211848 | tf_op jit(solution)/shard_map/ppermute | solution.py:429
  247.9 15.5 %collective-permute-start.28 = (bf16[192,1536]{1,0:T(8,128)(2,1)S(1)}, bf16[192,1536]{1,0:T(8,128)(2,1)S(1)}, u32[]{:S(2)}, u32[]{:S(2)}) collective-permute-start(bf16[192,1536]{1,0:T(8,128)(2,1)S(1)} %fusion.5), channel_id=1, source_target_pairs={{0,2},{2,0},{1,3},{3,1},{4,6},{6,4},{5,7},{7,5},{8,10},{10,8},{9,1... | collective-permute-start | bytes 1769480 | tf_op jit(solution)/shard_map/ppermute | solution.py:420
  252.5 13.8 %copy-start.4 = (f32[768,1152]{1,0:T(8,128)}, f32[768,1152]{1,0:T(8,128)S(1)}, u32[]{:S(2)}) copy-start(f32[768,1152]{1,0:T(8,128)S(1)} %convolution_add_fusion) | copy-start | bytes 10616836
  266.4 24.9 %collective-permute-start.30 = (bf16[384,1152]{1,0:T(8,128)(2,1)S(1)}, bf16[384,1152]{1,0:T(8,128)(2,1)}, u32[]{:S(2)}, u32[]{:S(2)}) collective-permute-start(bf16[384,1152]{1,0:T(8,128)(2,1)S(1)} %slice.302), channel_id=1, source_target_pairs={{0,2},{2,0},{1,3},{3,1},{4,6},{6,4},{5,7},{7,5},{8,10},{10,8},{9,1... | collective-permute-start | bytes 2654216 | tf_op jit(solution)/shard_map/ppermute | solution.py:420
  267.6 21.5 %collective-permute-start.31 = (f32[38,384]{1,0:T(8,128)S(1)}, f32[38,384]{1,0:T(8,128)}, u32[]{:S(2)}, u32[]{:S(2)}) collective-permute-start(f32[38,384]{1,0:T(8,128)S(1)} %concatenate.103), channel_id=1, source_target_pairs={{0,2},{2,0},{1,3},{3,1},{4,6},{6,4},{5,7},{7,5},{8,10},{10,8},{9,1... | collective-permute-start | bytes 175112 | tf_op jit(solution)/shard_map/ppermute | solution.py:420
  293.2 5.5 %collective-permute-start.34 = (bf16[1,76,384]{2,1,0:T(8,128)(2,1)}, bf16[1,76,384]{2,1,0:T(8,128)(2,1)}, u32[]{:S(2)}, u32[]{:S(2)}) collective-permute-start(bf16[1,76,384]{2,1,0:T(8,128)(2,1)} %maximum_bitcast_fusion.2), channel_id=1, source_target_pairs={{0,16},{4,20},{8,24},{12,28},{16,0},{20,4},{24,8},{28,12},{1,17},{... | collective-permute-start | bytes 175112 | tf_op jit(solution)/shard_map/ppermute | solution.py:429
  299.6 12.0 %collective-permute-start.35 = (bf16[2,76,384]{2,1,0:T(8,128)(2,1)S(1)}, bf16[2,76,384]{2,1,0:T(8,128)(2,1)S(1)}, u32[]{:S(2)}, u32[]{:S(2)}) collective-permute-start(bf16[2,76,384]{2,1,0:T(8,128)(2,1)S(1)} %pad_maximum_fusion.8), channel_id=1, source_target_pairs={{0,8},{4,12},{8,0},{12,4},{16,24},{20,28},{24,16},{28,20},{1,9},{5... | collective-permute-start | bytes 350216 | tf_op jit(solution)/shard_map/ppermute | solution.py:429
  312.5 6.3 %collective-permute-start.36 = (bf16[4,76,384]{2,1,0:T(8,128)(2,1)S(1)}, bf16[4,76,384]{2,1,0:T(8,128)(2,1)S(1)}, u32[]{:S(2)}, u32[]{:S(2)}) collective-permute-start(bf16[4,76,384]{2,1,0:T(8,128)(2,1)S(1)} %pad_maximum_fusion.6), channel_id=1, source_target_pairs={{0,4},{4,0},{8,12},{12,8},{16,20},{20,16},{24,28},{28,24},{1,5},{5... | collective-permute-start | bytes 700424 | tf_op jit(solution)/shard_map/ppermute | solution.py:429
  314.8 8.7 %collective-permute-start.39 = (bf16[4,48,1152]{2,1,0:T(8,128)(2,1)S(1)}, bf16[4,48,1152]{2,1,0:T(8,128)(2,1)S(1)}, u32[]{:S(2)}, u32[]{:S(2)}) collective-permute-start(bf16[4,48,1152]{2,1,0:T(8,128)(2,1)S(1)} %dynamic-slice_convert_fusion.2), channel_id=1, source_target_pairs={{0,4},{4,0},{8,12},{12,8},{16,20},{20,16},{24,28},{28,24},{1,5},{5... | collective-permute-start | bytes 1327112 | tf_op jit(solution)/shard_map/ppermute | solution.py:429
  315.5 48.7 %collective-permute-start.32 = (bf16[1024,384]{1,0:T(8,128)(2,1)}, bf16[1024,384]{1,0:T(8,128)(2,1)}, u32[]{:S(2)}, u32[]{:S(2)}) collective-permute-start(bf16[1024,384]{1,0:T(8,128)(2,1)} %get-tuple-element.142), channel_id=1, source_target_pairs={{0,2},{2,0},{1,3},{3,1},{4,6},{6,4},{5,7},{7,5},{8,10},{10,8},{9,1... | collective-permute-start | bytes 2359304 | tf_op jit(solution)/shard_map/ppermute | solution.py:420
  315.5 48.7 %collective-permute-start.33 = (bf16[1024,384]{1,0:T(8,128)(2,1)}, bf16[1024,384]{1,0:T(8,128)(2,1)}, u32[]{:S(2)}, u32[]{:S(2)}) collective-permute-start(bf16[1024,384]{1,0:T(8,128)(2,1)} %get-tuple-element.144), channel_id=1, source_target_pairs={{0,2},{2,0},{1,3},{3,1},{4,6},{6,4},{5,7},{7,5},{8,10},{10,8},{9,1... | collective-permute-start | bytes 2359304 | tf_op jit(solution)/shard_map/ppermute | solution.py:420
  323.7 7.2 %collective-permute-start.40 = (bf16[2,48,1152]{2,1,0:T(8,128)(2,1)S(1)}, bf16[2,48,1152]{2,1,0:T(8,128)(2,1)S(1)}, u32[]{:S(2)}, u32[]{:S(2)}) collective-permute-start(bf16[2,48,1152]{2,1,0:T(8,128)(2,1)S(1)} %dynamic-slice_convert_fusion.3), channel_id=1, source_target_pairs={{0,8},{4,12},{8,0},{12,4},{16,24},{20,28},{24,16},{28,20},{1,9},{5... | collective-permute-start | bytes 663560 | tf_op jit(solution)/shard_map/ppermute | solution.py:429
  323.8 10.8 %collective-permute-start.37 = (bf16[400,384]{1,0:T(8,128)(2,1)S(1)}, bf16[400,384]{1,0:T(8,128)(2,1)S(1)}, u32[]{:S(2)}, u32[]{:S(2)}) collective-permute-start(bf16[400,384]{1,0:T(8,128)(2,1)S(1)} %pad_maximum_fusion.5), channel_id=1, source_target_pairs={{0,1},{1,0},{2,3},{3,2},{4,5},{5,4},{6,7},{7,6},{8,9},{9,8},{10,11... | collective-permute-start | bytes 921608 | tf_op jit(solution)/shard_map/ppermute | solution.py:424
  331.7 15.9 %collective-permute-start.41 = (bf16[1,48,1152]{2,1,0:T(8,128)(2,1)}, bf16[1,48,1152]{2,1,0:T(8,128)(2,1)}, u32[]{:S(2)}, u32[]{:S(2)}) collective-permute-start(bf16[1,48,1152]{2,1,0:T(8,128)(2,1)} %dynamic-slice_convert_fusion.4), channel_id=1, source_target_pairs={{0,16},{4,20},{8,24},{12,28},{16,0},{20,4},{24,8},{28,12},{1,17},{... | collective-permute-start | bytes 331784 | tf_op jit(solution)/shard_map/ppermute | solution.py:429
  336.4 10.5 %collective-permute-start.38 = (f32[16,384]{1,0:T(8,128)S(1)}, f32[16,384]{1,0:T(8,128)S(1)}, u32[]{:S(2)}, u32[]{:S(2)}) collective-permute-start(f32[16,384]{1,0:T(8,128)S(1)} %convolution_bitcast_fusion.1), channel_id=1, source_target_pairs={{0,2},{2,0},{1,3},{3,1},{4,6},{6,4},{5,7},{7,5},{8,10},{10,8},{9,1... | collective-permute-start | bytes 73736 | tf_op jit(solution)/shard_map/ppermute | solution.py:420
  341.7 5.9 %copy-start.9 = (f32[2,48,1152]{2,1,0:T(8,128)S(1)}, f32[2,48,1152]{2,1,0:T(8,128)}, u32[]{:S(2)}) copy-start(f32[2,48,1152]{2,1,0:T(8,128)} %copy-done.8) | copy-start | bytes 1327108
  341.7 22.5 %copy-start.11 = (bf16[1024,384]{1,0:T(8,128)(2,1)S(1)}, bf16[1024,384]{1,0:T(8,128)(2,1)}, u32[]{:S(2)}) copy-start(bf16[1024,384]{1,0:T(8,128)(2,1)} %get-tuple-element.110) | copy-start | bytes 2359300
  360.6 43.6 %collective-permute-start.45 = (bf16[4,432,384]{2,1,0:T(8,128)(2,1)}, bf16[4,432,384]{2,1,0:T(8,128)(2,1)S(1)}, u32[]{:S(2)}, u32[]{:S(2)}) collective-permute-start(bf16[4,432,384]{2,1,0:T(8,128)(2,1)} %all-reduce.4.cloned.1.call-done.near), channel_id=1, source_target_pairs={{0,4},{4,0},{8,12},{12,8},{16,20},{20,16},{24,28},{28,24},{1,5},{5... | collective-permute-start | bytes 3981320 | tf_op jit(solution)/shard_map/ppermute | solution.py:429
  362.0 7.6 %collective-permute-start.42 = (bf16[1,48,1152]{2,1,0:T(8,128)(2,1)S(1)}, bf16[1,48,1152]{2,1,0:T(8,128)(2,1)S(1)}, u32[]{:S(2)}, u32[]{:S(2)}) collective-permute-start(bf16[1,48,1152]{2,1,0:T(8,128)(2,1)S(1)} %add_convert_fusion.1), channel_id=1, source_target_pairs={{0,16},{4,20},{8,24},{12,28},{16,0},{20,4},{24,8},{28,12},{1,17},{... | collective-permute-start | bytes 331784 | tf_op jit(solution)/shard_map/ppermute | solution.py:429
  369.7 6.0 %collective-permute-start.43 = (bf16[2,48,1152]{2,1,0:T(8,128)(2,1)S(1)}, bf16[2,48,1152]{2,1,0:T(8,128)(2,1)S(1)}, u32[]{:S(2)}, u32[]{:S(2)}) collective-permute-start(bf16[2,48,1152]{2,1,0:T(8,128)(2,1)S(1)} %pad_maximum_fusion.7), channel_id=1, source_target_pairs={{0,8},{4,12},{8,0},{12,4},{16,24},{20,28},{24,16},{28,20},{1,9},{5... | collective-permute-start | bytes 663560 | tf_op jit(solution)/shard_map/ppermute | solution.py:429
  375.7 25.2 %collective-permute-start.44 = (bf16[4,48,1152]{2,1,0:T(8,128)(2,1)S(1)}, bf16[4,48,1152]{2,1,0:T(8,128)(2,1)S(1)}, u32[]{:S(2)}, u32[]{:S(2)}) collective-permute-start(bf16[4,48,1152]{2,1,0:T(8,128)(2,1)S(1)} %constant_dynamic-update-slice_fusion.4.near), channel_id=1, source_target_pairs={{0,4},{4,0},{8,12},{12,8},{16,20},{20,16},{24,28},{28,24},{1,5},{5... | collective-permute-start | bytes 1327112 | tf_op jit(solution)/shard_map/ppermute | solution.py:429
  (47 other events, 139.1 us)
Sparse Core Ops, SparseCore 0:
  297.6 62.9 all-reduce.3

commit v4 on v3

--- a/solution.py
+++ b/solution.py
@@ -470,10 +470,44 @@
     return kept + swap_dp(sent.astype(B16), distance).astype(F32)
 
 
-def gather_dp(values):
-    for distance in reversed(distances()):
-        values = jnp.concatenate([values, swap_dp(values, distance)], axis=0)
+def far_groups():
+    far = distances()[1:]
+    return [far[at : at + 2] for at in range(0, len(far), 2)]
+
+
+def around(group):
+    if len(group) == 1:
+        return [group[0]]
+    return [group[1], group[0], group[0] + group[1]]
+
+
+def scatter_group(values, group):
+    me = lax.axis_index("dp")
+    place = 0
+    for distance in group:
+        place = 2 * place + (me // distance) % 2
+    size = values.shape[0] >> len(group)
+    total = lax.dynamic_slice_in_dim(values, place * size, size, 0)
+    for block, distance in enumerate(around(group), 1):
+        sent = lax.dynamic_slice_in_dim(values, (place ^ block) * size, size, 0)
+        total = total + swap_dp(sent.astype(B16), distance).astype(F32)
+    return total
+
+
+def gather_group(values, group):
+    return jnp.concatenate(
+        [values] + [swap_dp(values, distance) for distance in around(group)], axis=0
+    )
+
+
+def gather_far(values):
+    for group in reversed(far_groups()):
+        values = gather_group(values, group)
     return values
+
+
+def gather_near(values):
+    return jnp.concatenate([values, swap_dp(values, 1)], axis=0)
 
 
 def near_place():
@@ -487,12 +521,13 @@
     return jnp.full((1,), mine, jnp.int32)
 
 
-def order_grid_kernel(mine, near, far, shr_out, out_out, exp_out):
+def order_grid_kernel(mine, p0, p1, p2, p3, shr_out, out_out, exp_out):
     shr_rows, out_rows, exp_rows = shr_out.shape[1], out_out.shape[1], exp_out.shape[1]
-    count = near.shape[0]
-    for values, place in ((near, mine[0]), (far, 1 - mine[0])):
-        for block in range(count):
-            into = place * count + block
+    index = 0
+    for values in (p0, p1, p2, p3):
+        for block in range(values.shape[0]):
+            into = mine[0] ^ index
+            index += 1
             shr_out[into] = values[block, :shr_rows].astype(F32)
             out_out[into] = values[block, shr_rows : shr_rows + out_rows].astype(F32)
             for part in range(exp_out.shape[2] // HALF):
@@ -568,15 +603,14 @@
     first, qkv, attended = call_forward(
         tok_own, tok_oth, (*mods, col_own, col_oth), attend_pieces
     )
-    attended, exp_near, shr_near, outproj, cot_sent, act_late = lax.optimization_barrier(
-        (attended, exp_near, shr_near, outproj, cot_sent, act_cond)
+    attended, exp_near, shr_near, outproj, cot_sent = lax.optimization_barrier(
+        (attended, exp_near, shr_near, outproj, cot_sent)
     )
     cot_oth, out_over = swap_row(cot_sent), swap_row(outproj)
     exp_far, shr_far = swap_dp(exp_near, 1), swap_dp(shr_near, 1)
     early = [swap_col(values) for values in (expand, shrink, exp_near, shr_near)]
-    cond_all = gather_dp(act_late)
-    cot_oth, out_over, exp_far, shr_far, cond_all, *early = lax.optimization_barrier(
-        (cot_oth, out_over, exp_far, shr_far, cond_all, *early)
+    cot_oth, out_over, exp_far, shr_far, *early = lax.optimization_barrier(
+        (cot_oth, out_over, exp_far, shr_far, *early)
     )
     exp_pieces = (expand, exp_near, exp_far, early[0], early[2], swap_col(exp_far))
     shr_pieces = (shrink, shr_near, shr_far, early[1], early[3], swap_col(shr_far))
@@ -624,21 +658,19 @@
     exp_got = swap_row(exp_part[1].astype(B16))
     shr_got = swap_dp(shr_sent.astype(B16), near_step)
     att_total = dot_tn(first, dqkv_own) + att_got
-    att_total, exp_got, shr_got, mod_early, grad_oth, res_oth = lax.optimization_barrier(
-        (att_total, exp_got, shr_got, mod_early, grad_oth, res_oth)
+    att_total, exp_got, shr_got, mod_early, act_late = lax.optimization_barrier(
+        (att_total, exp_got, shr_got, mod_early, act_cond)
     )
     att_mine, att_theirs = halves(att_total, 0)
     att_part = att_mine + swap_row(att_theirs.astype(B16)).astype(F32)
-    exp_part = (exp_part[0] + exp_got.astype(F32)).astype(B16)
+    exp_part = exp_part[0] + exp_got.astype(F32)
     exp_part = exp_part.reshape(size // 2, HALF // size, -1)
     grid_part = jnp.concatenate(
-        [(shr_kept + shr_got.astype(F32)).astype(B16)]
+        [shr_kept + shr_got.astype(F32)]
         + [exp_part[:, :, at : at + HALF] for at in range(0, exp_part.shape[2], HALF)],
         axis=1,
     )
-    grid_part = lax.psum(
-        grid_part, "dp", axis_index_groups=[list(range(place, size, 2)) for place in range(2)]
-    )
+    grid_part = scatter_stage(grid_part, far_steps[0])
 
     d_modulation = jnp.concatenate([mod_early, mod_late], axis=1).astype(B16).astype(F32)
     sums_late = jnp.sum(sums_late, axis=(0, 1))
@@ -658,21 +690,45 @@
     low = (sums - high.astype(F32)).astype(B16)
     width = block.shape[0] + 2 * sums.shape[0]
     packed = jnp.concatenate([block, high, low], axis=0)[None]
-    att_part, packed, grad_oth, res_oth = lax.optimization_barrier(
-        (att_part, packed, grad_oth, res_oth)
-    )
-    packed_all = gather_dp(packed)
-    att_part = att_part.reshape(size, HALF // size, -1)
-    for distance in distances():
-        att_part = scatter_stage(att_part, distance)
-    att_part, grid_part = lax.optimization_barrier((att_part.astype(B16), grid_part))
-    for distance in reversed(far_steps):
-        att_part = jnp.concatenate([att_part, swap_dp(att_part, distance)], axis=0)
+    att_part, grid_part, packed, act_late, res_oth = lax.optimization_barrier(
+        (att_part, grid_part, packed, act_late, res_oth)
+    )
+
+    res_got = swap_row(res_oth)
+    att_part = scatter_stage(att_part.reshape(size, HALF // size, -1), near_step)
+    for distance in far_steps[1:]:
+        grid_part = scatter_stage(grid_part, distance)
+    packed_all = gather_far(packed)
+    att_part, near_one, packed_all, grad_oth = lax.optimization_barrier(
+        (att_part, grid_part.astype(B16), packed_all, grad_oth)
+    )
+
+    grad_got = swap_row(grad_oth)
+    for distance in reversed(far_steps[1:]):
+        near_one = jnp.concatenate([near_one, swap_dp(near_one, distance)], axis=0)
+    for places in far_groups():
+        att_part = scatter_group(att_part, places)
+    packed_all = gather_near(packed_all)
+    att_near, near_one, packed_all, act_late = lax.optimization_barrier(
+        (att_part.astype(B16), near_one, packed_all, act_late)
+    )
+
+    near_two = swap_dp(near_one, far_steps[0])
+    far_one = swap_dp(near_one, near_step)
+    att_near = gather_far(att_near)
+    cond_all = gather_far(act_late)
+    att_near, near_two, cond_all = lax.optimization_barrier((att_near, near_two, cond_all))
+
+    far_two = swap_dp(near_two, near_step)
+    att_far = swap_dp(att_near, near_step)
+    cond_all = gather_near(cond_all)
+    result = in_order(row, res_own, res_got)
+    input_gradient = in_order(row, grad_own, grad_got)
     exp_width = expand.shape[1]
     shrink_grad, outproj_grad, expand_grad = order(
         order_grid_kernel,
-        near_place(),
-        (grid_part, swap_dp(grid_part, near_step)),
+        sum_place(),
+        (near_one, near_two, far_one, far_two),
         [(size, depth // size, HALF), (size, HALF // size, HALF), (size, HALF // size, exp_width)],
     )
     shrink_grad, outproj_grad = [part.reshape(-1, HALF) for part in (shrink_grad, outproj_grad)]
@@ -680,7 +736,7 @@
     (attend_grad,) = order(
         order_attend_kernel,
         sum_place(),
-        (att_part, swap_dp(att_part, near_step)),
+        (att_near, att_far),
         [(3, size, HALF // size, HALF)],
     )
     attend_grad = attend_grad.reshape(3, HALF, HALF)
@@ -699,8 +755,6 @@
     attbias_grad = sums[2:4]
     expbias_grad = sums[4:].reshape(-1)
 
-    result = in_order(row, res_own, swap_row(res_oth))
-    input_gradient = in_order(row, grad_own, swap_row(grad_oth))
     mod_all = jnp.concatenate([block_all, other_all], axis=0).reshape(-1, 6, HALF)
     cond_mine, cond_theirs = pick(
         cond_all.reshape(-1, 2 * group, HALF).transpose(1, 0, 2), col

time: 422 us -> 404 us (0.957)
  waiting for transfers between devices: 169 us -> 149 us
  between operations: 15.4 us -> 2.02 us
  other arithmetic: 23.3 us -> 33.7 us
  starting transfers between devices: 42.6 us -> 48.9 us
    ppermute x14, waiting for transfers between devices: 83.6 us -> 64.6 us  [swap_row(): return lax.ppermute(values, 'row', SWAP)]
    psum x1 -> x0, waiting for transfers between devices: 12.1 us -> none  [shards(): lax.psum(grid_part, 'dp', axis_index_groups=[list(range(place, size, 2))...]
    ppermute x17 -> x26, waiting for transfers between devices: 67.1 us -> 78.2 us  [swap_dp(): lax.ppermute(values, 'dp', [(place, place ^ distance) for place in range(...]
    ppermute x17 -> x26, starting transfers between devices: 24 us -> 31 us  [swap_dp(): lax.ppermute(values, 'dp', [(place, place ^ distance) for place in range(...]
    unnamed x139 -> x130, local copies, waits for them, and re-layouts: 18.9 us -> 13.6 us
  transfers between devices with their start and end apart: 47 -> 55, of which waited for: 23 -> 24; matrix products, arithmetic and copies ran while one was open for 14% -> 17% of each run, Pallas kernels for 12% -> 13%
where the time goes in v4:
time: 404 us; the launch traced here: 398 us
  waiting for transfers between devices  149 us (37%)
  Pallas kernels  93.6 us (23%)
  starting transfers between devices  48.9 us (12%)
  matrix products  38.5 us (10%)
  other arithmetic  33.7 us (8%)
  local copies, waits for them, and re-layouts  33.1 us (8%)
    ppermute x26, waiting for transfers between devices, swap_dp(): lax.ppermute(values, 'dp', [(place, place ^ distance) for place in range(...  78.2 us
    ppermute x14, waiting for transfers between devices, swap_row(): return lax.ppermute(values, 'row', SWAP)  64.6 us
    pallas_call x1, Pallas kernels, call_middle(): pl.pallas_call(middle_kernel, grid=(steps,), in_specs=[pl.BlockSpec(memor...  38.3 us
    dot_general x8, matrix products, dot_tn(): lax.dot_general(left, right, (((0,), (0,)), ((), ())), preferred_element_...  34.5 us
    pallas_call x1, Pallas kernels, call_backward(): pl.pallas_call(backward_kernel, grid=(latents,), in_specs=[tiles(SEQ, HAL...  31.7 us
    ppermute x26, starting transfers between devices, swap_dp(): lax.ppermute(values, 'dp', [(place, place ^ distance) for place in range(...  31 us
    pallas_call x1, Pallas kernels, call_forward(): pl.pallas_call(forward_kernel, grid=(latents,), in_specs=[tiles(SEQ, HALF...  16.7 us
    ppermute x14, starting transfers between devices, swap_row(): return lax.ppermute(values, 'row', SWAP)  15.8 us
  transfers between devices with their start and end apart: 55, of which 24 were waited for; matrix products, arithmetic and copies ran while one was open for 17% of the time, Pallas kernels for 13%

profile of v4, /device:TPU:0, one launch (start us, length us, event | category | flops | bytes accessed | tf_op | source)
XLA Modules:
  0.0 398.4 jit_solution(7945694097157207301)
XLA Ops:
  0.7 2.8 constant_dynamic-slice_fusion.6
  3.5 3.0 collective-permute-start
  7.6 1.9 constant_dynamic-slice_fusion.2
  13.7 11.5 %collective-permute-done.2.mod_oth = f32[7,4,384]{2,1,0:T(4,128)S(1)} collective-permute-done((f32[7,4,384]{2,1,0:T(4,128)S(1)}, f32[7,4,384]{2,1,0:T(4,128)S(1)}, u32[]{:S(2)}, u32[]{:S(2)}) %collective-permute-start.2) | collective-permute-done | bytes 43040 | tf_op jit(solution)/shard_map/ppermute | solution.py:420
  25.2 1.8 collective-permute-start.3
  27.0 19.2 %collective-permute-done.3.w1 = bf16[3,384,384]{2,1,0:T(8,128)(2,1)S(1)} collective-permute-done((bf16[3,384,384]{2,1,0:T(8,128)(2,1)S(1)}, bf16[3,384,384]{2,1,0:T(8,128)(2,1)S(1)}, u32[]{:S(2)}, u32[]{:S(2)}) %collective-permute-start.3) | collective-permute-done | bytes 884768 | tf_op jit(solution)/shard_map/ppermute | solution.py:420
  46.7 3.1 collective-permute-done.5.w3
  49.9 1.4 collective-permute-start.6
  51.9 16.7 %forward.1 = (bf16[1024,768]{1,0:T(8,128)(2,1)}, bf16[1024,2304]{1,0:T(8,128)(2,1)}, bf16[1024,768]{1,0:T(8,128)(2,1)}) custom-call(bf16[1024,384]{1,0:T(8,128)(2,1)} %get-tuple-element.206.tok_own, bf16[1024,384]{1,0:T(8,128)(2,1)} %collective-permute-done.tok_oth, f32[6,4,384]{2,1,0:T(4,128)} %get-tuple-element.217.mod_own, f32[7,4,384]{2,1,0:T(4,128)} %copy-done.49, ...), custom_call_target="tpu_custom_call" | custom-call | flops 14000000000 | bytes 16000000 | tf_op jit(solution)/shard_map/forward/pallas_call | solution.py:324
  68.7 9.5 %collective-permute-done.7.s1 = bf16[768,384]{1,0:T(8,128)(2,1)} collective-permute-done((bf16[768,384]{1,0:T(8,128)(2,1)S(1)}, bf16[768,384]{1,0:T(8,128)(2,1)}, u32[]{:S(2)}, u32[]{:S(2)}) %collective-permute-start.7) | collective-permute-done | bytes 589856 | tf_op jit(solution)/shard_map/ppermute | solution.py:420
  78.2 1.4 collective-permute-start.9
  80.2 1.4 collective-permute-start.10
  82.3 6.0 %collective-permute-done.9.o1 = bf16[384,384]{1,0:T(8,128)(2,1)S(1)} collective-permute-done((bf16[384,384]{1,0:T(8,128)(2,1)}, bf16[384,384]{1,0:T(8,128)(2,1)S(1)}, u32[]{:S(2)}, u32[]{:S(2)}) %collective-permute-start.9) | collective-permute-done | bytes 294944 | tf_op jit(solution)/shard_map/ppermute | solution.py:420
  88.3 8.1 %collective-permute-done.10.x2 = bf16[192,1536]{1,0:T(8,128)(2,1)S(1)} collective-permute-done((bf16[192,1536]{1,0:T(8,128)(2,1)S(1)}, bf16[192,1536]{1,0:T(8,128)(2,1)S(1)}, u32[]{:S(2)}, u32[]{:S(2)}) %collective-permute-start.10) | collective-permute-done | bytes 589856 | tf_op jit(solution)/shard_map/ppermute | solution.py:429
  96.5 10.4 %collective-permute-done.11.s2 = bf16[768,384]{1,0:T(8,128)(2,1)S(1)} collective-permute-done((bf16[768,384]{1,0:T(8,128)(2,1)}, bf16[768,384]{1,0:T(8,128)(2,1)S(1)}, u32[]{:S(2)}, u32[]{:S(2)}) %collective-permute-start.11) | collective-permute-done | bytes 589856 | tf_op jit(solution)/shard_map/ppermute | solution.py:429
  108.0 2.0 collective-permute-done.16.o2
  111.8 38.3 %middle.1 = (bf16[1024,384]{1,0:T(8,128)(2,1)}, bf16[1024,384]{1,0:T(8,128)(2,1)}, bf16[1024,768]{1,0:T(8,128)(2,1)}, bf16[1024,1536]{1,0:T(8,128)(2,1)}, bf16[1...) custom-call(s32[1]{0:T(128)} %bitcast.place, ...), custom_call_target="tpu_custom_call" | custom-call | flops 30000001024 | bytes 50000000 | tf_op jit(solution)/shard_map/middle/pallas_call | solution.py:354
  150.1 6.6 %convolution_convert_fusion = bf16[768,1536]{1,0:T(8,128)(2,1)} fusion(bf16[1024,768]{1,0:T(8,128)(2,1)} %get-tuple-element.124, bf16[1024,1536]{1,0:T(8,128)(2,1)} %get-tuple-element.126), kind=kOutput, calls=%fused_computation.3 | convolution fusion | flops 2417098752 | bytes 7077888 | tf_op jit(solution)/shard_map/dot_general | solution.py:37
  159.2 2.9 convolution_convert_fusion.1
  162.1 1.8 pad_maximum_fusion
  165.0 5.5 %convert_add_fusion = f32[768,1536]{1,0:T(8,128)S(1)} fusion(bf16[768,1536]{1,0:T(8,128)(2,1)} %collective-permute-done.21, bf16[1024,768]{1,0:T(8,128)(2,1)S(1)} %copy-done.9, bf16[1024,1536]{1,0:T(8,128)(2,1)} %get-tuple-element.125), kind=kOutput, calls=%fused_computation | convolution fusion | flops 2418278400 | bytes 11796480 | tf_op jit(solution)/shard_map/dot_general | solution.py:37
  170.6 2.5 convolution_add_fusion.1
  173.1 1.6 copy-done.56
  175.2 4.5 %convert_add_fusion.1 = f32[1536,768]{1,0:T(8,128)S(1)} fusion(bf16[1024,1536]{1,0:T(8,128)(2,1)S(1)} %copy-done.56, bf16[1024,768]{1,0:T(8,128)(2,1)S(1)} %copy-done.59, bf16[1920,768]{1,0:T(8,128)(2,1)} %collective-permute-done.20), kind=kOutput, calls=%fused_computation.1 | convolution fusion | flops 2418278400 | bytes 11796480 | tf_op jit(solution)/shard_map/dot_general | solution.py:37
  179.9 1.5 pad_maximum_fusion.3
  182.2 1.4 collective-permute-start.22
  184.8 1.5 collective-permute-start.23
  186.3 31.7 %backward.1 = (bf16[1024,1152]{1,0:T(8,128)(2,1)}, bf16[1024,1152]{1,0:T(8,128)(2,1)}, bf16[1024,384]{1,0:T(8,128)(2,1)}, bf16[1024,384]{1,0:T(8,128)(2,1)}, f32...) custom-call(bf16[1024,384]{1,0:T(8,128)(2,1)} %get-tuple-element.206.tok_own, bf16[1024,384]{1,0:T(8,128)(2,1)} %collective-permute-done.tok_oth, ...), custom_call_target="tpu_custom_call" | custom-call | flops 24999999488 | bytes 20000000 | tf_op jit(solution)/shard_map/backward/pallas_call | solution.py:394
  218.0 6.1 %convolution_convert_fusion.2 = bf16[768,1152]{1,0:T(8,128)(2,1)} fusion(bf16[1024,768]{1,0:T(8,128)(2,1)} %get-tuple-element.117, bf16[1024,1152]{1,0:T(8,128)(2,1)} %get-tuple-element.135), kind=kOutput, calls=%fused_computation.5 | convolution fusion | flops 1812824064 | bytes 5701632 | tf_op jit(solution)/shard_map/dot_general | solution.py:37
  224.3 3.3 slice.180
  227.8 2.5 maximum_add_fusion
  231.1 1.9 convert_add_fusion.2
  233.8 5.6 %convolution_add_fusion = f32[768,1152]{1,0:T(8,128)} fusion(bf16[1024,768]{1,0:T(8,128)(2,1)S(1)} %copy-done.55, bf16[1024,1152]{1,0:T(8,128)(2,1)S(1)} %copy-done.54, bf16[768,1152]{1,0:T(8,128)(2,1)} %collective-permute-done.24), kind=kOutput, calls=%fused_computation.2 | convolution fusion | flops 1813708800 | bytes 9240576 | tf_op jit(solution)/shard_map/dot_general | solution.py:37
  239.4 9.5 %collective-permute-done.25 = bf16[192,1536]{1,0:T(8,128)(2,1)S(1)} collective-permute-done((bf16[192,1536]{1,0:T(8,128)(2,1)S(1)}, bf16[192,1536]{1,0:T(8,128)(2,1)S(1)}, u32[]{:S(2)}, u32[]{:S(2)}) %collective-permute-start.25) | collective-permute-done | bytes 589856 | tf_op jit(solution)/shard_map/ppermute | solution.py:420
  249.8 1.5 copy-done.2
  251.3 1.6 collective-permute-start.28
  253.7 1.6 slice.298
  255.3 1.6 collective-permute-start.27
  260.1 7.9 %collective-permute-done.28 = bf16[2,432,384]{2,1,0:T(8,128)(2,1)} collective-permute-done((bf16[2,432,384]{2,1,0:T(8,128)(2,1)S(1)}, bf16[2,432,384]{2,1,0:T(8,128)(2,1)}, u32[]{:S(2)}, u32[]{:S(2)}) %collective-permute-start.28) | collective-permute-done | bytes 663584 | tf_op jit(solution)/shard_map/ppermute | solution.py:429
  268.0 1.6 convert_add_fusion.4
  269.7 6.7 %collective-permute-done.27 = bf16[384,1152]{1,0:T(8,128)(2,1)} collective-permute-done((bf16[384,1152]{1,0:T(8,128)(2,1)S(1)}, bf16[384,1152]{1,0:T(8,128)(2,1)}, u32[]{:S(2)}, u32[]{:S(2)}) %collective-permute-start.27) | collective-permute-done | bytes 884768 | tf_op jit(solution)/shard_map/ppermute | solution.py:420
  276.4 1.4 convert_add_fusion.3
  278.6 2.6 collective-permute-start.32
  283.6 3.6 collective-permute-start.35
  287.2 11.9 %collective-permute-done.33 = bf16[1,76,384]{2,1,0:T(8,128)(2,1)} collective-permute-done((bf16[1,76,384]{2,1,0:T(8,128)(2,1)}, bf16[1,76,384]{2,1,0:T(8,128)(2,1)}, u32[]{:S(2)}, u32[]{:S(2)}) %collective-permute-start.33) | collective-permute-done | bytes 58400 | tf_op jit(solution)/shard_map/ppermute | solution.py:429
  299.1 1.7 pad_maximum_fusion.9
  300.7 2.0 add_convert_fusion
  304.8 3.0 collective-permute-start.37
  310.7 3.8 collective-permute-done.37
  315.6 2.1 collective-permute-done.39
  319.8 12.3 %collective-permute-done.40 = bf16[1,432,384]{2,1,0:T(8,128)(2,1)S(1)} collective-permute-done((bf16[1,432,384]{2,1,0:T(8,128)(2,1)}, bf16[1,432,384]{2,1,0:T(8,128)(2,1)S(1)}, u32[]{:S(2)}, u32[]{:S(2)}) %collective-permute-start.40) | collective-permute-done | bytes 331808 | tf_op jit(solution)/shard_map/ppermute | solution.py:429
  332.3 2.3 collective-permute-start.49
  334.5 2.1 collective-permute-start.50
  337.1 2.3 collective-permute-start.45
  340.4 2.2 collective-permute-start.46
  350.8 1.5 reshape.139
  358.3 1.5 broadcast_select_fusion.1
  359.8 4.2 %collective-permute-done.47.p1 = bf16[2,432,384]{2,1,0:T(8,128)(2,1)} collective-permute-done((bf16[2,432,384]{2,1,0:T(8,128)(2,1)S(1)}, bf16[2,432,384]{2,1,0:T(8,128)(2,1)}, u32[]{:S(2)}, u32[]{:S(2)}) %collective-permute-start.47) | collective-permute-done | bytes 663584 | tf_op jit(solution)/shard_map/ppermute | solution.py:429
  364.4 1.5 collective-permute-start.51
  367.8 15.2 %collective-permute-done.51 = bf16[64,384]{1,0:T(8,128)(2,1)S(1)} collective-permute-done((bf16[64,384]{1,0:T(8,128)(2,1)S(1)}, bf16[64,384]{1,0:T(8,128)(2,1)S(1)}, u32[]{:S(2)}, u32[]{:S(2)}) %collective-permute-start.51) | collective-permute-done | bytes 49184 | tf_op jit(solution)/shard_map/ppermute | solution.py:429
  383.1 2.5 convolution_bitcast_fusion
  385.5 5.2 %copy.31 = f32[6,384,384]{2,1,0:T(8,128)} copy(f32[6,384,384]{1,2,0:T(8,128)} %convolution_bitcast_fusion) | data formatting | bytes 7077888
  391.3 2.5 order.2
  393.8 4.4 %order.3 = (f32[8,192,384]{2,1,0:T(8,128)}, f32[8,48,384]{2,1,0:T(8,128)}, f32[8,48,1536]{2,1,0:T(8,128)}) custom-call(s32[1]{0:T(128)} %bitcast.25.mine, bf16[2,432,384]{2,1,0:T(8,128)(2,1)} %copy-done.5, bf16[2,432,384]{2,1,0:T(8,128)(2,1)} %collective-permute-done.47.p1, bf16[2,432,384]{2,1,0:T(8,128)(2,1)} %collective-permute-done.53.p2, ...), custom_call_target="tpu_custom_call" | custom-call | tf_op jit(solution)/shard_map/order/pallas_call | solution.py:551
  (288 shorter events, 53.3 us)
Async XLA Ops:
  3.5 21.6 %collective-permute-start = (bf16[1024,384]{1,0:T(8,128)(2,1)}, bf16[1024,384]{1,0:T(8,128)(2,1)}, u32[]{:S(2)}, u32[]{:S(2)}) collective-permute-start(bf16[1024,384]{1,0:T(8,128)(2,1)} %get-tuple-element.205), channel_id=1, source_target_pairs={{0,2},{2,0},{1,3},{3,1},{4,6},{6,4},{5,7},{7,5},{8,10},{10,8},{9,1... | collective-permute-start | bytes 2359304 | tf_op jit(solution)/shard_map/ppermute | solution.py:420
  7.6 3.3 collective-permute-start.1
  9.6 15.6 %copy-start.34 = (bf16[3,384,384]{2,1,0:T(8,128)(2,1)S(1)}, bf16[3,384,384]{2,1,0:T(8,128)(2,1)}, u32[]{:S(2)}) copy-start(bf16[3,384,384]{2,1,0:T(8,128)(2,1)} %w0.1) | copy-start | bytes 2654212
  10.9 57.8 %copy-start.28 = (f32[1,4,384]{2,1,0:T(4,128)}, f32[1,4,384]{2,1,0:T(4,128)S(1)}, u32[]{:S(2)}) copy-start(f32[1,4,384]{2,1,0:T(4,128)S(1)} %fusion.29.row_own) | copy-start | bytes 18436
  12.5 12.7 %collective-permute-start.2 = (f32[7,4,384]{2,1,0:T(4,128)S(1)}, f32[7,4,384]{2,1,0:T(4,128)S(1)}, u32[]{:S(2)}, u32[]{:S(2)}) collective-permute-start(f32[7,4,384]{2,1,0:T(4,128)S(1)} %pad_maximum_fusion.14), channel_id=1, source_target_pairs={{0,2},{2,0},{1,3},{3,1},{4,6},{6,4},{5,7},{7,5},{8,10},{10,8},{9,1... | collective-permute-start | bytes 129032 | tf_op jit(solution)/shard_map/ppermute | solution.py:420
  25.2 26.7 %copy-start.49 = (f32[7,4,384]{2,1,0:T(4,128)}, f32[7,4,384]{2,1,0:T(4,128)S(1)}, u32[]{:S(2)}) copy-start(f32[7,4,384]{2,1,0:T(4,128)S(1)} %collective-permute-done.2.mod_oth) | copy-start | bytes 129028
  25.2 21.0 %collective-permute-start.3 = (bf16[3,384,384]{2,1,0:T(8,128)(2,1)S(1)}, bf16[3,384,384]{2,1,0:T(8,128)(2,1)S(1)}, u32[]{:S(2)}, u32[]{:S(2)}) collective-permute-start(bf16[3,384,384]{2,1,0:T(8,128)(2,1)S(1)} %copy-done.34), channel_id=1, source_target_pairs={{0,2},{2,0},{1,3},{3,1},{4,6},{6,4},{5,7},{7,5},{8,10},{10,8},{9,1... | collective-permute-start | bytes 2654216 | tf_op jit(solution)/shard_map/ppermute | solution.py:420
  27.0 19.7 %collective-permute-start.4 = (bf16[3,384,384]{2,1,0:T(8,128)(2,1)S(1)}, bf16[3,384,384]{2,1,0:T(8,128)(2,1)S(1)}, u32[]{:S(2)}, u32[]{:S(2)}) collective-permute-start(bf16[3,384,384]{2,1,0:T(8,128)(2,1)S(1)} %copy-done.34), channel_id=1, source_target_pairs={{0,1},{1,0},{2,3},{3,2},{4,5},{5,4},{6,7},{7,6},{8,9},{9,8},{10,11... | collective-permute-start | bytes 2654216 | tf_op jit(solution)/shard_map/ppermute | solution.py:424
  46.2 3.7 collective-permute-start.5
  46.2 35.4 %collective-permute-start.12 = (bf16[384,1536]{1,0:T(8,128)(2,1)}, bf16[384,1536]{1,0:T(8,128)(2,1)}, u32[]{:S(2)}, u32[]{:S(2)}) collective-permute-start(bf16[384,1536]{1,0:T(8,128)(2,1)} %x0.1), channel_id=1, source_target_pairs={{0,1},{1,0},{2,3},{3,2},{4,5},{5,4},{6,7},{7,6},{8,9},{9,8},{10,11... | collective-permute-start | bytes 3538952 | tf_op jit(solution)/shard_map/ppermute | solution.py:424
  46.7 34.9 %collective-permute-start.13 = (bf16[1536,384]{1,0:T(8,128)(2,1)}, bf16[1536,384]{1,0:T(8,128)(2,1)}, u32[]{:S(2)}, u32[]{:S(2)}) collective-permute-start(bf16[1536,384]{1,0:T(8,128)(2,1)} %s0.1), channel_id=1, source_target_pairs={{0,1},{1,0},{2,3},{3,2},{4,5},{5,4},{6,7},{7,6},{8,9},{9,8},{10,11... | collective-permute-start | bytes 3538952 | tf_op jit(solution)/shard_map/ppermute | solution.py:424
  49.9 18.8 %collective-permute-start.6 = (bf16[192,1536]{1,0:T(8,128)(2,1)}, bf16[192,1536]{1,0:T(8,128)(2,1)S(1)}, u32[]{:S(2)}, u32[]{:S(2)}) collective-permute-start(bf16[192,1536]{1,0:T(8,128)(2,1)} %constant_dynamic-slice_fusion.2), channel_id=1, source_target_pairs={{0,2},{2,0},{1,3},{3,1},{4,6},{6,4},{5,7},{7,5},{8,10},{10,8},{9,1... | collective-permute-start | bytes 1769480 | tf_op jit(solution)/shard_map/ppermute | solution.py:420
  51.3 26.9 %collective-permute-start.7 = (bf16[768,384]{1,0:T(8,128)(2,1)S(1)}, bf16[768,384]{1,0:T(8,128)(2,1)}, u32[]{:S(2)}, u32[]{:S(2)}) collective-permute-start(bf16[768,384]{1,0:T(8,128)(2,1)S(1)} %constant_dynamic-slice_fusion.1), channel_id=1, source_target_pairs={{0,2},{2,0},{1,3},{3,1},{4,6},{6,4},{5,7},{7,5},{8,10},{10,8},{9,1... | collective-permute-start | bytes 1769480 | tf_op jit(solution)/shard_map/ppermute | solution.py:420
  51.9 27.7 %copy-start.12 = (bf16[1024,384]{1,0:T(8,128)(2,1)S(1)}, bf16[1024,384]{1,0:T(8,128)(2,1)}, u32[]{:S(2)}) copy-start(bf16[1024,384]{1,0:T(8,128)(2,1)} %get-tuple-element.103) | copy-start | bytes 2359300
  68.7 42.9 %copy-start.39 = (bf16[192,1536]{1,0:T(8,128)(2,1)}, bf16[192,1536]{1,0:T(8,128)(2,1)S(1)}, u32[]{:S(2)}) copy-start(bf16[192,1536]{1,0:T(8,128)(2,1)S(1)} %collective-permute-done.6.x1) | copy-start | bytes 1769476
  78.2 10.2 %collective-permute-start.9 = (bf16[384,384]{1,0:T(8,128)(2,1)}, bf16[384,384]{1,0:T(8,128)(2,1)S(1)}, u32[]{:S(2)}, u32[]{:S(2)}) collective-permute-start(bf16[384,384]{1,0:T(8,128)(2,1)} %o0), channel_id=1, source_target_pairs={{0,2},{2,0},{1,3},{3,1},{4,6},{6,4},{5,7},{7,5},{8,10},{10,8},{9,1... | collective-permute-start | bytes 884744 | tf_op jit(solution)/shard_map/ppermute | solution.py:420
  79.6 27.2 %collective-permute-start.8 = (bf16[1024,384]{1,0:T(8,128)(2,1)S(1)}, bf16[1024,384]{1,0:T(8,128)(2,1)S(1)}, u32[]{:S(2)}, u32[]{:S(2)}) collective-permute-start(bf16[1024,384]{1,0:T(8,128)(2,1)S(1)} %copy-done.12), channel_id=1, source_target_pairs={{0,2},{2,0},{1,3},{3,1},{4,6},{6,4},{5,7},{7,5},{8,10},{10,8},{9,1... | collective-permute-start | bytes 2359304 | tf_op jit(solution)/shard_map/ppermute | solution.py:420
  80.2 16.3 %collective-permute-start.10 = (bf16[192,1536]{1,0:T(8,128)(2,1)S(1)}, bf16[192,1536]{1,0:T(8,128)(2,1)S(1)}, u32[]{:S(2)}, u32[]{:S(2)}) collective-permute-start(bf16[192,1536]{1,0:T(8,128)(2,1)S(1)} %collective-permute-done.6.x1), channel_id=1, source_target_pairs={{0,4},{4,0},{8,12},{12,8},{16,20},{20,16},{24,28},{28,24},{1,5},{5... | collective-permute-start | bytes 1769480 | tf_op jit(solution)/shard_map/ppermute | solution.py:429
  81.6 25.2 %collective-permute-start.14 = (bf16[192,1536]{1,0:T(8,128)(2,1)S(1)}, bf16[192,1536]{1,0:T(8,128)(2,1)S(1)}, u32[]{:S(2)}, u32[]{:S(2)}) collective-permute-start(bf16[192,1536]{1,0:T(8,128)(2,1)S(1)} %collective-permute-done.6.x1), channel_id=1, source_target_pairs={{0,1},{1,0},{2,3},{3,2},{4,5},{5,4},{6,7},{7,6},{8,9},{9,8},{10,11... | collective-permute-start | bytes 1769480 | tf_op jit(solution)/shard_map/ppermute | solution.py:424
  81.6 25.2 %collective-permute-start.11 = (bf16[768,384]{1,0:T(8,128)(2,1)}, bf16[768,384]{1,0:T(8,128)(2,1)S(1)}, u32[]{:S(2)}, u32[]{:S(2)}) collective-permute-start(bf16[768,384]{1,0:T(8,128)(2,1)} %collective-permute-done.7.s1), channel_id=1, source_target_pairs={{0,4},{4,0},{8,12},{12,8},{16,20},{20,16},{24,28},{28,24},{1,5},{5... | collective-permute-start | bytes 1769480 | tf_op jit(solution)/shard_map/ppermute | solution.py:429
  88.3 22.4 %copy-start.46 = (bf16[384,384]{1,0:T(8,128)(2,1)}, bf16[384,384]{1,0:T(8,128)(2,1)S(1)}, u32[]{:S(2)}) copy-start(bf16[384,384]{1,0:T(8,128)(2,1)S(1)} %collective-permute-done.9.o1) | copy-start | bytes 884740
  88.3 18.5 %collective-permute-start.15 = (bf16[768,384]{1,0:T(8,128)(2,1)}, bf16[768,384]{1,0:T(8,128)(2,1)S(1)}, u32[]{:S(2)}, u32[]{:S(2)}) collective-permute-start(bf16[768,384]{1,0:T(8,128)(2,1)} %collective-permute-done.7.s1), channel_id=1, source_target_pairs={{0,1},{1,0},{2,3},{3,2},{4,5},{5,4},{6,7},{7,6},{8,9},{9,8},{10,11... | collective-permute-start | bytes 1769480 | tf_op jit(solution)/shard_map/ppermute | solution.py:424
  106.9 3.8 collective-permute-start.18
  107.0 3.7 collective-permute-start.19
  107.5 2.5 collective-permute-start.16
  107.5 3.1 collective-permute-start.17
  156.7 8.3 %collective-permute-start.21 = (bf16[768,1536]{1,0:T(8,128)(2,1)}, bf16[768,1536]{1,0:T(8,128)(2,1)}, u32[]{:S(2)}, u32[]{:S(2)}) collective-permute-start(bf16[768,1536]{1,0:T(8,128)(2,1)} %convolution_convert_fusion), channel_id=1, source_target_pairs={{0,1},{1,0},{2,3},{3,2},{4,5},{5,4},{6,7},{7,6},{8,9},{9,8},{10,11... | collective-permute-start | bytes 7077896 | tf_op jit(solution)/shard_map/ppermute | solution.py:424
  163.9 6.6 %collective-permute-start.20 = (bf16[1920,768]{1,0:T(8,128)(2,1)}, bf16[1920,768]{1,0:T(8,128)(2,1)}, u32[]{:S(2)}, u32[]{:S(2)}) collective-permute-start(bf16[1920,768]{1,0:T(8,128)(2,1)} %pad_maximum_fusion), channel_id=1, source_target_pairs={{0,1},{1,0},{2,3},{3,2},{4,5},{5,4},{6,7},{7,6},{8,9},{9,8},{10,11... | collective-permute-start | bytes 8847368 | tf_op jit(solution)/shard_map/ppermute | solution.py:424
  182.2 35.8 %collective-permute-start.22 = (bf16[8,240,384]{2,1,0:T(8,128)(2,1)}, bf16[8,240,384]{2,1,0:T(8,128)(2,1)S(1)}, u32[]{:S(2)}, u32[]{:S(2)}) collective-permute-start(bf16[8,240,384]{2,1,0:T(8,128)(2,1)} %pad_maximum_fusion.3), channel_id=1, source_target_pairs={{0,2},{2,0},{1,3},{3,1},{4,6},{6,4},{5,7},{7,5},{8,10},{10,8},{9,1... | collective-permute-start | bytes 4423688 | tf_op jit(solution)/shard_map/ppermute | solution.py:420
  184.8 33.2 %collective-permute-start.23 = (bf16[2,192,1536]{2,1,0:T(8,128)(2,1)}, bf16[2,192,1536]{2,1,0:T(8,128)(2,1)}, u32[]{:S(2)}, u32[]{:S(2)}) collective-permute-start(bf16[2,192,1536]{2,1,0:T(8,128)(2,1)} %dynamic-slice_convert_fusion), channel_id=1, source_target_pairs={{0,4},{4,0},{8,12},{12,8},{16,20},{20,16},{24,28},{28,24},{1,5},{5... | collective-permute-start | bytes 3538952 | tf_op jit(solution)/shard_map/ppermute | solution.py:429
  224.2 9.7 %collective-permute-start.24 = (bf16[768,1152]{1,0:T(8,128)(2,1)}, bf16[768,1152]{1,0:T(8,128)(2,1)}, u32[]{:S(2)}, u32[]{:S(2)}) collective-permute-start(bf16[768,1152]{1,0:T(8,128)(2,1)} %convolution_convert_fusion.2), channel_id=1, source_target_pairs={{0,1},{1,0},{2,3},{3,2},{4,5},{5,4},{6,7},{7,6},{8,9},{9,8},{10,11... | collective-permute-start | bytes 5308424 | tf_op jit(solution)/shard_map/ppermute | solution.py:424
  230.4 19.0 %collective-permute-start.26 = (bf16[4,240,384]{2,1,0:T(8,128)(2,1)S(1)}, bf16[4,240,384]{2,1,0:T(8,128)(2,1)S(1)}, u32[]{:S(2)}, u32[]{:S(2)}) collective-permute-start(bf16[4,240,384]{2,1,0:T(8,128)(2,1)S(1)} %dynamic-slice_convert_fusion.1), channel_id=1, source_target_pairs={{0,4},{4,0},{8,12},{12,8},{16,20},{20,16},{24,28},{28,24},{1,5},{5... | collective-permute-start | bytes 2211848 | tf_op jit(solution)/shard_map/ppermute | solution.py:429
  233.1 16.2 %copy-start.27 = (f32[4,2,768]{2,1,0:T(2,128)S(1)}, f32[4,2,768]{2,1,0:T(2,128)}, u32[]{:S(2)}) copy-start(f32[4,2,768]{2,1,0:T(2,128)} %get-tuple-element.142) | copy-start | bytes 73732
  233.1 15.8 %collective-permute-start.25 = (bf16[192,1536]{1,0:T(8,128)(2,1)S(1)}, bf16[192,1536]{1,0:T(8,128)(2,1)S(1)}, u32[]{:S(2)}, u32[]{:S(2)}) collective-permute-start(bf16[192,1536]{1,0:T(8,128)(2,1)S(1)} %fusion.3), channel_id=1, source_target_pairs={{0,2},{2,0},{1,3},{3,1},{4,6},{6,4},{5,7},{7,5},{8,10},{10,8},{9,1... | collective-permute-start | bytes 1769480 | tf_op jit(solution)/shard_map/ppermute | solution.py:420
  251.3 16.7 %collective-permute-start.28 = (bf16[2,432,384]{2,1,0:T(8,128)(2,1)S(1)}, bf16[2,432,384]{2,1,0:T(8,128)(2,1)}, u32[]{:S(2)}, u32[]{:S(2)}) collective-permute-start(bf16[2,432,384]{2,1,0:T(8,128)(2,1)S(1)} %dynamic-slice_convert_fusion.2), channel_id=1, source_target_pairs={{0,8},{4,12},{8,0},{12,4},{16,24},{20,28},{24,16},{28,20},{1,9},{5... | collective-permute-start | bytes 1990664 | tf_op jit(solution)/shard_map/ppermute | solution.py:429
  253.1 4.8 %collective-permute-start.29 = (f32[38,384]{1,0:T(8,128)S(1)}, f32[38,384]{1,0:T(8,128)}, u32[]{:S(2)}, u32[]{:S(2)}) collective-permute-start(f32[38,384]{1,0:T(8,128)S(1)} %concatenate.90), channel_id=1, source_target_pairs={{0,2},{2,0},{1,3},{3,1},{4,6},{6,4},{5,7},{7,5},{8,10},{10,8},{9,1... | collective-permute-start | bytes 175112 | tf_op jit(solution)/shard_map/ppermute | solution.py:420
  255.3 21.2 %collective-permute-start.27 = (bf16[384,1152]{1,0:T(8,128)(2,1)S(1)}, bf16[384,1152]{1,0:T(8,128)(2,1)}, u32[]{:S(2)}, u32[]{:S(2)}) collective-permute-start(bf16[384,1152]{1,0:T(8,128)(2,1)S(1)} %slice.298), channel_id=1, source_target_pairs={{0,2},{2,0},{1,3},{3,1},{4,6},{6,4},{5,7},{7,5},{8,10},{10,8},{9,1... | collective-permute-start | bytes 2654216 | tf_op jit(solution)/shard_map/ppermute | solution.py:420
  256.9 19.5 %copy-start.7 = (f32[768,1152]{1,0:T(8,128)S(1)}, f32[768,1152]{1,0:T(8,128)}, u32[]{:S(2)}) copy-start(f32[768,1152]{1,0:T(8,128)} %convolution_add_fusion) | copy-start | bytes 10616836
  278.6 22.2 %collective-permute-start.32 = (bf16[1,432,384]{2,1,0:T(8,128)(2,1)}, bf16[1,432,384]{2,1,0:T(8,128)(2,1)}, u32[]{:S(2)}, u32[]{:S(2)}) collective-permute-start(bf16[1,432,384]{2,1,0:T(8,128)(2,1)} %dynamic-slice_convert_fusion.4), channel_id=1, source_target_pairs={{0,16},{4,20},{8,24},{12,28},{16,0},{20,4},{24,8},{28,12},{1,17},{... | collective-permute-start | bytes 995336 | tf_op jit(solution)/shard_map/ppermute | solution.py:429
  282.0 20.7 %collective-permute-start.31 = (bf16[4,48,1152]{2,1,0:T(8,128)(2,1)}, bf16[4,48,1152]{2,1,0:T(8,128)(2,1)}, u32[]{:S(2)}, u32[]{:S(2)}) collective-permute-start(bf16[4,48,1152]{2,1,0:T(8,128)(2,1)} %dynamic-slice_convert_fusion.3), channel_id=1, source_target_pairs={{0,4},{4,0},{8,12},{12,8},{16,20},{20,16},{24,28},{28,24},{1,5},{5... | collective-permute-start | bytes 1327112 | tf_op jit(solution)/shard_map/ppermute | solution.py:429
  282.8 16.3 %collective-permute-start.33 = (bf16[1,76,384]{2,1,0:T(8,128)(2,1)}, bf16[1,76,384]{2,1,0:T(8,128)(2,1)}, u32[]{:S(2)}, u32[]{:S(2)}) collective-permute-start(bf16[1,76,384]{2,1,0:T(8,128)(2,1)} %maximum_bitcast_fusion.2), channel_id=1, source_target_pairs={{0,16},{4,20},{8,24},{12,28},{16,0},{20,4},{24,8},{28,12},{1,17},{... | collective-permute-start | bytes 175112 | tf_op jit(solution)/shard_map/ppermute | solution.py:429
  283.1 15.9 %collective-permute-start.34 = (bf16[1,76,384]{2,1,0:T(8,128)(2,1)}, bf16[1,76,384]{2,1,0:T(8,128)(2,1)}, u32[]{:S(2)}, u32[]{:S(2)}) collective-permute-start(bf16[1,76,384]{2,1,0:T(8,128)(2,1)} %maximum_bitcast_fusion.2), channel_id=1, source_target_pairs={{0,8},{4,12},{8,0},{12,4},{16,24},{20,28},{24,16},{28,20},{1,9},{5... | collective-permute-start | bytes 175112 | tf_op jit(solution)/shard_map/ppermute | solution.py:429
  283.6 15.5 %collective-permute-start.35 = (bf16[1,76,384]{2,1,0:T(8,128)(2,1)}, bf16[1,76,384]{2,1,0:T(8,128)(2,1)}, u32[]{:S(2)}, u32[]{:S(2)}) collective-permute-start(bf16[1,76,384]{2,1,0:T(8,128)(2,1)} %maximum_bitcast_fusion.2), channel_id=1, source_target_pairs={{0,24},{4,28},{8,16},{12,20},{16,8},{20,12},{24,0},{28,4},{1,25},{... | collective-permute-start | bytes 175112 | tf_op jit(solution)/shard_map/ppermute | solution.py:429
  303.8 28.3 %copy-start.11 = (bf16[1,432,384]{2,1,0:T(8,128)(2,1)S(1)}, bf16[1,432,384]{2,1,0:T(8,128)(2,1)}, u32[]{:S(2)}) copy-start(bf16[1,432,384]{2,1,0:T(8,128)(2,1)} %add_convert_fusion) | copy-start | bytes 995332
  304.8 9.7 %collective-permute-start.37 = (bf16[1,48,1152]{2,1,0:T(8,128)(2,1)S(1)}, bf16[1,48,1152]{2,1,0:T(8,128)(2,1)S(1)}, u32[]{:S(2)}, u32[]{:S(2)}) collective-permute-start(bf16[1,48,1152]{2,1,0:T(8,128)(2,1)S(1)} %get-tuple-element.207), channel_id=1, source_target_pairs={{0,16},{4,20},{8,24},{12,28},{16,0},{20,4},{24,8},{28,12},{1,17},{... | collective-permute-start | bytes 331784 | tf_op jit(solution)/shard_map/ppermute | solution.py:429
  307.8 7.0 %collective-permute-start.38 = (bf16[1,48,1152]{2,1,0:T(8,128)(2,1)S(1)}, bf16[1,48,1152]{2,1,0:T(8,128)(2,1)S(1)}, u32[]{:S(2)}, u32[]{:S(2)}) collective-permute-start(bf16[1,48,1152]{2,1,0:T(8,128)(2,1)S(1)} %get-tuple-element.209), channel_id=1, source_target_pairs={{0,8},{4,12},{8,0},{12,4},{16,24},{20,28},{24,16},{28,20},{1,9},{5... | collective-permute-start | bytes 331784 | tf_op jit(solution)/shard_map/ppermute | solution.py:429
  308.6 9.2 %collective-permute-start.39 = (bf16[1,48,1152]{2,1,0:T(8,128)(2,1)S(1)}, bf16[1,48,1152]{2,1,0:T(8,128)(2,1)S(1)}, u32[]{:S(2)}, u32[]{:S(2)}) collective-permute-start(bf16[1,48,1152]{2,1,0:T(8,128)(2,1)S(1)} %get-tuple-element.208), channel_id=1, source_target_pairs={{0,24},{4,28},{8,16},{12,20},{16,8},{20,12},{24,0},{28,4},{1,25},{... | collective-permute-start | bytes 331784 | tf_op jit(solution)/shard_map/ppermute | solution.py:429
  309.3 34.6 %collective-permute-start.30 = (bf16[1024,384]{1,0:T(8,128)(2,1)}, bf16[1024,384]{1,0:T(8,128)(2,1)S(1)}, u32[]{:S(2)}, u32[]{:S(2)}) collective-permute-start(bf16[1024,384]{1,0:T(8,128)(2,1)} %get-tuple-element.148), channel_id=1, source_target_pairs={{0,2},{2,0},{1,3},{3,1},{4,6},{6,4},{5,7},{7,5},{8,10},{10,8},{9,1... | collective-permute-start | bytes 2359304 | tf_op jit(solution)/shard_map/ppermute | solution.py:420
  310.2 8.6 %collective-permute-start.41 = (bf16[4,76,384]{2,1,0:T(8,128)(2,1)}, bf16[4,76,384]{2,1,0:T(8,128)(2,1)S(1)}, u32[]{:S(2)}, u32[]{:S(2)}) collective-permute-start(bf16[4,76,384]{2,1,0:T(8,128)(2,1)} %pad_maximum_fusion.9), channel_id=1, source_target_pairs={{0,4},{4,0},{8,12},{12,8},{16,20},{20,16},{24,28},{28,24},{1,5},{5... | collective-permute-start | bytes 700424 | tf_op jit(solution)/shard_map/ppermute | solution.py:429
  314.5 17.6 %collective-permute-start.40 = (bf16[1,432,384]{2,1,0:T(8,128)(2,1)}, bf16[1,432,384]{2,1,0:T(8,128)(2,1)S(1)}, u32[]{:S(2)}, u32[]{:S(2)}) collective-permute-start(bf16[1,432,384]{2,1,0:T(8,128)(2,1)} %add_convert_fusion), channel_id=1, source_target_pairs={{0,16},{4,20},{8,24},{12,28},{16,0},{20,4},{24,8},{28,12},{1,17},{... | collective-permute-start | bytes 995336 | tf_op jit(solution)/shard_map/ppermute | solution.py:429
  314.8 43.5 %collective-permute-start.36 = (bf16[1024,384]{1,0:T(8,128)(2,1)}, bf16[1024,384]{1,0:T(8,128)(2,1)}, u32[]{:S(2)}, u32[]{:S(2)}) collective-permute-start(bf16[1024,384]{1,0:T(8,128)(2,1)} %get-tuple-element.154), channel_id=1, source_target_pairs={{0,2},{2,0},{1,3},{3,1},{4,6},{6,4},{5,7},{7,5},{8,10},{10,8},{9,1... | collective-permute-start | bytes 2359304 | tf_op jit(solution)/shard_map/ppermute | solution.py:420
  332.2 4.9 %collective-permute-start.48 = (bf16[16,384]{1,0:T(8,128)(2,1)}, bf16[16,384]{1,0:T(8,128)(2,1)S(1)}, u32[]{:S(2)}, u32[]{:S(2)}) collective-permute-start(bf16[16,384]{1,0:T(8,128)(2,1)} %fusion.12), channel_id=1, source_target_pairs={{0,16},{4,20},{8,24},{12,28},{16,0},{20,4},{24,8},{28,12},{1,17},{... | collective-permute-start | bytes 36872 | tf_op jit(solution)/shard_map/ppermute | solution.py:429
  332.3 4.8 %collective-permute-start.49 = (bf16[16,384]{1,0:T(8,128)(2,1)}, bf16[16,384]{1,0:T(8,128)(2,1)S(1)}, u32[]{:S(2)}, u32[]{:S(2)}) collective-permute-start(bf16[16,384]{1,0:T(8,128)(2,1)} %fusion.12), channel_id=1, source_target_pairs={{0,8},{4,12},{8,0},{12,4},{16,24},{20,28},{24,16},{28,20},{1,9},{5... | collective-permute-start | bytes 36872 | tf_op jit(solution)/shard_map/ppermute | solution.py:429
  334.5 5.8 %collective-permute-start.50 = (bf16[16,384]{1,0:T(8,128)(2,1)}, bf16[16,384]{1,0:T(8,128)(2,1)S(1)}, u32[]{:S(2)}, u32[]{:S(2)}) collective-permute-start(bf16[16,384]{1,0:T(8,128)(2,1)} %fusion.12), channel_id=1, source_target_pairs={{0,24},{4,28},{8,16},{12,20},{16,8},{20,12},{24,0},{28,4},{1,25},{... | collective-permute-start | bytes 36872 | tf_op jit(solution)/shard_map/ppermute | solution.py:429
  337.1 9.5 %collective-permute-start.44 = (bf16[1,48,1152]{2,1,0:T(8,128)(2,1)S(1)}, bf16[1,48,1152]{2,1,0:T(8,128)(2,1)S(1)}, u32[]{:S(2)}, u32[]{:S(2)}) collective-permute-start(bf16[1,48,1152]{2,1,0:T(8,128)(2,1)S(1)} %add_convert_fusion.1), channel_id=1, source_target_pairs={{0,16},{4,20},{8,24},{12,28},{16,0},{20,4},{24,8},{28,12},{1,17},{... | collective-permute-start | bytes 331784 | tf_op jit(solution)/shard_map/ppermute | solution.py:429
  337.1 9.5 %collective-permute-start.45 = (bf16[1,48,1152]{2,1,0:T(8,128)(2,1)S(1)}, bf16[1,48,1152]{2,1,0:T(8,128)(2,1)S(1)}, u32[]{:S(2)}, u32[]{:S(2)}) collective-permute-start(bf16[1,48,1152]{2,1,0:T(8,128)(2,1)S(1)} %add_convert_fusion.1), channel_id=1, source_target_pairs={{0,8},{4,12},{8,0},{12,4},{16,24},{20,28},{24,16},{28,20},{1,9},{5... | collective-permute-start | bytes 331784 | tf_op jit(solution)/shard_map/ppermute | solution.py:429
  340.4 6.8 %collective-permute-start.46 = (bf16[1,48,1152]{2,1,0:T(8,128)(2,1)S(1)}, bf16[1,48,1152]{2,1,0:T(8,128)(2,1)S(1)}, u32[]{:S(2)}, u32[]{:S(2)}) collective-permute-start(bf16[1,48,1152]{2,1,0:T(8,128)(2,1)S(1)} %add_convert_fusion.1), channel_id=1, source_target_pairs={{0,24},{4,28},{8,16},{12,20},{16,8},{20,12},{24,0},{28,4},{1,25},{... | collective-permute-start | bytes 331784 | tf_op jit(solution)/shard_map/ppermute | solution.py:429
  343.9 4.0 %collective-permute-start.42 = (bf16[400,384]{1,0:T(8,128)(2,1)S(1)}, bf16[400,384]{1,0:T(8,128)(2,1)S(1)}, u32[]{:S(2)}, u32[]{:S(2)}) collective-permute-start(bf16[400,384]{1,0:T(8,128)(2,1)S(1)} %pad_maximum_fusion.8), channel_id=1, source_target_pairs={{0,1},{1,0},{2,3},{3,2},{4,5},{5,4},{6,7},{7,6},{8,9},{9,8},{10,11... | collective-permute-start | bytes 921608 | tf_op jit(solution)/shard_map/ppermute | solution.py:424
  346.5 17.4 %collective-permute-start.47 = (bf16[2,432,384]{2,1,0:T(8,128)(2,1)S(1)}, bf16[2,432,384]{2,1,0:T(8,128)(2,1)}, u32[]{:S(2)}, u32[]{:S(2)}) collective-permute-start(bf16[2,432,384]{2,1,0:T(8,128)(2,1)S(1)} %pad_maximum_fusion.4.p0), channel_id=1, source_target_pairs={{0,8},{4,12},{8,0},{12,4},{16,24},{20,28},{24,16},{28,20},{1,9},{5... | collective-permute-start | bytes 1990664 | tf_op jit(solution)/shard_map/ppermute | solution.py:429
  346.5 47.3 %collective-permute-start.53 = (bf16[2,432,384]{2,1,0:T(8,128)(2,1)S(1)}, bf16[2,432,384]{2,1,0:T(8,128)(2,1)}, u32[]{:S(2)}, u32[]{:S(2)}) collective-permute-start(bf16[2,432,384]{2,1,0:T(8,128)(2,1)S(1)} %pad_maximum_fusion.4.p0), channel_id=1, source_target_pairs={{0,4},{4,0},{8,12},{12,8},{16,20},{20,16},{24,28},{28,24},{1,5},{5... | collective-permute-start | bytes 1990664 | tf_op jit(solution)/shard_map/ppermute | solution.py:429
  353.1 3.8 collective-permute-start.43
  363.9 29.9 %collective-permute-start.54 = (bf16[2,432,384]{2,1,0:T(8,128)(2,1)}, bf16[2,432,384]{2,1,0:T(8,128)(2,1)}, u32[]{:S(2)}, u32[]{:S(2)}) collective-permute-start(bf16[2,432,384]{2,1,0:T(8,128)(2,1)} %collective-permute-done.47.p1), channel_id=1, source_target_pairs={{0,4},{4,0},{8,12},{12,8},{16,20},{20,16},{24,28},{28,24},{1,5},{5... | collective-permute-start | bytes 1990664 | tf_op jit(solution)/shard_map/ppermute | solution.py:429
  364.4 18.6 %collective-permute-start.51 = (bf16[64,384]{1,0:T(8,128)(2,1)S(1)}, bf16[64,384]{1,0:T(8,128)(2,1)S(1)}, u32[]{:S(2)}, u32[]{:S(2)}) collective-permute-start(bf16[64,384]{1,0:T(8,128)(2,1)S(1)} %copy-done.15), channel_id=1, source_target_pairs={{0,4},{4,0},{8,12},{12,8},{16,20},{20,16},{24,28},{28,24},{1,5},{5... | collective-permute-start | bytes 147464 | tf_op jit(solution)/shard_map/ppermute | solution.py:429
  367.3 24.1 %collective-permute-start.52 = (bf16[4,48,1152]{2,1,0:T(8,128)(2,1)}, bf16[4,48,1152]{2,1,0:T(8,128)(2,1)}, u32[]{:S(2)}, u32[]{:S(2)}) collective-permute-start(bf16[4,48,1152]{2,1,0:T(8,128)(2,1)} %pad_maximum_fusion.7.near), channel_id=1, source_target_pairs={{0,4},{4,0},{8,12},{12,8},{16,20},{20,16},{24,28},{28,24},{1,5},{5... | collective-permute-start | bytes 1327112 | tf_op jit(solution)/shard_map/ppermute | solution.py:429
  (53 other events, 247.1 us)
